TPU v7x, 32 devices: a whole 2x2x4 slice. The times are simulated.
32 devices in a mesh: ctx: 8 (over z, y), shard: 4 (over x, core).
Axes of the slice: x: 2, y: 2, z: 4, core: 2. Of those that a mesh axis runs over, the one named last changes fastest.
Arguments:
- inputs: bfloat16 [4096, 1600], P(('shard', 'ctx')), may hold values from -6 to 6
- positions: int32 [4096], P(('shard', 'ctx')), may hold values from 0 to 1279, as said below
- segments: int32 [4096], P(('shard', 'ctx')), may hold values from 0 to 7, as said below
- cotangent: bfloat16 [4096, 1600], P(('shard', 'ctx')), may hold values from -6 to 6
- ln1_gain: bfloat16 [1600], P('shard'), may hold values from 0.5 to 1.5
- ln1_bias: bfloat16 [1600], P('shard'), may hold values from -3 to 3
- w_qkv: bfloat16 [1600, 4800], P('shard'), may hold values from -0.15625 to 0.15625
- qv_bias: bfloat16 [3200], P('shard'), may hold values from -3 to 3
- w_out: bfloat16 [1600, 1600], P('shard'), may hold values from -2.5 to 2.5
- out_bias: bfloat16 [1600], P('shard'), may hold values from -3 to 3
- ln2_gain: bfloat16 [1600], P('shard'), may hold values from 0.5 to 1.5
- ln2_bias: bfloat16 [1600], P('shard'), may hold values from -3 to 3
- w_fc: bfloat16 [1600, 6400], P('shard'), may hold values from -0.15625 to 0.15625
- fc_bias: bfloat16 [6400], P('shard'), may hold values from -3 to 3
- w_proj: bfloat16 [6400, 1600], P('shard'), may hold values from -0.078125 to 0.078125
- proj_bias: bfloat16 [1600], P('shard'), may hold values from -3 to 3
Outputs:
- output: bfloat16 [4096, 1600], P(('shard', 'ctx'))
- input_grad: float32 [4096, 1600], P(('shard', 'ctx'))
- grad_ln1_gain: float32 [1600], P('shard')
- grad_ln1_bias: float32 [1600], P('shard')
- grad_w_qkv: float32 [1600, 4800], P('shard')
- grad_qv_bias: float32 [3200], P('shard')
- grad_w_out: float32 [1600, 1600], P('shard')
- grad_out_bias: float32 [1600], P('shard')
- grad_ln2_gain: float32 [1600], P('shard')
- grad_ln2_bias: float32 [1600], P('shard')
- grad_w_fc: float32 [1600, 6400], P('shard')
- grad_fc_bias: float32 [6400], P('shard')
- grad_w_proj: float32 [6400, 1600], P('shard')
- grad_proj_bias: float32 [1600], P('shard')
Inputs may be any that keep to these rules, and one draw needn't show every extreme that they name: The tokens form 4 sequences of 1024 consecutive rows. Each sequence holds two documents, first id 2 s then 2 s + 1 for sequence s; one of them has fewer than 128 tokens, at the start or at the end. Along a document positions rise by one. The short document starts below 1024, and at 0 in the first sequence; the long one ends at 1279. `segments`: ids never fall along a sequence.
All inputs are finite; a program needn't handle non-finite values.
Results may differ from a plain program's by a relative error of at most 0.018.
Values may be sent and summed in bfloat16 or wider, within the bound.
A program may use at most 448 MiB of HBM per device.

v0:
```python
import math

import jax
import jax.numpy as jnp
from jax import lax
from jax.sharding import PartitionSpec as P

HEAD_DIM = 64
BLOCK = 256


EPSILON = 1e-05
NEGATIVE = -1e30


def passed_along(x, axis, by):
    size = lax.axis_size(axis)
    return lax.ppermute(x, axis, [(i, (i + by) % size) for i in range(size)])


def normalize(values, gain, offset):
    centre = jnp.mean(values, axis=-1, keepdims=True)
    centred = values - centre
    spread = jnp.mean(centred * centred, axis=-1, keepdims=True)
    return centred * lax.rsqrt(spread + EPSILON) * gain + offset


def gelu_tanh(values):
    return jax.nn.gelu(values, approximate=True)


def allowed_pairs(query_pos, query_seg, key_pos, key_seg):
    same_doc = query_seg[:, None] == key_seg[None, :]
    earlier = (key_pos // BLOCK)[None, :] <= (query_pos // BLOCK)[:, None]
    return jnp.logical_and(same_doc, earlier)


def head_scores(queries, keys_in, allowed, score_scale):
    scores = (
        jnp.einsum("thd,shd->hts", queries, keys_in, preferred_element_type=jnp.float32)
        * score_scale
    )
    return jnp.where(allowed[None], scores, NEGATIVE)


def forward_step(softmax_state, queries, keys_in, values_in, allowed, score_scale):
    running, totals, accum = softmax_state
    scores = head_scores(queries, keys_in, allowed, score_scale)
    new_max = jnp.maximum(running, jnp.max(scores, axis=-1))
    factor = jnp.exp(running - new_max)
    unnorm = jnp.exp(scores - new_max[..., None])
    totals = totals * factor + jnp.sum(unnorm, axis=-1)
    accum = accum * factor[..., None] + jnp.einsum(
        "hts,shd->htd", unnorm.astype(jnp.bfloat16), values_in, preferred_element_type=jnp.float32
    )
    return (new_max, totals, accum)


def backward_step(queries, grad_out, logsum, delta, keys_in, values_in, allowed, score_scale):
    scores = head_scores(queries, keys_in, allowed, score_scale)
    probs = jnp.exp(scores - logsum[..., None])
    grad_probs = jnp.einsum("thd,shd->hts", grad_out, values_in, preferred_element_type=jnp.float32)
    grad_scores = (probs * (grad_probs - delta[..., None])).astype(jnp.bfloat16)
    part_query = (
        jnp.einsum("hts,shd->thd", grad_scores, keys_in, preferred_element_type=jnp.float32)
        * score_scale
    )
    part_keys = (
        jnp.einsum("hts,thd->shd", grad_scores, queries, preferred_element_type=jnp.float32)
        * score_scale
    )
    part_values = jnp.einsum(
        "hts,thd->shd", probs.astype(jnp.bfloat16), grad_out, preferred_element_type=jnp.float32
    )
    return (part_query, part_keys, part_values)


def local(
    inputs,
    positions,
    segments,
    cotangent,
    ln1_gain,
    ln1_bias,
    w_qkv,
    qv_bias,
    w_out,
    out_bias,
    ln2_gain,
    ln2_bias,
    w_fc,
    fc_bias,
    w_proj,
    proj_bias,
):
    gathered = (
        lax.all_gather(ln1_gain, "shard", axis=0, tiled=True),
        lax.all_gather(ln1_bias, "shard", axis=0, tiled=True),
        lax.all_gather(w_qkv, "shard", axis=0, tiled=True),
        lax.all_gather(qv_bias, "shard", axis=0, tiled=True),
        lax.all_gather(w_out, "shard", axis=0, tiled=True),
        lax.all_gather(out_bias, "shard", axis=0, tiled=True),
        lax.all_gather(ln2_gain, "shard", axis=0, tiled=True),
        lax.all_gather(ln2_bias, "shard", axis=0, tiled=True),
        lax.all_gather(w_fc, "shard", axis=0, tiled=True),
        lax.all_gather(fc_bias, "shard", axis=0, tiled=True),
        lax.all_gather(w_proj, "shard", axis=0, tiled=True),
        lax.all_gather(proj_bias, "shard", axis=0, tiled=True),
    )
    (
        gain_one,
        bias_one,
        full_qkv,
        full_qv,
        full_out,
        full_outb,
        gain_two,
        bias_two,
        full_fc,
        full_fcb,
        full_proj,
        full_projb,
    ) = gathered
    all_positions, all_segments = (
        lax.all_gather(positions, "ctx", axis=0, tiled=True),
        lax.all_gather(segments, "ctx", axis=0, tiled=True),
    )
    cycle_size = lax.axis_size("ctx")
    myself = lax.axis_index("ctx")
    row_count = inputs.shape[0]
    model_width = inputs.shape[1]
    head_count = model_width // HEAD_DIM
    score_scale = 1.0 / math.sqrt(HEAD_DIM)

    def marks_of(owner_index):
        start_row = owner_index * row_count
        return (
            lax.dynamic_slice_in_dim(all_positions, start_row, row_count),
            lax.dynamic_slice_in_dim(all_segments, start_row, row_count),
        )

    gain_one_f = gain_one.astype(jnp.float32)
    bias_one_f = bias_one.astype(jnp.float32)
    gain_two_f = gain_two.astype(jnp.float32)
    bias_two_f = bias_two.astype(jnp.float32)
    qv_float = full_qv.astype(jnp.float32)
    residual = inputs.astype(jnp.float32)
    hidden_one = normalize(residual, gain_one_f, bias_one_f).astype(jnp.bfloat16)
    packed = jnp.dot(hidden_one, full_qkv, preferred_element_type=jnp.float32)
    head_shape = (row_count, head_count, HEAD_DIM)
    queries = (
        (packed[:, :model_width] + qv_float[:model_width]).astype(jnp.bfloat16).reshape(head_shape)
    )
    keys_own = packed[:, model_width : 2 * model_width].astype(jnp.bfloat16).reshape(head_shape)
    values_own = (
        (packed[:, 2 * model_width :] + qv_float[model_width:])
        .astype(jnp.bfloat16)
        .reshape(head_shape)
    )
    allowed_own = allowed_pairs(positions, segments, positions, segments)
    softmax_state = (
        jnp.full((head_count, row_count), NEGATIVE, jnp.float32),
        jnp.zeros((head_count, row_count), jnp.float32),
        jnp.zeros((head_count, row_count, HEAD_DIM), jnp.float32),
    )
    softmax_state = forward_step(
        softmax_state, queries, keys_own, values_own, allowed_own, score_scale
    )

    def cycle_forward(cycle_step, carry):
        travel, softmax_state = carry
        travel = passed_along((travel[0], travel[1]), "ctx", 1)
        key_pos, key_seg = marks_of((myself - cycle_step) % cycle_size)
        allowed = allowed_pairs(positions, segments, key_pos, key_seg)

        def advance(carried):
            return forward_step(carried, queries, travel[0], travel[1], allowed, score_scale)

        softmax_state = advance(softmax_state)
        return (travel, softmax_state)

    travel, softmax_state = lax.fori_loop(
        1, cycle_size, cycle_forward, ((keys_own, values_own), softmax_state)
    )
    running, totals, accum = softmax_state
    logsum = running + jnp.log(totals)
    attended = jnp.transpose(accum / totals[..., None], (1, 0, 2))
    attended_low = attended.reshape(row_count, model_width).astype(jnp.bfloat16)
    middle = residual + (
        jnp.dot(attended_low, full_out, preferred_element_type=jnp.float32)
        + full_outb.astype(jnp.float32)
    )
    hidden_two = normalize(middle, gain_two_f, bias_two_f).astype(jnp.bfloat16)
    pre_act = jnp.dot(hidden_two, full_fc, preferred_element_type=jnp.float32) + full_fcb.astype(
        jnp.float32
    )
    activated = gelu_tanh(pre_act).astype(jnp.bfloat16)
    result = middle + (
        jnp.dot(activated, full_proj, preferred_element_type=jnp.float32)
        + full_projb.astype(jnp.float32)
    )
    output = result.astype(jnp.bfloat16)
    grad_result = cotangent.astype(jnp.float32)
    grad_w_proj = jnp.einsum("tf,td->fd", activated, cotangent, preferred_element_type=jnp.float32)
    grad_proj_bias = jnp.sum(grad_result, axis=0)
    grad_act = jnp.einsum("td,fd->tf", cotangent, full_proj, preferred_element_type=jnp.float32)
    _, gelu_pull = jax.vjp(gelu_tanh, pre_act)
    grad_pre = gelu_pull(grad_act)[0].astype(jnp.bfloat16)
    grad_w_fc = jnp.einsum("td,tf->df", hidden_two, grad_pre, preferred_element_type=jnp.float32)
    grad_fc_bias = jnp.sum(grad_pre.astype(jnp.float32), axis=0)
    grad_hidden_two = jnp.einsum("tf,df->td", grad_pre, full_fc, preferred_element_type=jnp.float32)
    _, norm_pull_two = jax.vjp(normalize, middle, gain_two_f, bias_two_f)
    grad_middle_part, grad_gain_two, grad_bias_two = norm_pull_two(grad_hidden_two)
    grad_middle = grad_result + grad_middle_part
    grad_branch = grad_middle.astype(jnp.bfloat16)
    grad_w_out = jnp.einsum(
        "te,td->ed", attended_low, grad_branch, preferred_element_type=jnp.float32
    )
    grad_out_bias = jnp.sum(grad_branch.astype(jnp.float32), axis=0)
    grad_attended = (
        jnp.einsum("td,ed->te", grad_branch, full_out, preferred_element_type=jnp.float32)
        .astype(jnp.bfloat16)
        .reshape(head_shape)
    )
    delta = jnp.einsum("thd,thd->ht", grad_attended.astype(jnp.float32), attended)
    first_query, first_keys, first_values = backward_step(
        queries, grad_attended, logsum, delta, keys_own, values_own, allowed_own, score_scale
    )

    def cycle_keys(cycle_step, carry):
        travel, grads_kv, grad_query = carry
        travel = passed_along((travel[0], travel[1]), "ctx", 1)
        grads_kv = (
            passed_along(grads_kv[0].astype(jnp.bfloat16), "ctx", 1).astype(jnp.float32),
            passed_along(grads_kv[1].astype(jnp.bfloat16), "ctx", 1).astype(jnp.float32),
        )
        key_pos, key_seg = marks_of((myself - cycle_step) % cycle_size)
        allowed = allowed_pairs(positions, segments, key_pos, key_seg)

        def advance(carried):
            kv_sums, query_sum = carried
            part_query, part_keys, part_values = backward_step(
                queries, grad_attended, logsum, delta, travel[0], travel[1], allowed, score_scale
            )
            return ((kv_sums[0] + part_keys, kv_sums[1] + part_values), query_sum + part_query)

        grads_kv, grad_query = advance((grads_kv, grad_query))
        return (travel, grads_kv, grad_query)

    travel, grads_kv, grad_query = lax.fori_loop(
        1, cycle_size, cycle_keys, ((keys_own, values_own), (first_keys, first_values), first_query)
    )
    grad_keys, grad_values = (
        passed_along(grads_kv[0].astype(jnp.bfloat16), "ctx", 1).astype(jnp.float32),
        passed_along(grads_kv[1].astype(jnp.bfloat16), "ctx", 1).astype(jnp.float32),
    )
    flat_shape = (row_count, model_width)
    grad_query_low = grad_query.reshape(flat_shape).astype(jnp.bfloat16)
    grad_keys_low = grad_keys.reshape(flat_shape).astype(jnp.bfloat16)
    grad_values_low = grad_values.reshape(flat_shape).astype(jnp.bfloat16)
    grad_packed = jnp.concatenate([grad_query_low, grad_keys_low, grad_values_low], axis=1)
    grad_w_qkv = jnp.einsum(
        "td,te->de", hidden_one, grad_packed, preferred_element_type=jnp.float32
    )
    grad_qv_bias = jnp.concatenate(
        [
            jnp.sum(grad_query_low.astype(jnp.float32), axis=0),
            jnp.sum(grad_values_low.astype(jnp.float32), axis=0),
        ]
    )
    grad_hidden_one = jnp.einsum(
        "te,de->td", grad_packed, full_qkv, preferred_element_type=jnp.float32
    )
    _, norm_pull_one = jax.vjp(normalize, residual, gain_one_f, bias_one_f)
    grad_resid_part, grad_gain_one, grad_bias_one = norm_pull_one(grad_hidden_one)
    input_grad = grad_middle + grad_resid_part
    local_grads = (
        grad_gain_one,
        grad_bias_one,
        grad_w_qkv,
        grad_qv_bias,
        grad_w_out,
        grad_out_bias,
        grad_gain_two,
        grad_bias_two,
        grad_w_fc,
        grad_fc_bias,
        grad_w_proj,
        grad_proj_bias,
    )
    shard_grads = (
        lax.psum_scatter(
            local_grads[0].astype(jnp.bfloat16), "shard", scatter_dimension=0, tiled=True
        ).astype(jnp.float32),
        lax.psum_scatter(
            local_grads[1].astype(jnp.bfloat16), "shard", scatter_dimension=0, tiled=True
        ).astype(jnp.float32),
        lax.psum_scatter(
            local_grads[2].astype(jnp.bfloat16), "shard", scatter_dimension=0, tiled=True
        ).astype(jnp.float32),
        lax.psum_scatter(
            local_grads[3].astype(jnp.bfloat16), "shard", scatter_dimension=0, tiled=True
        ).astype(jnp.float32),
        lax.psum_scatter(
            local_grads[4].astype(jnp.bfloat16), "shard", scatter_dimension=0, tiled=True
        ).astype(jnp.float32),
        lax.psum_scatter(
            local_grads[5].astype(jnp.bfloat16), "shard", scatter_dimension=0, tiled=True
        ).astype(jnp.float32),
        lax.psum_scatter(
            local_grads[6].astype(jnp.bfloat16), "shard", scatter_dimension=0, tiled=True
        ).astype(jnp.float32),
        lax.psum_scatter(
            local_grads[7].astype(jnp.bfloat16), "shard", scatter_dimension=0, tiled=True
        ).astype(jnp.float32),
        lax.psum_scatter(
            local_grads[8].astype(jnp.bfloat16), "shard", scatter_dimension=0, tiled=True
        ).astype(jnp.float32),
        lax.psum_scatter(
            local_grads[9].astype(jnp.bfloat16), "shard", scatter_dimension=0, tiled=True
        ).astype(jnp.float32),
        lax.psum_scatter(
            local_grads[10].astype(jnp.bfloat16), "shard", scatter_dimension=0, tiled=True
        ).astype(jnp.float32),
        lax.psum_scatter(
            local_grads[11].astype(jnp.bfloat16), "shard", scatter_dimension=0, tiled=True
        ).astype(jnp.float32),
    )
    summed = (
        lax.psum(shard_grads[0].astype(jnp.bfloat16), "ctx").astype(jnp.float32),
        lax.psum(shard_grads[1].astype(jnp.bfloat16), "ctx").astype(jnp.float32),
        lax.psum(shard_grads[2].astype(jnp.bfloat16), "ctx").astype(jnp.float32),
        lax.psum(shard_grads[3].astype(jnp.bfloat16), "ctx").astype(jnp.float32),
        lax.psum(shard_grads[4].astype(jnp.bfloat16), "ctx").astype(jnp.float32),
        lax.psum(shard_grads[5].astype(jnp.bfloat16), "ctx").astype(jnp.float32),
        lax.psum(shard_grads[6].astype(jnp.bfloat16), "ctx").astype(jnp.float32),
        lax.psum(shard_grads[7].astype(jnp.bfloat16), "ctx").astype(jnp.float32),
        lax.psum(shard_grads[8].astype(jnp.bfloat16), "ctx").astype(jnp.float32),
        lax.psum(shard_grads[9].astype(jnp.bfloat16), "ctx").astype(jnp.float32),
        lax.psum(shard_grads[10].astype(jnp.bfloat16), "ctx").astype(jnp.float32),
        lax.psum(shard_grads[11].astype(jnp.bfloat16), "ctx").astype(jnp.float32),
    )
    return (
        output,
        input_grad,
        summed[0],
        summed[1],
        summed[2],
        summed[3],
        summed[4],
        summed[5],
        summed[6],
        summed[7],
        summed[8],
        summed[9],
        summed[10],
        summed[11],
    )


def solution(mesh):
    return jax.shard_map(
        local,
        mesh=mesh,
        in_specs=(
            P(("shard", "ctx"), None),
            P(("shard", "ctx")),
            P(("shard", "ctx")),
            P(("shard", "ctx"), None),
            P("shard"),
            P("shard"),
            P("shard", None),
            P("shard"),
            P("shard", None),
            P("shard"),
            P("shard"),
            P("shard"),
            P("shard", None),
            P("shard"),
            P("shard", None),
            P("shard"),
        ),
        out_specs=(
            P(("shard", "ctx"), None),
            P(("shard", "ctx"), None),
            P("shard"),
            P("shard"),
            P("shard", None),
            P("shard"),
            P("shard", None),
            P("shard"),
            P("shard"),
            P("shard"),
            P("shard", None),
            P("shard"),
            P("shard", None),
            P("shard"),
        ),
        check_vma=False,
    )
```

profile of v0, /device:TPU:1, one launch (start us, length us, event | category | flops | bytes accessed | tf_op | source)
XLA Modules:
  0.0 1750.0 jit_solution(1748334838641314329)
XLA Ops:
  14.5 11.8 all-reduce.19
  26.4 17.1 all-gather
  43.5 13.0 all-gather.1
  57.2 54.1 %all-gather.7.cloned.1.call-done = bf16[1600,4800]{1,0:T(8,128)(2,1)} async-done(((bf16[400,4800]{1,0:T(8,128)(2,1)}), bf16[1600,4800]{1,0:T(8,128)(2,1)}) %all-gather.7.cloned.1.call-update) | async-done | bytes 15360016 | tf_op jit(solution)/shard_map/all_gather | solution.py:99
  111.3 12.3 fusion.52
  132.9 147.1 %while.48 = (s32[]{:T(128)}, bf16[128,25,64]{0,2,1:T(8,128)(2,1)}, bf16[128,25,64]{0,2,1:T(8,128)(2,1)}, f32[25,128]{1,0:T(8,128)S(1)}, f32[25,128]{1,0:T(8,128)...) while((s32[]{:T(128)}, bf16[128,25,64]{0,2,1:T(8,128)(2,1)}, ...), condition=%wide.region_7.8_spmd, body=%wide.region_4.7_spmd.sunk | while | flops 108193552 | bytes 12941748 | solution.py:182
  135.7 11.1 collective-permute-done
  148.3 7.2 collective-permute-done.1
  157.6 12.0 collective-permute-done
  171.2 7.2 collective-permute-done.1
  180.0 11.6 collective-permute-done
  193.1 7.2 collective-permute-done.1
  201.9 10.6 collective-permute-done
  214.1 7.2 collective-permute-done.1
  222.9 9.7 collective-permute-done
  234.2 7.2 collective-permute-done.1
  243.0 9.3 collective-permute-done
  253.9 6.7 collective-permute-done.1
  262.2 9.3 collective-permute-done
  273.1 5.7 collective-permute-done.1
  280.9 4.9 fusion.65
  286.1 2.8 all-gather.13.cloned.1.call-done
  288.9 13.5 fusion.66
  302.5 116.8 %all-gather.11.cloned.1.call-done = bf16[1600,6400]{1,0:T(8,128)(2,1)} async-done(((bf16[400,6400]{1,0:T(8,128)(2,1)}), bf16[1600,6400]{1,0:T(8,128)(2,1)}) %all-gather.11.cloned.1.call-update) | async-done | bytes 20480016 | tf_op jit(solution)/shard_map/all_gather | solution.py:105
  419.3 11.8 fusion.55
  431.1 12.3 multiply_reduce_fusion
  451.2 3.9 convolution_convert_fusion.3
  455.3 313.3 %while.49 = (s32[]{:T(128)}, bf16[128,25,64]{0,2,1:T(8,128)(2,1)}, bf16[128,25,64]{0,2,1:T(8,128)(2,1)S(1)}, bf16[128,25,64]{0,2,1:T(8,128)(2,1)}, bf16[128,25,6...) while((s32[]{:T(128)}, bf16[128,25,64]{0,2,1:T(8,128)(2,1)}, ...), condition=%wide.region_13.14_spmd, body=%wide.region_12.13_spmd.sunk | while | flops 266907152 | bytes 25050708 | solution.py:250
  460.4 8.7 collective-permute-done.2
  469.8 25.7 %collective-permute-done.5 = bf16[128,25,64]{0,2,1:T(8,128)(2,1)} collective-permute-done((bf16[128,25,64]{0,2,1:T(8,128)(2,1)}, bf16[128,25,64]{0,2,1:T(8,128)(2,1)}, u32[]{:S(2)}, u32[]{:S(2)}) %collective-permute-start.5) | collective-permute-done | bytes 409632 | tf_op jit(solution)/shard_map/while/body/eval_jaxpr/ppermute | solution.py:18
  499.9 2.2 convert_add_fusion.4
  506.1 9.6 collective-permute-done.2
  516.4 25.7 %collective-permute-done.5 = bf16[128,25,64]{0,2,1:T(8,128)(2,1)} collective-permute-done((bf16[128,25,64]{0,2,1:T(8,128)(2,1)}, bf16[128,25,64]{0,2,1:T(8,128)(2,1)}, u32[]{:S(2)}, u32[]{:S(2)}) %collective-permute-start.5) | collective-permute-done | bytes 409632 | tf_op jit(solution)/shard_map/while/body/eval_jaxpr/ppermute | solution.py:18
  546.6 2.2 convert_add_fusion.4
  550.8 10.5 collective-permute-done.2
  562.1 25.7 %collective-permute-done.5 = bf16[128,25,64]{0,2,1:T(8,128)(2,1)} collective-permute-done((bf16[128,25,64]{0,2,1:T(8,128)(2,1)}, bf16[128,25,64]{0,2,1:T(8,128)(2,1)}, u32[]{:S(2)}, u32[]{:S(2)}) %collective-permute-start.5) | collective-permute-done | bytes 409632 | tf_op jit(solution)/shard_map/while/body/eval_jaxpr/ppermute | solution.py:18
  592.2 2.2 convert_add_fusion.4
  596.2 9.9 collective-permute-done.2
  606.9 25.7 %collective-permute-done.5 = bf16[128,25,64]{0,2,1:T(8,128)(2,1)} collective-permute-done((bf16[128,25,64]{0,2,1:T(8,128)(2,1)}, bf16[128,25,64]{0,2,1:T(8,128)(2,1)}, u32[]{:S(2)}, u32[]{:S(2)}) %collective-permute-start.5) | collective-permute-done | bytes 409632 | tf_op jit(solution)/shard_map/while/body/eval_jaxpr/ppermute | solution.py:18
  637.0 2.2 convert_add_fusion.4
  640.9 9.0 collective-permute-done.2
  650.7 25.7 %collective-permute-done.5 = bf16[128,25,64]{0,2,1:T(8,128)(2,1)} collective-permute-done((bf16[128,25,64]{0,2,1:T(8,128)(2,1)}, bf16[128,25,64]{0,2,1:T(8,128)(2,1)}, u32[]{:S(2)}, u32[]{:S(2)}) %collective-permute-start.5) | collective-permute-done | bytes 409632 | tf_op jit(solution)/shard_map/while/body/eval_jaxpr/ppermute | solution.py:18
  680.8 2.2 convert_add_fusion.4
  684.8 8.7 collective-permute-done.2
  694.2 25.1 %collective-permute-done.5 = bf16[128,25,64]{0,2,1:T(8,128)(2,1)} collective-permute-done((bf16[128,25,64]{0,2,1:T(8,128)(2,1)}, bf16[128,25,64]{0,2,1:T(8,128)(2,1)}, u32[]{:S(2)}, u32[]{:S(2)}) %collective-permute-start.5) | collective-permute-done | bytes 409632 | tf_op jit(solution)/shard_map/while/body/eval_jaxpr/ppermute | solution.py:18
  723.8 2.2 convert_add_fusion.4
  727.7 8.7 collective-permute-done.2
  737.1 24.2 %collective-permute-done.5 = bf16[128,25,64]{0,2,1:T(8,128)(2,1)} collective-permute-done((bf16[128,25,64]{0,2,1:T(8,128)(2,1)}, bf16[128,25,64]{0,2,1:T(8,128)(2,1)}, u32[]{:S(2)}, u32[]{:S(2)}) %collective-permute-start.5) | collective-permute-done | bytes 409632 | tf_op jit(solution)/shard_map/while/body/eval_jaxpr/ppermute | solution.py:18
  769.0 9.3 collective-permute-done.7
  778.4 6.3 collective-permute-done.6
  784.7 12.0 convolution_convert_fusion.2
  798.1 12.0 convolution_convert_fusion.1
  811.2 14.4 convolution_convert_fusion
  825.7 93.2 %reduce-scatter.5.cloned.1.call-done = bf16[400,4800]{1,0:T(8,128)(2,1)} async-done(((bf16[1600,4800]{1,0:T(8,128)(2,1)}), bf16[400,4800]{1,0:T(8,128)(2,1)}) %reduce-scatter.5.cloned.1.call-update) | async-done | bytes 3840016 | tf_op jit(solution)/shard_map/reduce_scatter | solution.py:298
  918.9 159.9 %reduce-scatter.9.cloned.1.call-done = bf16[400,6400]{1,0:T(8,128)(2,1)} async-done(((bf16[1600,6400]{1,0:T(8,128)(2,1)}), bf16[400,6400]{1,0:T(8,128)(2,1)}) %reduce-scatter.9.cloned.1.call-update) | async-done | bytes 5120016 | tf_op jit(solution)/shard_map/reduce_scatter | solution.py:316
  1078.8 157.9 %reduce-scatter.11.cloned.1.call-done = bf16[1600,1600]{1,0:T(8,128)(2,1)} async-done(((bf16[6400,1600]{1,0:T(8,128)(2,1)}), bf16[1600,1600]{1,0:T(8,128)(2,1)}) %reduce-scatter.11.cloned.1.call-update) | async-done | bytes 5120016 | tf_op jit(solution)/shard_map/reduce_scatter | solution.py:322
  1239.8 9.3 fusion.54
  1249.7 11.6 all-reduce.18
  1261.9 32.8 %all-reduce.16 = (bf16[400]{0:T(512)(128)(2,1)S(1)}, bf16[400]{0:T(512)(128)(2,1)S(1)}, bf16[800]{0:T(1024)(128)(2,1)S(1)}, bf16[400]{0:T(512)(128)(2,1)S(1)}, b...) all-reduce(bf16[400]{0:T(512)(128)(2,1)S(1)} %dynamic-slice.9, ...), channel_id=1, replica_groups=mesh['ctx'=8,'shard'=4] {'ctx'}, use_global_device_ids=true, to_apply=%region_18.19 | all-reduce | flops 4800 | bytes 19200 | tf_op jit(solution)/shard_map/psum | solution.py:330
  1300.6 15.0 fusion.19
  1315.6 410.4 %all-reduce.22.cloned.1.call-done = (bf16[400,4800]{1,0:T(8,128)(2,1)}, bf16[400,1600]{1,0:T(8,128)(2,1)}, bf16[400,6400]{1,0:T(8,128)(2,1)}, bf16[1600,1600]{1,0:T(8,128)(2,1)}) async-done(((bf16[400,4800]{1,0:T(8,128)(2,1)}, bf16[400,1600]{1,0:T(8,128)(2,1)}, bf16[400,6400]{1,0:T(8,128)(2,1)}, bf16[1600,1600]{1,0:T(8,128)(2,1)}), (bf16[400,4800]{1,0:T(8,128)(2,1)}, bf16[400,1600]{1,0:T(8,128)(2,1)}, ...) | async-done | bytes 15360016 | tf_op jit(solution)/shard_map/psum | solution.py:332
  1726.0 6.0 convert_element_type.308
  1733.7 4.7 convert_element_type.320
  1738.4 4.8 convert_element_type.323
  (395 shorter events, 118.5 us)
Async XLA Ops:
  7.2 104.1 %all-gather.7.cloned.1.call-start = ((), (), s32[]{:S(2)}) async-start(), calls=%async_computation.4 | async-start | bytes 19456000 | tf_op jit(solution)/shard_map/all_gather | solution.py:99
  7.9 273.0 %all-gather.9.cloned.1.call-start = ((), (), s32[]{:S(2)}) async-start(), calls=%async_computation.5 | async-start | bytes 6656000 | tf_op jit(solution)/shard_map/all_gather | solution.py:101
  8.7 280.3 %all-gather.13.cloned.1.call-start = ((), (), s32[]{:S(2)}) async-start(), calls=%async_computation.7 | async-start | bytes 26624000 | tf_op jit(solution)/shard_map/all_gather | solution.py:107
  9.5 16.9 copy-start.17
  9.5 34.0 %copy-start.18 = (s32[128]{0:T(128)S(1)}, s32[128]{0:T(128)}, u32[]{:S(2)}) copy-start(s32[128]{0:T(128)} %param.21) | copy-start | bytes 1540
  9.5 47.0 %copy-start.2 = (bf16[128,1600]{0,1:T(8,128)(2,1)S(1)}, bf16[128,1600]{0,1:T(8,128)(2,1)}, u32[]{:S(2)}) copy-start(bf16[128,1600]{0,1:T(8,128)(2,1)} %param.20) | copy-start | bytes 1228804
  9.5 409.8 %all-gather.11.cloned.1.call-start = ((), (), s32[]{:S(2)}) async-start(), calls=%async_computation.6 | async-start | bytes 25600000 | tf_op jit(solution)/shard_map/all_gather | solution.py:105
  10.1 815.6 %reduce-scatter.7.cloned.1.call-start = ((), (), s32[]{:S(2)}) async-start(), calls=%async_computation.9 | async-start | bytes 6656000 | tf_op jit(solution)/shard_map/reduce_scatter | solution.py:304
  132.9 13.8 collective-permute-start
  134.2 21.3 %collective-permute-start.1 = (bf16[128,25,64]{0,2,1:T(8,128)(2,1)}, bf16[128,25,64]{0,2,1:T(8,128)(2,1)S(1)}, u32[]{:S(2)}, u32[]{:S(2)}) collective-permute-start(bf16[128,25,64]{0,2,1:T(8,128)(2,1)} %get-tuple-element.1140), channel_id=1, source_target_pairs={{0,4},{4,8},{8,12},{12,16},{16,20},{20,24},{24,28},{28,0},{1,5},{5... | collective-permute-start | bytes 1228808 | tf_op jit(solution)/shard_map/while/body/eval_jaxpr/ppermute | solution.py:18
  156.7 12.9 collective-permute-start
  156.8 21.6 %collective-permute-start.1 = (bf16[128,25,64]{0,2,1:T(8,128)(2,1)}, bf16[128,25,64]{0,2,1:T(8,128)(2,1)S(1)}, u32[]{:S(2)}, u32[]{:S(2)}) collective-permute-start(bf16[128,25,64]{0,2,1:T(8,128)(2,1)} %get-tuple-element.1140), channel_id=1, source_target_pairs={{0,4},{4,8},{8,12},{12,16},{16,20},{20,24},{24,28},{28,0},{1,5},{5... | collective-permute-start | bytes 1228808 | tf_op jit(solution)/shard_map/while/body/eval_jaxpr/ppermute | solution.py:18
  179.6 12.0 collective-permute-start
  179.6 20.7 %collective-permute-start.1 = (bf16[128,25,64]{0,2,1:T(8,128)(2,1)}, bf16[128,25,64]{0,2,1:T(8,128)(2,1)S(1)}, u32[]{:S(2)}, u32[]{:S(2)}) collective-permute-start(bf16[128,25,64]{0,2,1:T(8,128)(2,1)} %get-tuple-element.1140), channel_id=1, source_target_pairs={{0,4},{4,8},{8,12},{12,16},{16,20},{20,24},{24,28},{28,0},{1,5},{5... | collective-permute-start | bytes 1228808 | tf_op jit(solution)/shard_map/while/body/eval_jaxpr/ppermute | solution.py:18
  201.5 11.1 collective-permute-start
  201.6 19.8 %collective-permute-start.1 = (bf16[128,25,64]{0,2,1:T(8,128)(2,1)}, bf16[128,25,64]{0,2,1:T(8,128)(2,1)S(1)}, u32[]{:S(2)}, u32[]{:S(2)}) collective-permute-start(bf16[128,25,64]{0,2,1:T(8,128)(2,1)} %get-tuple-element.1140), channel_id=1, source_target_pairs={{0,4},{4,8},{8,12},{12,16},{16,20},{20,24},{24,28},{28,0},{1,5},{5... | collective-permute-start | bytes 1228808 | tf_op jit(solution)/shard_map/while/body/eval_jaxpr/ppermute | solution.py:18
  222.5 10.1 collective-permute-start
  222.6 18.9 %collective-permute-start.1 = (bf16[128,25,64]{0,2,1:T(8,128)(2,1)}, bf16[128,25,64]{0,2,1:T(8,128)(2,1)S(1)}, u32[]{:S(2)}, u32[]{:S(2)}) collective-permute-start(bf16[128,25,64]{0,2,1:T(8,128)(2,1)} %get-tuple-element.1140), channel_id=1, source_target_pairs={{0,4},{4,8},{8,12},{12,16},{16,20},{20,24},{24,28},{28,0},{1,5},{5... | collective-permute-start | bytes 1228808 | tf_op jit(solution)/shard_map/while/body/eval_jaxpr/ppermute | solution.py:18
  242.6 9.8 collective-permute-start
  242.7 17.9 %collective-permute-start.1 = (bf16[128,25,64]{0,2,1:T(8,128)(2,1)}, bf16[128,25,64]{0,2,1:T(8,128)(2,1)S(1)}, u32[]{:S(2)}, u32[]{:S(2)}) collective-permute-start(bf16[128,25,64]{0,2,1:T(8,128)(2,1)} %get-tuple-element.1140), channel_id=1, source_target_pairs={{0,4},{4,8},{8,12},{12,16},{16,20},{20,24},{24,28},{28,0},{1,5},{5... | collective-permute-start | bytes 1228808 | tf_op jit(solution)/shard_map/while/body/eval_jaxpr/ppermute | solution.py:18
  261.8 9.8 collective-permute-start
  261.8 17.0 collective-permute-start.1
  280.9 8.1 copy-start.6
  431.1 12.3 copy-start.4
  431.1 13.6 slice-start.2
  431.1 13.6 slice-start.3
  455.2 463.7 %reduce-scatter.5.cloned.1.call-start = ((), (), s32[]{:S(2)}) async-start(), calls=%async_computation.8 | async-start | bytes 19456000 | tf_op jit(solution)/shard_map/reduce_scatter | solution.py:298
  455.3 13.8 collective-permute-start.2
  456.5 41.9 %collective-permute-start.3 = (bf16[128,25,64]{0,2,1:T(8,128)(2,1)}, bf16[128,25,64]{0,2,1:T(8,128)(2,1)S(1)}, u32[]{:S(2)}, u32[]{:S(2)}) collective-permute-start(bf16[128,25,64]{0,2,1:T(8,128)(2,1)} %copy-done.10), channel_id=1, source_target_pairs={{0,4},{4,8},{8,12},{12,16},{16,20},{20,24},{24,28},{28,0},{1,5},{5... | collective-permute-start | bytes 1228808 | tf_op jit(solution)/shard_map/while/body/eval_jaxpr/ppermute | solution.py:18
  457.7 42.2 %collective-permute-start.4 = (bf16[128,25,64]{0,2,1:T(8,128)(2,1)}, bf16[128,25,64]{0,2,1:T(8,128)(2,1)}, u32[]{:S(2)}, u32[]{:S(2)}) collective-permute-start(bf16[128,25,64]{0,2,1:T(8,128)(2,1)} %get-tuple-element.1204), channel_id=1, source_target_pairs={{0,4},{4,8},{8,12},{12,16},{16,20},{20,24},{24,28},{28,0},{1,5},{5... | collective-permute-start | bytes 1228808 | tf_op jit(solution)/shard_map/while/body/eval_jaxpr/ppermute | solution.py:18
  458.9 36.6 %collective-permute-start.5 = (bf16[128,25,64]{0,2,1:T(8,128)(2,1)}, bf16[128,25,64]{0,2,1:T(8,128)(2,1)}, u32[]{:S(2)}, u32[]{:S(2)}) collective-permute-start(bf16[128,25,64]{0,2,1:T(8,128)(2,1)} %get-tuple-element.1205), channel_id=1, source_target_pairs={{0,4},{4,8},{8,12},{12,16},{16,20},{20,24},{24,28},{28,0},{1,5},{5... | collective-permute-start | bytes 1228808 | tf_op jit(solution)/shard_map/while/body/eval_jaxpr/ppermute | solution.py:18
  502.8 12.9 collective-permute-start.2
  503.6 41.4 %collective-permute-start.3 = (bf16[128,25,64]{0,2,1:T(8,128)(2,1)}, bf16[128,25,64]{0,2,1:T(8,128)(2,1)S(1)}, u32[]{:S(2)}, u32[]{:S(2)}) collective-permute-start(bf16[128,25,64]{0,2,1:T(8,128)(2,1)} %copy-done.10), channel_id=1, source_target_pairs={{0,4},{4,8},{8,12},{12,16},{16,20},{20,24},{24,28},{28,0},{1,5},{5... | collective-permute-start | bytes 1228808 | tf_op jit(solution)/shard_map/while/body/eval_jaxpr/ppermute | solution.py:18
  503.6 43.0 %collective-permute-start.4 = (bf16[128,25,64]{0,2,1:T(8,128)(2,1)}, bf16[128,25,64]{0,2,1:T(8,128)(2,1)}, u32[]{:S(2)}, u32[]{:S(2)}) collective-permute-start(bf16[128,25,64]{0,2,1:T(8,128)(2,1)} %get-tuple-element.1204), channel_id=1, source_target_pairs={{0,4},{4,8},{8,12},{12,16},{16,20},{20,24},{24,28},{28,0},{1,5},{5... | collective-permute-start | bytes 1228808 | tf_op jit(solution)/shard_map/while/body/eval_jaxpr/ppermute | solution.py:18
  504.1 38.0 %collective-permute-start.5 = (bf16[128,25,64]{0,2,1:T(8,128)(2,1)}, bf16[128,25,64]{0,2,1:T(8,128)(2,1)}, u32[]{:S(2)}, u32[]{:S(2)}) collective-permute-start(bf16[128,25,64]{0,2,1:T(8,128)(2,1)} %get-tuple-element.1205), channel_id=1, source_target_pairs={{0,4},{4,8},{8,12},{12,16},{16,20},{20,24},{24,28},{28,0},{1,5},{5... | collective-permute-start | bytes 1228808 | tf_op jit(solution)/shard_map/while/body/eval_jaxpr/ppermute | solution.py:18
  549.4 11.9 collective-permute-start.2
  550.2 40.5 %collective-permute-start.3 = (bf16[128,25,64]{0,2,1:T(8,128)(2,1)}, bf16[128,25,64]{0,2,1:T(8,128)(2,1)S(1)}, u32[]{:S(2)}, u32[]{:S(2)}) collective-permute-start(bf16[128,25,64]{0,2,1:T(8,128)(2,1)} %copy-done.10), channel_id=1, source_target_pairs={{0,4},{4,8},{8,12},{12,16},{16,20},{20,24},{24,28},{28,0},{1,5},{5... | collective-permute-start | bytes 1228808 | tf_op jit(solution)/shard_map/while/body/eval_jaxpr/ppermute | solution.py:18
  550.2 42.0 %collective-permute-start.4 = (bf16[128,25,64]{0,2,1:T(8,128)(2,1)}, bf16[128,25,64]{0,2,1:T(8,128)(2,1)}, u32[]{:S(2)}, u32[]{:S(2)}) collective-permute-start(bf16[128,25,64]{0,2,1:T(8,128)(2,1)} %get-tuple-element.1204), channel_id=1, source_target_pairs={{0,4},{4,8},{8,12},{12,16},{16,20},{20,24},{24,28},{28,0},{1,5},{5... | collective-permute-start | bytes 1228808 | tf_op jit(solution)/shard_map/while/body/eval_jaxpr/ppermute | solution.py:18
  550.2 37.6 %collective-permute-start.5 = (bf16[128,25,64]{0,2,1:T(8,128)(2,1)}, bf16[128,25,64]{0,2,1:T(8,128)(2,1)}, u32[]{:S(2)}, u32[]{:S(2)}) collective-permute-start(bf16[128,25,64]{0,2,1:T(8,128)(2,1)} %get-tuple-element.1205), channel_id=1, source_target_pairs={{0,4},{4,8},{8,12},{12,16},{16,20},{20,24},{24,28},{28,0},{1,5},{5... | collective-permute-start | bytes 1228808 | tf_op jit(solution)/shard_map/while/body/eval_jaxpr/ppermute | solution.py:18
  595.1 11.0 collective-permute-start.2
  595.9 39.6 %collective-permute-start.3 = (bf16[128,25,64]{0,2,1:T(8,128)(2,1)}, bf16[128,25,64]{0,2,1:T(8,128)(2,1)S(1)}, u32[]{:S(2)}, u32[]{:S(2)}) collective-permute-start(bf16[128,25,64]{0,2,1:T(8,128)(2,1)} %copy-done.10), channel_id=1, source_target_pairs={{0,4},{4,8},{8,12},{12,16},{16,20},{20,24},{24,28},{28,0},{1,5},{5... | collective-permute-start | bytes 1228808 | tf_op jit(solution)/shard_map/while/body/eval_jaxpr/ppermute | solution.py:18
  595.9 41.1 %collective-permute-start.4 = (bf16[128,25,64]{0,2,1:T(8,128)(2,1)}, bf16[128,25,64]{0,2,1:T(8,128)(2,1)}, u32[]{:S(2)}, u32[]{:S(2)}) collective-permute-start(bf16[128,25,64]{0,2,1:T(8,128)(2,1)} %get-tuple-element.1204), channel_id=1, source_target_pairs={{0,4},{4,8},{8,12},{12,16},{16,20},{20,24},{24,28},{28,0},{1,5},{5... | collective-permute-start | bytes 1228808 | tf_op jit(solution)/shard_map/while/body/eval_jaxpr/ppermute | solution.py:18
  595.9 36.7 %collective-permute-start.5 = (bf16[128,25,64]{0,2,1:T(8,128)(2,1)}, bf16[128,25,64]{0,2,1:T(8,128)(2,1)}, u32[]{:S(2)}, u32[]{:S(2)}) collective-permute-start(bf16[128,25,64]{0,2,1:T(8,128)(2,1)} %get-tuple-element.1205), channel_id=1, source_target_pairs={{0,4},{4,8},{8,12},{12,16},{16,20},{20,24},{24,28},{28,0},{1,5},{5... | collective-permute-start | bytes 1228808 | tf_op jit(solution)/shard_map/while/body/eval_jaxpr/ppermute | solution.py:18
  639.9 10.1 collective-permute-start.2
  640.6 38.7 %collective-permute-start.3 = (bf16[128,25,64]{0,2,1:T(8,128)(2,1)}, bf16[128,25,64]{0,2,1:T(8,128)(2,1)S(1)}, u32[]{:S(2)}, u32[]{:S(2)}) collective-permute-start(bf16[128,25,64]{0,2,1:T(8,128)(2,1)} %copy-done.10), channel_id=1, source_target_pairs={{0,4},{4,8},{8,12},{12,16},{16,20},{20,24},{24,28},{28,0},{1,5},{5... | collective-permute-start | bytes 1228808 | tf_op jit(solution)/shard_map/while/body/eval_jaxpr/ppermute | solution.py:18
  640.6 40.2 %collective-permute-start.4 = (bf16[128,25,64]{0,2,1:T(8,128)(2,1)}, bf16[128,25,64]{0,2,1:T(8,128)(2,1)}, u32[]{:S(2)}, u32[]{:S(2)}) collective-permute-start(bf16[128,25,64]{0,2,1:T(8,128)(2,1)} %get-tuple-element.1204), channel_id=1, source_target_pairs={{0,4},{4,8},{8,12},{12,16},{16,20},{20,24},{24,28},{28,0},{1,5},{5... | collective-permute-start | bytes 1228808 | tf_op jit(solution)/shard_map/while/body/eval_jaxpr/ppermute | solution.py:18
  640.6 35.8 %collective-permute-start.5 = (bf16[128,25,64]{0,2,1:T(8,128)(2,1)}, bf16[128,25,64]{0,2,1:T(8,128)(2,1)}, u32[]{:S(2)}, u32[]{:S(2)}) collective-permute-start(bf16[128,25,64]{0,2,1:T(8,128)(2,1)} %get-tuple-element.1205), channel_id=1, source_target_pairs={{0,4},{4,8},{8,12},{12,16},{16,20},{20,24},{24,28},{28,0},{1,5},{5... | collective-permute-start | bytes 1228808 | tf_op jit(solution)/shard_map/while/body/eval_jaxpr/ppermute | solution.py:18
  683.7 9.8 collective-permute-start.2
  684.5 37.7 %collective-permute-start.3 = (bf16[128,25,64]{0,2,1:T(8,128)(2,1)}, bf16[128,25,64]{0,2,1:T(8,128)(2,1)S(1)}, u32[]{:S(2)}, u32[]{:S(2)}) collective-permute-start(bf16[128,25,64]{0,2,1:T(8,128)(2,1)} %copy-done.10), channel_id=1, source_target_pairs={{0,4},{4,8},{8,12},{12,16},{16,20},{20,24},{24,28},{28,0},{1,5},{5... | collective-permute-start | bytes 1228808 | tf_op jit(solution)/shard_map/while/body/eval_jaxpr/ppermute | solution.py:18
  684.5 39.3 %collective-permute-start.4 = (bf16[128,25,64]{0,2,1:T(8,128)(2,1)}, bf16[128,25,64]{0,2,1:T(8,128)(2,1)}, u32[]{:S(2)}, u32[]{:S(2)}) collective-permute-start(bf16[128,25,64]{0,2,1:T(8,128)(2,1)} %get-tuple-element.1204), channel_id=1, source_target_pairs={{0,4},{4,8},{8,12},{12,16},{16,20},{20,24},{24,28},{28,0},{1,5},{5... | collective-permute-start | bytes 1228808 | tf_op jit(solution)/shard_map/while/body/eval_jaxpr/ppermute | solution.py:18
  684.5 34.8 %collective-permute-start.5 = (bf16[128,25,64]{0,2,1:T(8,128)(2,1)}, bf16[128,25,64]{0,2,1:T(8,128)(2,1)}, u32[]{:S(2)}, u32[]{:S(2)}) collective-permute-start(bf16[128,25,64]{0,2,1:T(8,128)(2,1)} %get-tuple-element.1205), channel_id=1, source_target_pairs={{0,4},{4,8},{8,12},{12,16},{16,20},{20,24},{24,28},{28,0},{1,5},{5... | collective-permute-start | bytes 1228808 | tf_op jit(solution)/shard_map/while/body/eval_jaxpr/ppermute | solution.py:18
  726.6 9.8 collective-permute-start.2
  727.4 36.8 %collective-permute-start.3 = (bf16[128,25,64]{0,2,1:T(8,128)(2,1)}, bf16[128,25,64]{0,2,1:T(8,128)(2,1)S(1)}, u32[]{:S(2)}, u32[]{:S(2)}) collective-permute-start(bf16[128,25,64]{0,2,1:T(8,128)(2,1)} %copy-done.10), channel_id=1, source_target_pairs={{0,4},{4,8},{8,12},{12,16},{16,20},{20,24},{24,28},{28,0},{1,5},{5... | collective-permute-start | bytes 1228808 | tf_op jit(solution)/shard_map/while/body/eval_jaxpr/ppermute | solution.py:18
  727.4 38.4 %collective-permute-start.4 = (bf16[128,25,64]{0,2,1:T(8,128)(2,1)}, bf16[128,25,64]{0,2,1:T(8,128)(2,1)}, u32[]{:S(2)}, u32[]{:S(2)}) collective-permute-start(bf16[128,25,64]{0,2,1:T(8,128)(2,1)} %get-tuple-element.1204), channel_id=1, source_target_pairs={{0,4},{4,8},{8,12},{12,16},{16,20},{20,24},{24,28},{28,0},{1,5},{5... | collective-permute-start | bytes 1228808 | tf_op jit(solution)/shard_map/while/body/eval_jaxpr/ppermute | solution.py:18
  727.4 33.9 %collective-permute-start.5 = (bf16[128,25,64]{0,2,1:T(8,128)(2,1)}, bf16[128,25,64]{0,2,1:T(8,128)(2,1)}, u32[]{:S(2)}, u32[]{:S(2)}) collective-permute-start(bf16[128,25,64]{0,2,1:T(8,128)(2,1)} %get-tuple-element.1205), channel_id=1, source_target_pairs={{0,4},{4,8},{8,12},{12,16},{16,20},{20,24},{24,28},{28,0},{1,5},{5... | collective-permute-start | bytes 1228808 | tf_op jit(solution)/shard_map/while/body/eval_jaxpr/ppermute | solution.py:18
  768.6 9.8 collective-permute-start.7
  768.7 16.0 collective-permute-start.6
  769.0 27.7 %copy-start.14 = (bf16[128,25,64]{0,2,1:T(8,128)(2,1)}, bf16[128,25,64]{0,2,1:T(8,128)(2,1)S(1)}, u32[]{:S(2)}) copy-start(bf16[128,25,64]{0,2,1:T(8,128)(2,1)S(1)} %get-tuple-element.886) | copy-start | bytes 1228804
  778.4 461.0 %copy-start.13 = (bf16[128,25,64]{0,2,1:T(8,128)(2,1)}, bf16[128,25,64]{0,2,1:T(8,128)(2,1)S(1)}, u32[]{:S(2)}) copy-start(bf16[128,25,64]{0,2,1:T(8,128)(2,1)S(1)} %collective-permute-done.7) | copy-start | bytes 1228804
  784.7 12.0 copy-start.16
  796.7 282.0 %reduce-scatter.9.cloned.1.call-start = ((), (), s32[]{:S(2)}) async-start(), calls=%async_computation.10 | async-start | bytes 25600000 | tf_op jit(solution)/shard_map/reduce_scatter | solution.py:316
  810.1 426.6 %reduce-scatter.11.cloned.1.call-start = ((), (), s32[]{:S(2)}) async-start(), calls=%async_computation.11 | async-start | bytes 26624000 | tf_op jit(solution)/shard_map/reduce_scatter | solution.py:322
  825.6 900.4 %all-reduce.22.cloned.1.call-start = ((), (), s32[]{:S(2)}) async-start(), calls=%async_computation.12 | async-start | bytes 31334400 | tf_op jit(solution)/shard_map/psum | solution.py:332
  1239.8 59.6 %copy-start.9 = (f32[128,1600]{0,1:T(8,128)S(1)}, f32[128,1600]{0,1:T(8,128)}, u32[]{:S(2)}) copy-start(f32[128,1600]{0,1:T(8,128)} %copy-done.8) | copy-start | bytes 2457604
  (35 other events, 102.1 us)
Sparse Core Ops, SparseCore 0:
  9.6 101.6 all-gather.6
  112.8 41.0 all-gather.8
  155.5 133.4 all-gather.12
  290.4 128.8 all-gather.10
  455.3 51.5 reduce-scatter.6
  796.8 121.9 reduce-scatter.4
  921.7 157.0 reduce-scatter.8
  1081.4 155.2 reduce-scatter.10
  1242.2 483.8 all-reduce.21
where the time goes:
time: 1750 us
  waiting for transfers between devices  1380 us (79%)
  matrix products  181 us (10%)
  blocking collectives  86.2 us (5%)
  local copies, waits for them, and re-layouts  38.3 us (2%)
  other arithmetic  34.1 us (2%)
  between operations  18.5 us (1%)
    psum x1, waiting for transfers between devices, local(): lax.psum(shard_grads[2].astype(jnp.bfloat16), 'ctx').astype(jnp.float32)  410 us
    ppermute x44, waiting for transfers between devices, passed_along(): return lax.ppermute(x, axis, [(i, (i + by) % size) for i in range(size)])  381 us
    reduce_scatter x1, waiting for transfers between devices, local(): lax.psum_scatter(local_grads[8].astype(jnp.bfloat16), 'shard', scatter_di...  160 us
    reduce_scatter x1, waiting for transfers between devices, local(): lax.psum_scatter(local_grads[10].astype(jnp.bfloat16), 'shard', scatter_d...  158 us
    all_gather x1, waiting for transfers between devices, local(): lax.all_gather(w_fc, 'shard', axis=0, tiled=True)  117 us
    reduce_scatter x1, waiting for transfers between devices, local(): lax.psum_scatter(local_grads[2].astype(jnp.bfloat16), 'shard', scatter_di...  93.2 us
    all_gather x1, waiting for transfers between devices, local(): lax.all_gather(w_qkv, 'shard', axis=0, tiled=True)  54.1 us
  transfers between devices with their start and end apart: 53, of which 37 were waited for; matrix products, arithmetic and copies ran while one was open for 11% of the time, Pallas kernels for 0%

commit v1 on v0

v1 whole, which is shorter than its diff:
```python
import functools
import math

import jax
import jax.numpy as jnp
from jax import lax
from jax.experimental import pallas as pl
from jax.experimental.pallas import tpu as pltpu
from jax.sharding import Mesh, PartitionSpec as P

HEAD_DIM = 64
BLOCK = 256
EPSILON = 1e-05
NEGATIVE = -1e30
SEG_STEP = 65536
BF16 = jnp.bfloat16
F32 = jnp.float32


def attention_forward_kernel(q_ref, k_ref, v_ref, codeq_ref, codek_ref, out_ref, lse_ref):
    heads = q_ref.shape[1] // HEAD_DIM
    code_q = codeq_ref[...]
    low_q = (code_q // SEG_STEP) * SEG_STEP
    code_k = codek_ref[...]
    allowed = jnp.logical_and(code_k >= low_q, code_k <= code_q)
    outs = []
    sums = []
    for h in range(heads):
        cols = slice(h * HEAD_DIM, (h + 1) * HEAD_DIM)
        scores = lax.dot_general(
            q_ref[:, cols], k_ref[:, cols], (((1,), (1,)), ((), ())), preferred_element_type=F32
        )
        scores = jnp.where(allowed, scores, NEGATIVE)
        top = jnp.max(scores, axis=-1, keepdims=True)
        unnorm = jnp.exp(scores - top)
        total = jnp.sum(unnorm, axis=-1, keepdims=True)
        mixed = jnp.dot(unnorm.astype(BF16), v_ref[:, cols], preferred_element_type=F32)
        outs.append((mixed / total).astype(BF16))
        sums.append(top + jnp.log(total))
    out_ref[...] = jnp.concatenate(outs, axis=1)
    lse_ref[...] = jnp.concatenate(sums, axis=1)


def attention_backward_kernel(
    q_ref, k_ref, v_ref, do_ref, lse_ref, codeq_ref, codek_ref, dq_ref, dk_ref, dv_ref, dk_acc, dv_acc
):
    step = pl.program_id(0)
    heads = q_ref.shape[1] // HEAD_DIM

    @pl.when(step == 0)
    def _():
        dk_acc[...] = jnp.zeros_like(dk_acc)
        dv_acc[...] = jnp.zeros_like(dv_acc)

    code_q = codeq_ref[...]
    low_q = (code_q // SEG_STEP) * SEG_STEP
    code_k = codek_ref[...]
    allowed = jnp.logical_and(code_k >= low_q, code_k <= code_q)
    dqs = []
    dks = []
    dvs = []
    contract_last = (((1,), (1,)), ((), ()))
    contract_first = (((0,), (0,)), ((), ()))
    for h in range(heads):
        cols = slice(h * HEAD_DIM, (h + 1) * HEAD_DIM)
        q = q_ref[:, cols]
        do = do_ref[:, cols]
        k = k_ref[:, cols]
        scores = lax.dot_general(q, k, contract_last, preferred_element_type=F32)
        scores = jnp.where(allowed, scores, NEGATIVE)
        probs = jnp.exp(scores - lse_ref[:, h : h + 1])
        dp = lax.dot_general(do, v_ref[:, cols], contract_last, preferred_element_type=F32)
        delta = jnp.sum(probs * dp, axis=-1, keepdims=True)
        ds = (probs * (dp - delta)).astype(BF16)
        dqs.append(jnp.dot(ds, k, preferred_element_type=F32))
        dks.append(lax.dot_general(ds, q, contract_first, preferred_element_type=F32))
        dvs.append(
            lax.dot_general(probs.astype(BF16), do, contract_first, preferred_element_type=F32)
        )
    scale = 1.0 / math.sqrt(HEAD_DIM)
    dq_ref[...] = (jnp.concatenate(dqs, axis=1) * scale).astype(BF16)
    dk_acc[...] += jnp.concatenate(dks, axis=1)
    dv_acc[...] += jnp.concatenate(dvs, axis=1)

    @pl.when(step == pl.num_programs(0) - 1)
    def _():
        dk_ref[...] = dk_acc[...].astype(BF16)
        dv_ref[...] = dv_acc[...].astype(BF16)


QUERY_ROWS = 256


def attention_forward(q, k, v, code):
    tokens, width = q.shape
    heads = width // HEAD_DIM
    rows = min(QUERY_ROWS, tokens)
    row_block = pl.BlockSpec((rows, width), lambda i: (i, 0))
    whole = pl.BlockSpec((tokens, width), lambda i: (0, 0))
    pairs = heads * tokens * tokens
    return pl.pallas_call(
        attention_forward_kernel,
        grid=(tokens // rows,),
        in_specs=[
            row_block,
            whole,
            whole,
            pl.BlockSpec((rows, 1), lambda i: (i, 0)),
            pl.BlockSpec((1, tokens), lambda i: (0, 0)),
        ],
        out_specs=[row_block, pl.BlockSpec((rows, heads), lambda i: (i, 0))],
        out_shape=[
            jax.ShapeDtypeStruct((tokens, width), BF16),
            jax.ShapeDtypeStruct((tokens, heads), F32),
        ],
        compiler_params=pltpu.CompilerParams(vmem_limit_bytes=48 << 20),
        cost_estimate=pl.CostEstimate(
            flops=4 * pairs * HEAD_DIM, bytes_accessed=8 * tokens * width, transcendentals=pairs
        ),
        name="attention_forward",
    )(q, k, v, code.reshape(tokens, 1), code.reshape(1, tokens))


def attention_backward(q, k, v, do, lse, code):
    tokens, width = q.shape
    heads = width // HEAD_DIM
    rows = min(QUERY_ROWS, tokens)
    row_block = pl.BlockSpec((rows, width), lambda i: (i, 0))
    whole = pl.BlockSpec((tokens, width), lambda i: (0, 0))
    pairs = heads * tokens * tokens
    return pl.pallas_call(
        attention_backward_kernel,
        grid=(tokens // rows,),
        in_specs=[
            row_block,
            whole,
            whole,
            row_block,
            pl.BlockSpec((rows, heads), lambda i: (i, 0)),
            pl.BlockSpec((rows, 1), lambda i: (i, 0)),
            pl.BlockSpec((1, tokens), lambda i: (0, 0)),
        ],
        out_specs=[row_block, whole, whole],
        out_shape=[jax.ShapeDtypeStruct((tokens, width), BF16)] * 3,
        scratch_shapes=[pltpu.VMEM((tokens, width), F32)] * 2,
        compiler_params=pltpu.CompilerParams(vmem_limit_bytes=48 << 20),
        cost_estimate=pl.CostEstimate(
            flops=10 * pairs * HEAD_DIM, bytes_accessed=14 * tokens * width, transcendentals=pairs
        ),
        name="attention_backward",
    )(q, k, v, do, lse, code.reshape(tokens, 1), code.reshape(1, tokens))


def swap(x, axis, bit):
    size = lax.axis_size(axis)
    return lax.ppermute(x, axis, [(i, i ^ bit) for i in range(size)])


def bits_of(size):
    return [1 << i for i in range(size.bit_length() - 1)]


def unxor(blocks, index):
    blocks = list(blocks)
    for bit in bits_of(len(blocks)):
        on = (index & bit) != 0
        blocks = [jnp.where(on, blocks[m ^ bit], blocks[m]) for m in range(len(blocks))]
    return blocks


CORE = ("s", 1)


def plane_orders():
    chips = [("s", 2)] + [("r", bit) for bit in bits_of(lax.axis_size("r"))]
    return [chips + [CORE], chips[::-1] + [CORE]]


def plane_gather(x):
    rows = x.shape[0]
    halves = []
    for part, order in enumerate(plane_orders()):
        state = x[part * rows // 2 : (part + 1) * rows // 2][None]
        for axis, bit in order:
            state = jnp.concatenate([state, swap(state, axis, bit)], axis=0)
        halves.append(state)
    return jnp.stack(halves)


def plane_masks():
    found = []
    for order in plane_orders():
        masks = [(0, 0)]
        for axis, bit in order:
            step = (bit, 0) if axis == "s" else (0, bit)
            masks = masks + [(a ^ step[0], b ^ step[1]) for a, b in masks]
        found.append(masks)
    return found


def plane_scatter(partial):
    done = []
    for part, order in enumerate(plane_orders()):
        state = partial[part]
        for axis, bit in order[::-1]:
            keep, send = jnp.split(state, 2, axis=0)
            state = keep.astype(F32) + swap(send.astype(BF16), axis, bit).astype(F32)
        done.append(state[0])
    return jnp.concatenate(done, axis=0)


def sum_over_line(x, backward):
    size = lax.axis_size("z")
    me = lax.axis_index("z")
    order = list(range(size))
    if backward:
        order = order[::-1]
    total = x
    for i in range(size - 1):
        arrived = lax.ppermute(total, "z", [(order[i], order[i + 1])])
        total = (x.astype(F32) + arrived.astype(F32)).astype(BF16)
    current = total
    for i in reversed(range(size - 1)):
        current = lax.ppermute(current, "z", [(order[i + 1], order[i])])
        total = jnp.where(me == order[i], current, total)
    return total


def gather_over_r(x):
    state = x[None]
    for bit in bits_of(lax.axis_size("r")):
        state = jnp.concatenate([state, swap(state, "r", bit)], axis=0)
    return [state[m] for m in range(state.shape[0])]


def sum_everywhere(x):
    for axis in ("s", "r", "z"):
        for bit in bits_of(lax.axis_size(axis)):
            x = x + swap(x, axis, bit)
    return x


def transposed(x):
    z_size, r_size, s_size = (lax.axis_size(a) for a in ("z", "r", "s"))
    perm = [
        ((z * r_size + r) * s_size + s, (s * r_size + r) * s_size + z)
        for z in range(z_size)
        for r in range(r_size)
        for s in range(s_size)
    ]
    return lax.ppermute(x, ("z", "r", "s"), perm)


def gather_over_s(x):
    state = x[None]
    for bit in (2, 1):
        state = jnp.concatenate([state, swap(state, "s", bit)], axis=0)
    return [state[0], state[2], state[1], state[3]]


def norm_parts(values):
    centre = jnp.mean(values, axis=-1, keepdims=True)
    centred = values - centre
    spread = jnp.mean(centred * centred, axis=-1, keepdims=True)
    inverse = lax.rsqrt(spread + EPSILON)
    return centred * inverse, inverse


def norm_backward(grad, normed, inverse, gain):
    scaled = grad * gain
    mean_scaled = jnp.mean(scaled, axis=-1, keepdims=True)
    mean_product = jnp.mean(scaled * normed, axis=-1, keepdims=True)
    grad_in = inverse * (scaled - mean_scaled - normed * mean_product)
    return grad_in, jnp.sum(grad * normed, axis=0), jnp.sum(grad, axis=0)


def gelu_parts(u):
    c = math.sqrt(2.0 / math.pi)
    squared = u * u
    t = jnp.tanh(c * (u + 0.044715 * (u * squared)))
    half = 0.5 * (1.0 + t)
    slope = half + 0.5 * u * (1.0 - t * t) * (c * (1.0 + 3.0 * 0.044715 * squared))
    return u * half, slope


def dot(a, b, contract=((1,), (0,))):
    return lax.dot_general(a, b, (contract, ((), ())), preferred_element_type=F32)


ACROSS_TOKENS = ((0,), (0,))
ON_LAST = ((1,), (1,))


def local(
    inputs,
    positions,
    segments,
    cotangent,
    ln1_gain,
    ln1_bias,
    w_qkv,
    qv_bias,
    w_out,
    out_bias,
    ln2_gain,
    ln2_bias,
    w_fc,
    fc_bias,
    w_proj,
    proj_bias,
):
    s = lax.axis_index("s")
    r = lax.axis_index("r")
    s_size = lax.axis_size("s")
    r_size = lax.axis_size("r")
    devices = s_size * r_size
    me = s * r_size + r
    rows, width = inputs.shape
    heads = width // HEAD_DIM
    tokens = rows * devices
    own_heads = -(-heads // devices)
    own_cols = own_heads * HEAD_DIM
    ff = w_fc.shape[1]
    own_ff = ff // devices
    shard_rows = width // s_size
    score_scale = 1.0 / math.sqrt(HEAD_DIM)

    x_low = transposed(inputs)
    cot_low = transposed(cotangent)
    code = transposed(segments * SEG_STEP + positions // BLOCK)

    small = [ln1_gain, ln1_bias, qv_bias, out_bias, ln2_gain, ln2_bias, proj_bias]
    small_sizes = [a.shape[0] for a in small]
    small_blocks = jnp.stack(unxor(gather_over_s(jnp.concatenate(small)), s))
    small_full = []
    start = 0
    for size in small_sizes:
        small_full.append(small_blocks[:, start : start + size].reshape(-1).astype(F32))
        start += size
    gain_one, bias_one, qv_full, outb_full, gain_two, bias_two, projb_full = small_full

    def head_pad(a):
        missing = own_heads * devices * HEAD_DIM - width
        return jnp.pad(a, [(0, 0)] * (a.ndim - 1) + [(0, missing)])

    qkv_split = jnp.stack(
        [head_pad(part).reshape(shard_rows, devices, own_cols) for part in jnp.split(w_qkv, 3, axis=1)],
        axis=2,
    )
    qkv_split = jnp.transpose(qkv_split, (1, 0, 2, 3)).reshape(devices, shard_rows, 3 * own_cols)

    def for_others(split):
        got = []
        for m in range(s_size):
            mine = lax.dynamic_index_in_dim(split, (s ^ m) * r_size + r, 0, keepdims=False)
            got.append(mine if m == 0 else swap(mine, "s", m))
        return jnp.concatenate(unxor(got, s), axis=0)

    own_qkv = for_others(qkv_split)

    resid = x_low.astype(F32)
    normed_one, inverse_one = norm_parts(resid)
    hidden_one_own = (normed_one * gain_one + bias_one).astype(BF16)
    hidden_one = plane_gather(hidden_one_own).reshape(tokens, width)
    code_all = plane_gather(code).reshape(tokens)
    packed = dot(hidden_one, own_qkv)
    q_bias = lax.dynamic_slice_in_dim(head_pad(qv_full[:width]), me * own_cols, own_cols)
    v_bias = lax.dynamic_slice_in_dim(head_pad(qv_full[width:]), me * own_cols, own_cols)
    queries = (packed[:, :own_cols] + q_bias).astype(BF16) * jnp.asarray(score_scale, BF16)
    keys = packed[:, own_cols : 2 * own_cols].astype(BF16)
    values = (packed[:, 2 * own_cols :] + v_bias).astype(BF16)
    attended, lse = attention_forward(queries, keys, values, code_all)

    att_blocks = attended.reshape(2, devices, rows // 2, own_cols)
    masks = plane_masks()
    got = {}
    for m in range(devices):
        mask = (m // r_size, m % r_size)
        block = jnp.concatenate([att_blocks[part, masks[part].index(mask)] for part in range(2)], axis=0)
        if mask[0]:
            block = swap(block, "s", mask[0]) if not mask[1] else block
        if mask[1] and not mask[0]:
            block = swap(block, "r", mask[1])
        elif mask[0] and mask[1]:
            pairs = [
                (a * s_size + b, (a ^ mask[1]) * s_size + (b ^ mask[0]))
                for a in range(r_size)
                for b in range(s_size)
            ]
            block = lax.ppermute(block, ("r", "s"), pairs)
        got[m] = block
    attended_own = jnp.concatenate(unxor([got[m] for m in range(devices)], me), axis=1)[:, :width]

    full_out = jnp.concatenate(unxor(gather_over_s(w_out), s), axis=0)
    middle = resid + (dot(attended_own, full_out) + outb_full)
    normed_two, inverse_two = norm_parts(middle)
    hidden_two_own = (normed_two * gain_two + bias_two).astype(BF16)
    hidden_two = plane_gather(hidden_two_own).reshape(tokens, width)
    cot = plane_gather(cot_low).reshape(tokens, width)

    fc_split = jnp.stack(jnp.split(w_fc, devices, axis=1))
    own_fc = for_others(fc_split)
    own_fcb = lax.dynamic_slice_in_dim(fc_bias, r * own_ff, own_ff).astype(F32)
    own_proj = lax.dynamic_slice_in_dim(w_proj, r * own_ff, own_ff, axis=0)
    pre_act = dot(hidden_two, own_fc) + own_fcb
    activated, slope = gelu_parts(pre_act)
    activated = activated.astype(BF16)
    grad_act = dot(cot, own_proj, ON_LAST)
    grad_pre = (grad_act * slope).astype(BF16)
    plane_shape = (2, devices, rows // 2, width)
    grad_w_proj = dot(activated, cot, ACROSS_TOKENS).astype(BF16)
    grad_hidden_two = plane_scatter(dot(grad_pre, own_fc, ON_LAST).astype(BF16).reshape(plane_shape))
    grad_w_fc = dot(hidden_two, grad_pre, ACROSS_TOKENS).astype(BF16)
    proj_sum = plane_scatter(dot(activated, own_proj).astype(BF16).reshape(plane_shape))
    output_own = (middle + (proj_sum + projb_full)).astype(BF16)
    grad_fcb = jnp.sum(grad_pre.astype(F32), axis=0)

    cot_own = cot_low.astype(F32)
    grad_in_two, grad_gain_two, grad_bias_two = norm_backward(
        grad_hidden_two, normed_two, inverse_two, gain_two
    )
    grad_middle = cot_own + grad_in_two
    grad_branch_own = grad_middle.astype(BF16)
    grad_outb = jnp.sum(grad_branch_own.astype(F32), axis=0)
    grad_projb = jnp.sum(cot_own, axis=0)
    grad_branch = plane_gather(grad_branch_own).reshape(tokens, width)
    padded_out = jnp.pad(full_out, ((0, own_cols * devices - width), (0, 0)))
    own_out = lax.dynamic_slice_in_dim(padded_out, me * own_cols, own_cols, axis=0)
    grad_attended = dot(grad_branch, own_out, ON_LAST).astype(BF16)
    dq, dk, dv = attention_backward(queries, keys, values, grad_attended, lse, code_all)
    grad_packed = jnp.concatenate([dq, dk, dv], axis=1)

    attended_all = plane_gather(attended_own).reshape(tokens, width)
    own_rows = shard_rows // r_size
    attended_cols = lax.dynamic_slice_in_dim(attended_all, me * own_rows, own_rows, axis=1)
    grad_w_out = dot(attended_cols, grad_branch, ACROSS_TOKENS).astype(BF16)

    grad_hidden_one = plane_scatter(dot(grad_packed, own_qkv, ON_LAST).astype(BF16).reshape(plane_shape))
    grad_w_qkv = dot(hidden_one, grad_packed, ACROSS_TOKENS).astype(BF16)
    grad_in_one, grad_gain_one, grad_bias_one = norm_backward(
        grad_hidden_one, normed_one, inverse_one, gain_one
    )
    input_grad_own = grad_middle + grad_in_one
    output = transposed(output_own)
    input_grad = transposed(input_grad_own.astype(BF16)).astype(F32)

    grad_qb = jnp.sum(dq.astype(F32), axis=0)
    grad_vb = jnp.sum(dv.astype(F32), axis=0)

    def placed(values_in, total, offset):
        zeros = jnp.zeros((total,), F32)
        return lax.dynamic_update_slice_in_dim(zeros, values_in, offset, axis=0)

    head_total = own_cols * devices
    vector = jnp.concatenate(
        [
            grad_gain_one,
            grad_bias_one,
            placed(grad_qb, head_total, me * own_cols)[:width],
            placed(grad_vb, head_total, me * own_cols)[:width],
            grad_outb,
            grad_gain_two,
            grad_bias_two,
            placed(grad_fcb, ff, me * own_ff),
            grad_projb,
        ]
    )
    summed = sum_everywhere(vector)
    pieces = []
    start = 0
    for size in (width, width, 2 * width, width, width, width, ff, width):
        own = size // s_size
        pieces.append(lax.dynamic_slice_in_dim(summed, start + s * own, own))
        start += size
    g_gain_one, g_bias_one, g_qv, g_outb, g_gain_two, g_bias_two, g_fcb, g_projb = pieces

    def rows_home(grad, chunks):
        size = grad.shape[0] // chunks
        parts = [
            sum_over_line(grad[i * size : (i + 1) * size], i % 2 == 1) for i in range(chunks)
        ]
        per_part = [gather_over_r(part) for part in parts]
        by_r = [
            jnp.concatenate([per_part[i][m] for i in range(chunks)], axis=0) for m in range(r_size)
        ]
        return jnp.concatenate(unxor(by_r, r), axis=0).astype(F32)

    def columns_home(grad):
        blocks = unxor(jnp.split(grad, s_size, axis=0), s)
        found = [[None] * s_size for _ in range(r_size)]
        for m in range(s_size):
            part = sum_over_line(blocks[m], m % 2 == 1)
            part = part if m == 0 else swap(part, "s", m)
            for j, block in enumerate(gather_over_r(part)):
                found[j][m] = block
        by_r = [unxor(found[j], s) for j in range(r_size)]
        by_s = [unxor([by_r[j][i] for j in range(r_size)], r) for i in range(s_size)]
        return [by_s[i][j] for i in range(s_size) for j in range(r_size)]

    g_proj = rows_home(grad_w_proj, 4)
    g_fc = jnp.concatenate(columns_home(grad_w_fc), axis=1).astype(F32)
    g_out = rows_home(grad_w_out, 1)
    qkv_blocks = columns_home(grad_w_qkv)
    g_qkv = jnp.concatenate(
        [
            jnp.concatenate([b[:, i * own_cols : (i + 1) * own_cols] for b in qkv_blocks], axis=1)[
                :, :width
            ]
            for i in range(3)
        ],
        axis=1,
    ).astype(F32)

    return (
        output,
        input_grad,
        g_gain_one,
        g_bias_one,
        g_qkv,
        g_qv,
        g_out,
        g_outb,
        g_gain_two,
        g_bias_two,
        g_fc,
        g_fcb,
        g_proj,
        g_projb,
    )


def solution(mesh):
    ctx, shard = mesh.devices.shape
    fine = Mesh(mesh.devices.reshape(shard, ctx // shard, shard), ("z", "r", "s"))
    tokens = ("s", "z", "r")
    arg_specs = (
        P(tokens, None),
        P(tokens),
        P(tokens),
        P(tokens, None),
        P("s"),
        P("s"),
        P("s", None),
        P("s"),
        P("s", None),
        P("s"),
        P("s"),
        P("s"),
        P("s", None),
        P("s"),
        P("s", None),
        P("s"),
    )
    out_specs = (P(tokens, None), P(tokens, None)) + arg_specs[4:]
    return jax.shard_map(local, mesh=fine, in_specs=arg_specs, out_specs=out_specs, check_vma=False)
```

time: 1750 us -> 1100 us (0.63)
  waiting for transfers between devices: 1380 us -> 411 us
  starting transfers between devices: 11.9 us -> 329 us
  matrix products: 181 us -> 48.8 us
  other arithmetic: 34.1 us -> 149 us
  blocking collectives: 86.2 us -> 0 us
  local copies, waits for them, and re-layouts: 38.3 us -> 117 us
  Pallas kernels: 0 us -> 27.8 us
    reduce_scatter x4 -> x0, waiting for transfers between devices: 411 us -> none  [the longest x1 160 us: local(): lax.psum_scatter(local_grads[8].astype(jnp.bfloat16), 'shard', scatter_di...]
    psum x1 -> x0, waiting for transfers between devices: 410 us -> none  [local(): lax.psum(shard_grads[2].astype(jnp.bfloat16), 'ctx').astype(jnp.float32)]
    ppermute x44 -> x178, starting transfers between devices: 11.6 us -> 329 us  [the longest x92 129 us: swap(): return lax.ppermute(x, axis, [(i, i ^ bit) for i in range(size)])]
    all_gather x4 -> x0, waiting for transfers between devices: 174 us -> none  [the longest x1 117 us: local(): lax.all_gather(w_fc, 'shard', axis=0, tiled=True)]
    dot_general x67 -> x12, matrix products: 181 us -> 48.8 us  [dot(): lax.dot_general(a, b, (contract, ((), ())), preferred_element_type=F32)]
    convert_element_type x21 -> x43, other arithmetic: 24.6 us -> 65.1 us  [the longest x32 44.2 us: sum_over_line(): total = (x.astype(F32) + arrived.astype(F32)).astype(BF16)]
    psum x1 -> x0, blocking collectives: 32.8 us -> none  [local(): lax.psum(shard_grads[0].astype(jnp.bfloat16), 'ctx').astype(jnp.float32)]
    select_n x14 -> x25, other arithmetic: 1.16 us -> 31.6 us  [the longest x12 22.1 us: unxor(): jnp.where(on, blocks[m ^ bit], blocks[m])]
  transfers between devices with their start and end apart: 53 -> 178, of which waited for: 37 -> 62; matrix products, arithmetic and copies ran while one was open for 11% -> 23% of each run, Pallas kernels for 0% -> 3%
where the time goes in v1:
time: 1100 us; the launch traced here: 1090 us
  waiting for transfers between devices  411 us (37%)
  starting transfers between devices  329 us (30%)
  other arithmetic  149 us (14%)
  local copies, waits for them, and re-layouts  117 us (11%)
  matrix products  48.8 us (4%)
  Pallas kernels  27.8 us (3%)
    ppermute x92, waiting for transfers between devices, swap(): return lax.ppermute(x, axis, [(i, i ^ bit) for i in range(size)])  265 us
    ppermute x92, starting transfers between devices, swap(): return lax.ppermute(x, axis, [(i, i ^ bit) for i in range(size)])  129 us
    ppermute x39, starting transfers between devices, sum_over_line(): arrived = lax.ppermute(total, 'z', [(order[i], order[i + 1])])  75.9 us
    ppermute x39, starting transfers between devices, sum_over_line(): current = lax.ppermute(current, 'z', [(order[i + 1], order[i])])  69.6 us
    ppermute x39, waiting for transfers between devices, sum_over_line(): arrived = lax.ppermute(total, 'z', [(order[i], order[i + 1])])  67.8 us
    ppermute x39, waiting for transfers between devices, sum_over_line(): current = lax.ppermute(current, 'z', [(order[i + 1], order[i])])  54.5 us
    dot_general x12, matrix products, dot(): lax.dot_general(a, b, (contract, ((), ())), preferred_element_type=F32)  48.8 us
    convert_element_type x32, other arithmetic, sum_over_line(): total = (x.astype(F32) + arrived.astype(F32)).astype(BF16)  44.2 us
  transfers between devices with their start and end apart: 178, of which 62 were waited for; matrix products, arithmetic and copies ran while one was open for 23% of the time, Pallas kernels for 3%

profile of v1, /device:TPU:1, one launch (start us, length us, event | category | flops | bytes accessed | tf_op | source)
XLA Modules:
  0.0 1086.2 jit_solution(5750330731282996036)
XLA Ops:
  0.6 4.9 concatenate.239
  27.0 12.4 %maximum_bitcast_fusion = bf16[8,400,3,256]{3,2,1,0:T(4,128)(2,1)} fusion(bf16[400,8,1,256]{3,2,0,1:T(2,128)(2,1)S(1)} %copy.224, bf16[400,8,1,256]{3,2,0,1:T(2,128)(2,1)S(1)} %copy.223, bf16[400,8,1,256]{3,2,0,1:T(2,128)(2,1)S(1)} %copy.222), kind=kLoop, calls=%fused_computation.1 | loop fusion | flops 14745600 | bytes 9830400 | tf_op jit(solution)/shard_map/transpose | solution.py:350
  39.4 14.0 %reshape.247 = bf16[8,400,768]{2,1,0:T(8,128)(2,1)} reshape(bf16[8,400,3,256]{3,2,1,0:T(4,128)(2,1)} %maximum_bitcast_fusion) | data formatting | bytes 9830400 | tf_op jit(solution)/shard_map/reshape | solution.py:350
  86.3 5.6 collective-permute-start.18
  101.9 9.5 collective-permute-done.44
  111.5 11.6 %collective-permute-start.34 = (bf16[400,800]{1,0:T(8,128)(2,1)}, bf16[400,800]{1,0:T(8,128)(2,1)S(1)}, u32[]{:S(2)}, u32[]{:S(2)}) collective-permute-start(bf16[400,800]{1,0:T(8,128)(2,1)} %get-tuple-element.134), channel_id=1, source_target_pairs={{0,3},{1,2},{2,1},{3,0},{4,7},{5,6},{6,5},{7,4},{8,11},{9,10},{10,... | collective-permute-start | bytes 1920008 | tf_op jit(solution)/shard_map/ppermute | solution.py:156
  131.3 22.6 %collective-permute-done.3 = bf16[1,64,1600]{2,1,0:T(8,128)(2,1)S(1)} collective-permute-done((bf16[1,64,1600]{2,1,0:T(8,128)(2,1)S(1)}, bf16[1,64,1600]{2,1,0:T(8,128)(2,1)S(1)}, u32[]{:S(2)}, u32[]{:S(2)}) %collective-permute-start.3) | collective-permute-done | bytes 204832 | tf_op jit(solution)/shard_map/ppermute | solution.py:156
  155.2 5.1 collective-permute-done.48
  160.8 6.1 collective-permute-done.45
  181.5 5.0 collective-permute-done.49
  194.5 10.1 attention_forward.1
  209.8 6.9 collective-permute-start.19
  224.9 4.8 collective-permute-done.109
  234.2 6.0 collective-permute-done.110
  264.6 7.1 collective-permute-done.32
  284.4 6.1 convolution_convert_fusion.2
  294.8 6.5 convolution_convert_fusion
  301.3 5.0 convolution_convert_fusion.3
  306.3 5.5 convolution_convert_fusion.4
  353.9 4.8 collective-permute-done.127
  360.9 12.1 %collective-permute-done.150 = bf16[200,1600]{1,0:T(8,128)(2,1)S(1)} collective-permute-done((bf16[200,1600]{1,0:T(8,128)(2,1)}, bf16[200,1600]{1,0:T(8,128)(2,1)S(1)}, u32[]{:S(2)}, u32[]{:S(2)}) %collective-permute-start.150) | collective-permute-done | bytes 640032 | tf_op jit(solution)/shard_map/ppermute | solution.py:220
  375.6 4.9 collective-permute-start.164
  387.1 9.6 collective-permute-done.55
  396.8 10.0 collective-permute-done.52
  407.0 8.8 collective-permute-done.41
  416.0 8.0 collective-permute-done.38
  439.5 4.7 collective-permute-done.39
  452.7 30.5 %collective-permute-start.43 = (bf16[128,1600]{1,0:T(8,128)(2,1)S(1)}, bf16[128,1600]{1,0:T(8,128)(2,1)S(1)}, u32[]{:S(2)}, u32[]{:S(2)}) collective-permute-start(bf16[128,1600]{1,0:T(8,128)(2,1)S(1)} %get-tuple-element.208), channel_id=1, source_target_pairs={{0,0},{1,8},{2,16},{3,24},{4,4},{5,12},{6,20},{7,28},{8,1},{9,9},{... | collective-permute-start | bytes 1228808 | tf_op jit(solution)/shard_map/ppermute | solution.py:251
  485.7 8.8 collective-permute-done.43
  510.4 9.6 collective-permute-done.137
  525.8 7.0 collective-permute-done.121
  546.5 17.7 %attention_backward.1 = (bf16[1024,256]{1,0:T(8,128)(2,1)S(1)}, bf16[1024,256]{1,0:T(8,128)(2,1)S(1)}, bf16[1024,256]{1,0:T(8,128)(2,1)S(1)}) custom-call(bf16[1024,256]{1,0:T(8,128)(2,1)S(1)} %get-tuple-element.164.q_ref, bf16[1024,256]{1,0:T(8,128)(2,1)S(1)} %get-tuple-element.163.k_ref, bf16[1024,256]{1,0:T(8,128)(2,1)S(1)} %fusion.55.v_ref, ...), custom_call_target="tpu_custom_call" | custom-call | flops 2684354560 | bytes 3670016 | tf_op jit(solution)/shard_map/attention_backward/pallas_call | solution.py:131
  565.9 5.2 convolution_convert_fusion.1
  574.2 24.5 %collective-permute-start.99 = (bf16[400,768]{1,0:T(8,128)(2,1)S(1)}, bf16[400,768]{1,0:T(8,128)(2,1)}, u32[]{:S(2)}, u32[]{:S(2)}) collective-permute-start(bf16[400,768]{1,0:T(8,128)(2,1)S(1)} %get-tuple-element.197), channel_id=1, source_target_pairs={{0,8},{1,9},{2,10},{3,11},{4,12},{5,13},{6,14},{7,15}} | collective-permute-start | bytes 1843208 | tf_op jit(solution)/shard_map/ppermute | solution.py:220
  652.3 7.8 collective-permute-done.112
  667.0 8.5 collective-permute-done.122
  685.0 9.6 collective-permute-done.67
  694.8 9.6 collective-permute-done.64
  704.5 13.3 %collective-permute-done.148 = bf16[400,800]{1,0:T(8,128)(2,1)S(1)} collective-permute-done((bf16[400,800]{1,0:T(8,128)(2,1)S(1)}, bf16[400,800]{1,0:T(8,128)(2,1)S(1)}, u32[]{:S(2)}, u32[]{:S(2)}) %collective-permute-start.148) | collective-permute-done | bytes 640032 | tf_op jit(solution)/shard_map/ppermute | solution.py:224
  720.1 8.8 collective-permute-start.174
  734.9 6.6 collective-permute-start.70
  751.5 12.6 %collective-permute-start.160 = (bf16[200,1600]{1,0:T(8,128)(2,1)S(1)}, bf16[200,1600]{1,0:T(8,128)(2,1)}, u32[]{:S(2)}, u32[]{:S(2)}) collective-permute-start(bf16[200,1600]{1,0:T(8,128)(2,1)S(1)} %copy-done.38), channel_id=1, source_target_pairs={{0,8},{1,9},{2,10},{3,11},{4,12},{5,13},{6,14},{7,15}} | collective-permute-start | bytes 1920008 | tf_op jit(solution)/shard_map/ppermute | solution.py:224
  766.5 9.3 collective-permute-done.72
  775.8 9.8 collective-permute-start.141
  785.8 4.7 collective-permute-start.73
  795.0 7.3 collective-permute-start.74
  802.8 5.5 collective-permute-done.133
  808.9 14.9 %collective-permute-done.125 = bf16[400,800]{1,0:T(8,128)(2,1)S(1)} collective-permute-done((bf16[400,800]{1,0:T(8,128)(2,1)S(1)}, bf16[400,800]{1,0:T(8,128)(2,1)S(1)}, u32[]{:S(2)}, u32[]{:S(2)}) %collective-permute-start.125) | collective-permute-done | bytes 640032 | tf_op jit(solution)/shard_map/ppermute | solution.py:156
  836.8 11.5 %collective-permute-done.93 = bf16[400,768]{1,0:T(8,128)(2,1)S(1)} collective-permute-done((bf16[400,768]{1,0:T(8,128)(2,1)S(1)}, bf16[400,768]{1,0:T(8,128)(2,1)S(1)}, u32[]{:S(2)}, u32[]{:S(2)}) %collective-permute-start.93) | collective-permute-done | bytes 614432 | tf_op jit(solution)/shard_map/ppermute | solution.py:220
  851.3 12.0 %collective-permute-done.77 = bf16[400,768]{1,0:T(8,128)(2,1)S(1)} collective-permute-done((bf16[400,768]{1,0:T(8,128)(2,1)S(1)}, bf16[400,768]{1,0:T(8,128)(2,1)S(1)}, u32[]{:S(2)}, u32[]{:S(2)}) %collective-permute-start.77) | collective-permute-done | bytes 614432 | tf_op jit(solution)/shard_map/ppermute | solution.py:220
  885.0 11.0 %collective-permute-done.134 = bf16[1,400,800]{2,1,0:T(8,128)(2,1)S(1)} collective-permute-done((bf16[1,400,800]{2,1,0:T(8,128)(2,1)}, bf16[1,400,800]{2,1,0:T(8,128)(2,1)S(1)}, u32[]{:S(2)}, u32[]{:S(2)}) %collective-permute-start.134) | collective-permute-done | bytes 640032 | tf_op jit(solution)/shard_map/ppermute | solution.py:156
  898.2 13.2 %collective-permute-done.126 = bf16[1,400,800]{2,1,0:T(8,128)(2,1)S(1)} collective-permute-done((bf16[1,400,800]{2,1,0:T(8,128)(2,1)}, bf16[1,400,800]{2,1,0:T(8,128)(2,1)S(1)}, u32[]{:S(2)}, u32[]{:S(2)}) %collective-permute-start.126) | collective-permute-done | bytes 640032 | tf_op jit(solution)/shard_map/ppermute | solution.py:156
  937.3 9.7 concatenate.308
  947.0 7.3 convert_element_type.697
  955.0 5.0 collective-permute-done.163
  978.2 6.8 collective-permute-start.81
  985.0 18.9 %collective-permute-done.117 = bf16[200,1600]{1,0:T(8,128)(2,1)S(1)} collective-permute-done((bf16[200,1600]{1,0:T(8,128)(2,1)S(1)}, bf16[200,1600]{1,0:T(8,128)(2,1)S(1)}, u32[]{:S(2)}, u32[]{:S(2)}) %collective-permute-start.117) | collective-permute-done | bytes 640032 | tf_op jit(solution)/shard_map/ppermute | solution.py:224
  1006.0 4.8 maximum_convert_fusion
  1019.7 11.4 %collective-permute-done.105 = bf16[1,400,768]{2,1,0:T(8,128)(2,1)S(1)} collective-permute-done((bf16[1,400,768]{2,1,0:T(8,128)(2,1)S(1)}, bf16[1,400,768]{2,1,0:T(8,128)(2,1)S(1)}, u32[]{:S(2)}, u32[]{:S(2)}) %collective-permute-start.105) | collective-permute-done | bytes 614432 | tf_op jit(solution)/shard_map/ppermute | solution.py:156
  1031.1 13.2 %collective-permute-done.98 = bf16[1,400,768]{2,1,0:T(8,128)(2,1)S(1)} collective-permute-done((bf16[1,400,768]{2,1,0:T(8,128)(2,1)S(1)}, bf16[1,400,768]{2,1,0:T(8,128)(2,1)S(1)}, u32[]{:S(2)}, u32[]{:S(2)}) %collective-permute-start.98) | collective-permute-done | bytes 614432 | tf_op jit(solution)/shard_map/ppermute | solution.py:156
  1044.2 13.2 %collective-permute-done.90 = bf16[1,400,768]{2,1,0:T(8,128)(2,1)S(1)} collective-permute-done((bf16[1,400,768]{2,1,0:T(8,128)(2,1)S(1)}, bf16[1,400,768]{2,1,0:T(8,128)(2,1)S(1)}, u32[]{:S(2)}, u32[]{:S(2)}) %collective-permute-start.90) | collective-permute-done | bytes 614432 | tf_op jit(solution)/shard_map/ppermute | solution.py:156
  1057.4 13.2 %collective-permute-done.82 = bf16[1,400,768]{2,1,0:T(8,128)(2,1)S(1)} collective-permute-done((bf16[1,400,768]{2,1,0:T(8,128)(2,1)S(1)}, bf16[1,400,768]{2,1,0:T(8,128)(2,1)S(1)}, u32[]{:S(2)}, u32[]{:S(2)}) %collective-permute-start.82) | collective-permute-done | bytes 614432 | tf_op jit(solution)/shard_map/ppermute | solution.py:156
  1073.1 6.9 concatenate.300
  1079.9 5.8 convert_element_type.658
  (863 shorter events, 468.4 us)
Async XLA Ops:
  5.6 90.0 %collective-permute-start.1 = (bf16[1,3200]{1,0:T(2,128)(2,1)S(1)}, bf16[1,3200]{1,0:T(2,128)(2,1)S(1)}, u32[]{:S(2)}, u32[]{:S(2)}) collective-permute-start(bf16[1,3200]{1,0:T(2,128)(2,1)S(1)} %broadcast_in_dim.103), channel_id=1, source_target_pairs={{0,2},{1,3},{2,0},{3,1},{4,6},{5,7},{6,4},{7,5},{8,10},{9,11},{10,... | collective-permute-start | bytes 19208 | tf_op jit(solution)/shard_map/ppermute | solution.py:156
  7.7 181.0 %collective-permute-start.26 = (bf16[1,400,1600]{2,1,0:T(8,128)(2,1)}, bf16[1,400,1600]{2,1,0:T(8,128)(2,1)}, u32[]{:S(2)}, u32[]{:S(2)}) collective-permute-start(bf16[1,400,1600]{2,1,0:T(8,128)(2,1)} %bitcast.270), channel_id=1, source_target_pairs={{0,2},{1,3},{2,0},{3,1},{4,6},{5,7},{6,4},{7,5},{8,10},{9,11},{10,... | collective-permute-start | bytes 3840008 | tf_op jit(solution)/shard_map/ppermute | solution.py:156
  9.0 89.6 %collective-permute-start = (bf16[128,1600]{1,0:T(8,128)(2,1)S(1)}, bf16[128,1600]{1,0:T(8,128)(2,1)S(1)}, u32[]{:S(2)}, u32[]{:S(2)}) collective-permute-start(bf16[128,1600]{1,0:T(8,128)(2,1)S(1)} %copy.221), channel_id=1, source_target_pairs={{0,0},{1,8},{2,16},{3,24},{4,4},{5,12},{6,20},{7,28},{8,1},{9,9},{... | collective-permute-start | bytes 1228808 | tf_op jit(solution)/shard_map/ppermute | solution.py:251
  56.3 66.9 %collective-permute-start.9 = (bf16[400,768]{1,0:T(8,128)(2,1)}, bf16[400,768]{1,0:T(8,128)(2,1)}, u32[]{:S(2)}, u32[]{:S(2)}) collective-permute-start(bf16[400,768]{1,0:T(8,128)(2,1)} %get-tuple-element.148), channel_id=1, source_target_pairs={{0,3},{1,2},{2,1},{3,0},{4,7},{5,6},{6,5},{7,4},{8,11},{9,10},{10,... | collective-permute-start | bytes 1843208 | tf_op jit(solution)/shard_map/ppermute | solution.py:156
  93.8 29.4 %collective-permute-start.10 = (bf16[400,768]{1,0:T(8,128)(2,1)}, bf16[400,768]{1,0:T(8,128)(2,1)}, u32[]{:S(2)}, u32[]{:S(2)}) collective-permute-start(bf16[400,768]{1,0:T(8,128)(2,1)} %get-tuple-element.147), channel_id=1, source_target_pairs={{0,2},{1,3},{2,0},{3,1},{4,6},{5,7},{6,4},{7,5},{8,10},{9,11},{10,... | collective-permute-start | bytes 1843208 | tf_op jit(solution)/shard_map/ppermute | solution.py:156
  111.5 56.4 %collective-permute-start.34 = (bf16[400,800]{1,0:T(8,128)(2,1)}, bf16[400,800]{1,0:T(8,128)(2,1)S(1)}, u32[]{:S(2)}, u32[]{:S(2)}) collective-permute-start(bf16[400,800]{1,0:T(8,128)(2,1)} %get-tuple-element.134), channel_id=1, source_target_pairs={{0,3},{1,2},{2,1},{3,0},{4,7},{5,6},{6,5},{7,4},{8,11},{9,10},{10,... | collective-permute-start | bytes 1920008 | tf_op jit(solution)/shard_map/ppermute | solution.py:156
  123.2 46.0 %collective-permute-start.35 = (bf16[400,800]{1,0:T(8,128)(2,1)S(1)}, bf16[400,800]{1,0:T(8,128)(2,1)S(1)}, u32[]{:S(2)}, u32[]{:S(2)}) collective-permute-start(bf16[400,800]{1,0:T(8,128)(2,1)S(1)} %copy-done.87), channel_id=1, source_target_pairs={{0,2},{1,3},{2,0},{3,1},{4,6},{5,7},{6,4},{7,5},{8,10},{9,11},{10,... | collective-permute-start | bytes 1920008 | tf_op jit(solution)/shard_map/ppermute | solution.py:156
  123.3 46.6 %collective-permute-start.36 = (bf16[400,800]{1,0:T(8,128)(2,1)S(1)}, bf16[400,800]{1,0:T(8,128)(2,1)S(1)}, u32[]{:S(2)}, u32[]{:S(2)}) collective-permute-start(bf16[400,800]{1,0:T(8,128)(2,1)S(1)} %copy-done.86), channel_id=1, source_target_pairs={{0,1},{1,0},{2,3},{3,2},{4,5},{5,4},{6,7},{7,6},{8,9},{9,8},{10,11... | collective-permute-start | bytes 1920008 | tf_op jit(solution)/shard_map/ppermute | solution.py:156
  318.9 56.7 %collective-permute-start.54 = (bf16[4,64,1600]{2,1,0:T(8,128)(2,1)}, bf16[4,64,1600]{2,1,0:T(8,128)(2,1)}, u32[]{:S(2)}, u32[]{:S(2)}) collective-permute-start(bf16[4,64,1600]{2,1,0:T(8,128)(2,1)} %bitcast.286), channel_id=1, source_target_pairs={{0,1},{1,0},{2,3},{3,2},{4,5},{5,4},{6,7},{7,6},{8,9},{9,8},{10,11... | collective-permute-start | bytes 2457608 | tf_op jit(solution)/shard_map/ppermute | solution.py:156
  320.2 61.7 %collective-permute-start.51 = (bf16[4,64,1600]{2,1,0:T(8,128)(2,1)}, bf16[4,64,1600]{2,1,0:T(8,128)(2,1)}, u32[]{:S(2)}, u32[]{:S(2)}) collective-permute-start(bf16[4,64,1600]{2,1,0:T(8,128)(2,1)} %bitcast.285), channel_id=1, source_target_pairs={{0,1},{1,0},{2,3},{3,2},{4,5},{5,4},{6,7},{7,6},{8,9},{9,8},{10,11... | collective-permute-start | bytes 2457608 | tf_op jit(solution)/shard_map/ppermute | solution.py:156
  352.0 32.2 %collective-permute-start.40 = (bf16[4,64,1600]{2,1,0:T(8,128)(2,1)S(1)}, bf16[4,64,1600]{2,1,0:T(8,128)(2,1)S(1)}, u32[]{:S(2)}, u32[]{:S(2)}) collective-permute-start(bf16[4,64,1600]{2,1,0:T(8,128)(2,1)S(1)} %bitcast.288), channel_id=1, source_target_pairs={{0,1},{1,0},{2,3},{3,2},{4,5},{5,4},{6,7},{7,6},{8,9},{9,8},{10,11... | collective-permute-start | bytes 2457608 | tf_op jit(solution)/shard_map/ppermute | solution.py:156
  373.8 125.8 %collective-permute-start.157 = (bf16[200,1600]{1,0:T(8,128)(2,1)}, bf16[200,1600]{1,0:T(8,128)(2,1)}, u32[]{:S(2)}, u32[]{:S(2)}) collective-permute-start(bf16[200,1600]{1,0:T(8,128)(2,1)} %get-tuple-element.182), channel_id=1, source_target_pairs={{24,16},{25,17},{26,18},{27,19},{28,20},{29,21},{30,22},{31,23}} | collective-permute-start | bytes 1920008 | tf_op jit(solution)/shard_map/ppermute | solution.py:220
  375.6 125.5 %collective-permute-start.164 = (bf16[200,1600]{1,0:T(8,128)(2,1)}, bf16[200,1600]{1,0:T(8,128)(2,1)}, u32[]{:S(2)}, u32[]{:S(2)}) collective-permute-start(bf16[200,1600]{1,0:T(8,128)(2,1)} %get-tuple-element.181), channel_id=1, source_target_pairs={{0,8},{1,9},{2,10},{3,11},{4,12},{5,13},{6,14},{7,15}} | collective-permute-start | bytes 1920008 | tf_op jit(solution)/shard_map/ppermute | solution.py:220
  381.9 42.9 %collective-permute-start.144 = (bf16[400,800]{1,0:T(8,128)(2,1)S(1)}, bf16[400,800]{1,0:T(8,128)(2,1)S(1)}, u32[]{:S(2)}, u32[]{:S(2)}) collective-permute-start(bf16[400,800]{1,0:T(8,128)(2,1)S(1)} %fusion.25), channel_id=1, source_target_pairs={{8,16},{9,17},{10,18},{11,19},{12,20},{13,21},{14,22},{15,23}} | collective-permute-start | bytes 1920008 | tf_op jit(solution)/shard_map/ppermute | solution.py:220
  384.1 44.6 %collective-permute-start.136 = (bf16[400,800]{1,0:T(8,128)(2,1)S(1)}, bf16[400,800]{1,0:T(8,128)(2,1)S(1)}, u32[]{:S(2)}, u32[]{:S(2)}) collective-permute-start(bf16[400,800]{1,0:T(8,128)(2,1)S(1)} %fusion.22), channel_id=1, source_target_pairs={{16,8},{17,9},{18,10},{19,11},{20,12},{21,13},{22,14},{23,15}} | collective-permute-start | bytes 1920008 | tf_op jit(solution)/shard_map/ppermute | solution.py:220
  449.7 52.1 %collective-permute-start.171 = (bf16[200,1600]{1,0:T(8,128)(2,1)}, bf16[200,1600]{1,0:T(8,128)(2,1)}, u32[]{:S(2)}, u32[]{:S(2)}) collective-permute-start(bf16[200,1600]{1,0:T(8,128)(2,1)} %get-tuple-element.180), channel_id=1, source_target_pairs={{24,16},{25,17},{26,18},{27,19},{28,20},{29,21},{30,22},{31,23}} | collective-permute-start | bytes 1920008 | tf_op jit(solution)/shard_map/ppermute | solution.py:220
  451.2 51.9 %collective-permute-start.152 = (bf16[200,1600]{1,0:T(8,128)(2,1)}, bf16[200,1600]{1,0:T(8,128)(2,1)}, u32[]{:S(2)}, u32[]{:S(2)}) collective-permute-start(bf16[200,1600]{1,0:T(8,128)(2,1)} %fusion.32), channel_id=1, source_target_pairs={{16,24},{17,25},{18,26},{19,27},{20,28},{21,29},{22,30},{23,31}} | collective-permute-start | bytes 1920008 | tf_op jit(solution)/shard_map/ppermute | solution.py:220
  452.7 41.8 %collective-permute-start.43 = (bf16[128,1600]{1,0:T(8,128)(2,1)S(1)}, bf16[128,1600]{1,0:T(8,128)(2,1)S(1)}, u32[]{:S(2)}, u32[]{:S(2)}) collective-permute-start(bf16[128,1600]{1,0:T(8,128)(2,1)S(1)} %get-tuple-element.208), channel_id=1, source_target_pairs={{0,0},{1,8},{2,16},{3,24},{4,4},{5,12},{6,20},{7,28},{8,1},{9,9},{... | collective-permute-start | bytes 1228808 | tf_op jit(solution)/shard_map/ppermute | solution.py:251
  501.8 31.1 %collective-permute-start.121 = (bf16[400,800]{1,0:T(8,128)(2,1)}, bf16[400,800]{1,0:T(8,128)(2,1)S(1)}, u32[]{:S(2)}, u32[]{:S(2)}) collective-permute-start(bf16[400,800]{1,0:T(8,128)(2,1)} %fusion.17), channel_id=1, source_target_pairs={{8,0},{9,1},{10,2},{11,3},{12,4},{13,5},{14,6},{15,7}} | collective-permute-start | bytes 1920008 | tf_op jit(solution)/shard_map/ppermute | solution.py:220
  503.1 31.7 %collective-permute-start.61 = (bf16[2,64,1600]{2,1,0:T(8,128)(2,1)}, bf16[2,64,1600]{2,1,0:T(8,128)(2,1)S(1)}, u32[]{:S(2)}, u32[]{:S(2)}) collective-permute-start(bf16[2,64,1600]{2,1,0:T(8,128)(2,1)} %pad_maximum_fusion.32), channel_id=1, source_target_pairs={{0,2},{1,3},{2,0},{3,1},{4,6},{5,7},{6,4},{7,5},{8,10},{9,11},{10,... | collective-permute-start | bytes 1228808 | tf_op jit(solution)/shard_map/ppermute | solution.py:156
  507.9 28.6 %collective-permute-start.58 = (bf16[2,64,1600]{2,1,0:T(8,128)(2,1)S(1)}, bf16[2,64,1600]{2,1,0:T(8,128)(2,1)S(1)}, u32[]{:S(2)}, u32[]{:S(2)}) collective-permute-start(bf16[2,64,1600]{2,1,0:T(8,128)(2,1)S(1)} %copy-done.111), channel_id=1, source_target_pairs={{0,4},{4,0},{1,5},{5,1},{2,6},{6,2},{3,7},{7,3},{8,12},{12,8},{9,1... | collective-permute-start | bytes 1228808 | tf_op jit(solution)/shard_map/ppermute | solution.py:156
  534.8 90.1 %collective-permute-start.146 = (bf16[400,800]{1,0:T(8,128)(2,1)}, bf16[400,800]{1,0:T(8,128)(2,1)}, u32[]{:S(2)}, u32[]{:S(2)}) collective-permute-start(bf16[400,800]{1,0:T(8,128)(2,1)} %fusion.27), channel_id=1, source_target_pairs={{24,16},{25,17},{26,18},{27,19},{28,20},{29,21},{30,22},{31,23}} | collective-permute-start | bytes 1920008 | tf_op jit(solution)/shard_map/ppermute | solution.py:224
  538.9 77.1 %collective-permute-start.159 = (bf16[200,1600]{1,0:T(8,128)(2,1)}, bf16[200,1600]{1,0:T(8,128)(2,1)}, u32[]{:S(2)}, u32[]{:S(2)}) collective-permute-start(bf16[200,1600]{1,0:T(8,128)(2,1)} %get-tuple-element.186), channel_id=1, source_target_pairs={{8,0},{9,1},{10,2},{11,3},{12,4},{13,5},{14,6},{15,7}} | collective-permute-start | bytes 1920008 | tf_op jit(solution)/shard_map/ppermute | solution.py:220
  540.3 76.4 %collective-permute-start.166 = (bf16[200,1600]{1,0:T(8,128)(2,1)}, bf16[200,1600]{1,0:T(8,128)(2,1)}, u32[]{:S(2)}, u32[]{:S(2)}) collective-permute-start(bf16[200,1600]{1,0:T(8,128)(2,1)} %get-tuple-element.187), channel_id=1, source_target_pairs={{16,24},{17,25},{18,26},{19,27},{20,28},{21,29},{22,30},{23,31}} | collective-permute-start | bytes 1920008 | tf_op jit(solution)/shard_map/ppermute | solution.py:220
  541.8 75.6 %collective-permute-start.173 = (bf16[200,1600]{1,0:T(8,128)(2,1)}, bf16[200,1600]{1,0:T(8,128)(2,1)}, u32[]{:S(2)}, u32[]{:S(2)}) collective-permute-start(bf16[200,1600]{1,0:T(8,128)(2,1)} %get-tuple-element.188), channel_id=1, source_target_pairs={{8,0},{9,1},{10,2},{11,3},{12,4},{13,5},{14,6},{15,7}} | collective-permute-start | bytes 1920008 | tf_op jit(solution)/shard_map/ppermute | solution.py:220
  574.2 44.6 %collective-permute-start.99 = (bf16[400,768]{1,0:T(8,128)(2,1)S(1)}, bf16[400,768]{1,0:T(8,128)(2,1)}, u32[]{:S(2)}, u32[]{:S(2)}) collective-permute-start(bf16[400,768]{1,0:T(8,128)(2,1)S(1)} %get-tuple-element.197), channel_id=1, source_target_pairs={{0,8},{1,9},{2,10},{3,11},{4,12},{5,13},{6,14},{7,15}} | collective-permute-start | bytes 1843208 | tf_op jit(solution)/shard_map/ppermute | solution.py:220
  630.5 29.6 %collective-permute-start.112 = (bf16[200,1600]{1,0:T(8,128)(2,1)S(1)}, bf16[200,1600]{1,0:T(8,128)(2,1)S(1)}, u32[]{:S(2)}, u32[]{:S(2)}) collective-permute-start(bf16[200,1600]{1,0:T(8,128)(2,1)S(1)} %convolution_convert_fusion.6), channel_id=1, source_target_pairs={{0,8},{1,9},{2,10},{3,11},{4,12},{5,13},{6,14},{7,15}} | collective-permute-start | bytes 1920008 | tf_op jit(solution)/shard_map/ppermute | solution.py:220
  635.7 29.7 %collective-permute-start.66 = (bf16[4,64,1600]{2,1,0:T(8,128)(2,1)S(1)}, bf16[4,64,1600]{2,1,0:T(8,128)(2,1)S(1)}, u32[]{:S(2)}, u32[]{:S(2)}) collective-permute-start(bf16[4,64,1600]{2,1,0:T(8,128)(2,1)S(1)} %bitcast.284), channel_id=1, source_target_pairs={{0,1},{1,0},{2,3},{3,2},{4,5},{5,4},{6,7},{7,6},{8,9},{9,8},{10,11... | collective-permute-start | bytes 2457608 | tf_op jit(solution)/shard_map/ppermute | solution.py:156
  645.9 29.6 %collective-permute-start.122 = (bf16[400,800]{1,0:T(8,128)(2,1)S(1)}, bf16[400,800]{1,0:T(8,128)(2,1)S(1)}, u32[]{:S(2)}, u32[]{:S(2)}) collective-permute-start(bf16[400,800]{1,0:T(8,128)(2,1)S(1)} %copy-done.35), channel_id=1, source_target_pairs={{0,8},{1,9},{2,10},{3,11},{4,12},{5,13},{6,14},{7,15}} | collective-permute-start | bytes 1920008 | tf_op jit(solution)/shard_map/ppermute | solution.py:224
  650.8 27.8 %collective-permute-start.131 = (bf16[400,800]{1,0:T(8,128)(2,1)S(1)}, bf16[400,800]{1,0:T(8,128)(2,1)}, u32[]{:S(2)}, u32[]{:S(2)}) collective-permute-start(bf16[400,800]{1,0:T(8,128)(2,1)S(1)} %collective-permute-done.130), channel_id=1, source_target_pairs={{16,8},{17,9},{18,10},{19,11},{20,12},{21,13},{22,14},{23,15}} | collective-permute-start | bytes 1920008 | tf_op jit(solution)/shard_map/ppermute | solution.py:224
  675.5 44.5 %collective-permute-start.139 = (bf16[400,800]{1,0:T(8,128)(2,1)S(1)}, bf16[400,800]{1,0:T(8,128)(2,1)}, u32[]{:S(2)}, u32[]{:S(2)}) collective-permute-start(bf16[400,800]{1,0:T(8,128)(2,1)S(1)} %collective-permute-done.138), channel_id=1, source_target_pairs={{8,16},{9,17},{10,18},{11,19},{12,20},{13,21},{14,22},{15,23}} | collective-permute-start | bytes 1920008 | tf_op jit(solution)/shard_map/ppermute | solution.py:224
  677.1 51.8 %collective-permute-start.123 = (bf16[400,800]{1,0:T(8,128)(2,1)S(1)}, bf16[400,800]{1,0:T(8,128)(2,1)}, u32[]{:S(2)}, u32[]{:S(2)}) collective-permute-start(bf16[400,800]{1,0:T(8,128)(2,1)S(1)} %collective-permute-done.122), channel_id=1, source_target_pairs={{8,16},{9,17},{10,18},{11,19},{12,20},{13,21},{14,22},{15,23}} | collective-permute-start | bytes 1920008 | tf_op jit(solution)/shard_map/ppermute | solution.py:224
  678.6 39.2 %collective-permute-start.148 = (bf16[400,800]{1,0:T(8,128)(2,1)S(1)}, bf16[400,800]{1,0:T(8,128)(2,1)S(1)}, u32[]{:S(2)}, u32[]{:S(2)}) collective-permute-start(bf16[400,800]{1,0:T(8,128)(2,1)S(1)} %collective-permute-done.147), channel_id=1, source_target_pairs={{8,0},{9,1},{10,2},{11,3},{12,4},{13,5},{14,6},{15,7}} | collective-permute-start | bytes 1920008 | tf_op jit(solution)/shard_map/ppermute | solution.py:224
  679.9 55.0 %collective-permute-start.132 = (bf16[400,800]{1,0:T(8,128)(2,1)}, bf16[400,800]{1,0:T(8,128)(2,1)}, u32[]{:S(2)}, u32[]{:S(2)}) collective-permute-start(bf16[400,800]{1,0:T(8,128)(2,1)} %collective-permute-done.131), channel_id=1, source_target_pairs={{8,0},{9,1},{10,2},{11,3},{12,4},{13,5},{14,6},{15,7}} | collective-permute-start | bytes 1920008 | tf_op jit(solution)/shard_map/ppermute | solution.py:224
  720.1 31.4 %collective-permute-start.174 = (bf16[200,1600]{1,0:T(8,128)(2,1)}, bf16[200,1600]{1,0:T(8,128)(2,1)}, u32[]{:S(2)}, u32[]{:S(2)}) collective-permute-start(bf16[200,1600]{1,0:T(8,128)(2,1)} %get-tuple-element.185), channel_id=1, source_target_pairs={{0,8},{1,9},{2,10},{3,11},{4,12},{5,13},{6,14},{7,15}} | collective-permute-start | bytes 1920008 | tf_op jit(solution)/shard_map/ppermute | solution.py:224
  749.5 36.3 %collective-permute-start.76 = (bf16[400,768]{1,0:T(8,128)(2,1)S(1)}, bf16[400,768]{1,0:T(8,128)(2,1)S(1)}, u32[]{:S(2)}, u32[]{:S(2)}) collective-permute-start(bf16[400,768]{1,0:T(8,128)(2,1)S(1)} %copy-done.97), channel_id=1, source_target_pairs={{16,8},{17,9},{18,10},{19,11},{20,12},{21,13},{22,14},{23,15}} | collective-permute-start | bytes 1843208 | tf_op jit(solution)/shard_map/ppermute | solution.py:220
  751.5 39.2 %collective-permute-start.160 = (bf16[200,1600]{1,0:T(8,128)(2,1)S(1)}, bf16[200,1600]{1,0:T(8,128)(2,1)}, u32[]{:S(2)}, u32[]{:S(2)}) collective-permute-start(bf16[200,1600]{1,0:T(8,128)(2,1)S(1)} %copy-done.38), channel_id=1, source_target_pairs={{0,8},{1,9},{2,10},{3,11},{4,12},{5,13},{6,14},{7,15}} | collective-permute-start | bytes 1920008 | tf_op jit(solution)/shard_map/ppermute | solution.py:224
  764.1 28.0 %collective-permute-start.113 = (bf16[200,1600]{1,0:T(8,128)(2,1)S(1)}, bf16[200,1600]{1,0:T(8,128)(2,1)S(1)}, u32[]{:S(2)}, u32[]{:S(2)}) collective-permute-start(bf16[200,1600]{1,0:T(8,128)(2,1)S(1)} %copy-done.94), channel_id=1, source_target_pairs={{8,16},{9,17},{10,18},{11,19},{12,20},{13,21},{14,22},{15,23}} | collective-permute-start | bytes 1920008 | tf_op jit(solution)/shard_map/ppermute | solution.py:220
  764.8 27.7 %collective-permute-start.149 = (bf16[1,400,800]{2,1,0:T(8,128)(2,1)S(1)}, bf16[1,400,800]{2,1,0:T(8,128)(2,1)S(1)}, u32[]{:S(2)}, u32[]{:S(2)}) collective-permute-start(bf16[1,400,800]{2,1,0:T(8,128)(2,1)S(1)} %bitcast.279), channel_id=1, source_target_pairs={{0,4},{4,0},{1,5},{5,1},{2,6},{6,2},{3,7},{7,3},{8,12},{12,8},{9,1... | collective-permute-start | bytes 1920008 | tf_op jit(solution)/shard_map/ppermute | solution.py:156
  792.1 31.7 %collective-permute-start.125 = (bf16[400,800]{1,0:T(8,128)(2,1)S(1)}, bf16[400,800]{1,0:T(8,128)(2,1)S(1)}, u32[]{:S(2)}, u32[]{:S(2)}) collective-permute-start(bf16[400,800]{1,0:T(8,128)(2,1)S(1)} %select_select_fusion.3), channel_id=1, source_target_pairs={{0,3},{1,2},{2,1},{3,0},{4,7},{5,6},{6,5},{7,4},{8,11},{9,10},{10,... | collective-permute-start | bytes 1920008 | tf_op jit(solution)/shard_map/ppermute | solution.py:156
  792.5 32.6 %collective-permute-start.175 = (bf16[200,1600]{1,0:T(8,128)(2,1)}, bf16[200,1600]{1,0:T(8,128)(2,1)}, u32[]{:S(2)}, u32[]{:S(2)}) collective-permute-start(bf16[200,1600]{1,0:T(8,128)(2,1)} %collective-permute-done.174), channel_id=1, source_target_pairs={{8,16},{9,17},{10,18},{11,19},{12,20},{13,21},{14,22},{15,23}} | collective-permute-start | bytes 1920008 | tf_op jit(solution)/shard_map/ppermute | solution.py:224
  794.3 32.9 %collective-permute-start.101 = (bf16[400,768]{1,0:T(8,128)(2,1)S(1)}, bf16[400,768]{1,0:T(8,128)(2,1)S(1)}, u32[]{:S(2)}, u32[]{:S(2)}) collective-permute-start(bf16[400,768]{1,0:T(8,128)(2,1)S(1)} %fusion.53), channel_id=1, source_target_pairs={{16,24},{17,25},{18,26},{19,27},{20,28},{21,29},{22,30},{23,31}} | collective-permute-start | bytes 1843208 | tf_op jit(solution)/shard_map/ppermute | solution.py:220
  795.0 30.8 %collective-permute-start.74 = (f32[19200]{0:T(1024)S(1)}, f32[19200]{0:T(1024)S(1)}, u32[]{:S(2)}, u32[]{:S(2)}) collective-permute-start(f32[19200]{0:T(1024)S(1)} %add.447), channel_id=1, source_target_pairs={{0,16},{8,24},{16,0},{24,8},{1,17},{9,25},{17,1},{25,9},{2,18},{10... | collective-permute-start | bytes 230408 | tf_op jit(solution)/shard_map/ppermute | solution.py:156
  808.2 27.4 %collective-permute-start.168 = (bf16[200,1600]{1,0:T(8,128)(2,1)S(1)}, bf16[200,1600]{1,0:T(8,128)(2,1)S(1)}, u32[]{:S(2)}, u32[]{:S(2)}) collective-permute-start(bf16[200,1600]{1,0:T(8,128)(2,1)S(1)} %collective-permute-done.167), channel_id=1, source_target_pairs={{16,8},{17,9},{18,10},{19,11},{20,12},{21,13},{22,14},{23,15}} | collective-permute-start | bytes 1920008 | tf_op jit(solution)/shard_map/ppermute | solution.py:224
  825.9 37.5 %collective-permute-start.77 = (bf16[400,768]{1,0:T(8,128)(2,1)S(1)}, bf16[400,768]{1,0:T(8,128)(2,1)S(1)}, u32[]{:S(2)}, u32[]{:S(2)}) collective-permute-start(bf16[400,768]{1,0:T(8,128)(2,1)S(1)} %fusion.44), channel_id=1, source_target_pairs={{8,0},{9,1},{10,2},{11,3},{12,4},{13,5},{14,6},{15,7}} | collective-permute-start | bytes 1843208 | tf_op jit(solution)/shard_map/ppermute | solution.py:220
  827.2 41.4 %collective-permute-start.69 = (bf16[128,1600]{1,0:T(8,128)(2,1)S(1)}, bf16[128,1600]{1,0:T(8,128)(2,1)S(1)}, u32[]{:S(2)}, u32[]{:S(2)}) collective-permute-start(bf16[128,1600]{1,0:T(8,128)(2,1)S(1)} %fusion.69), channel_id=1, source_target_pairs={{0,0},{1,8},{2,16},{3,24},{4,4},{5,12},{6,20},{7,28},{8,1},{9,9},{... | collective-permute-start | bytes 1228808 | tf_op jit(solution)/shard_map/ppermute | solution.py:251
  835.6 41.0 %collective-permute-start.156 = (bf16[1,200,1600]{2,1,0:T(8,128)(2,1)}, bf16[1,200,1600]{2,1,0:T(8,128)(2,1)}, u32[]{:S(2)}, u32[]{:S(2)}) collective-permute-start(bf16[1,200,1600]{2,1,0:T(8,128)(2,1)} %bitcast.103), channel_id=1, source_target_pairs={{0,4},{4,0},{1,5},{5,1},{2,6},{6,2},{3,7},{7,3},{8,12},{12,8},{9,1... | collective-permute-start | bytes 1920008 | tf_op jit(solution)/shard_map/ppermute | solution.py:156
  876.6 34.7 %collective-permute-start.126 = (bf16[1,400,800]{2,1,0:T(8,128)(2,1)}, bf16[1,400,800]{2,1,0:T(8,128)(2,1)S(1)}, u32[]{:S(2)}, u32[]{:S(2)}) collective-permute-start(bf16[1,400,800]{2,1,0:T(8,128)(2,1)} %bitcast.290), channel_id=1, source_target_pairs={{0,4},{4,0},{1,5},{5,1},{2,6},{6,2},{3,7},{7,3},{8,12},{12,8},{9,1... | collective-permute-start | bytes 1920008 | tf_op jit(solution)/shard_map/ppermute | solution.py:156
  876.7 36.1 %collective-permute-start.169 = (bf16[200,1600]{1,0:T(8,128)(2,1)}, bf16[200,1600]{1,0:T(8,128)(2,1)S(1)}, u32[]{:S(2)}, u32[]{:S(2)}) collective-permute-start(bf16[200,1600]{1,0:T(8,128)(2,1)} %copy-done.92), channel_id=1, source_target_pairs={{8,0},{9,1},{10,2},{11,3},{12,4},{13,5},{14,6},{15,7}} | collective-permute-start | bytes 1920008 | tf_op jit(solution)/shard_map/ppermute | solution.py:224
  880.7 34.2 %collective-permute-start.162 = (bf16[200,1600]{1,0:T(8,128)(2,1)}, bf16[200,1600]{1,0:T(8,128)(2,1)S(1)}, u32[]{:S(2)}, u32[]{:S(2)}) collective-permute-start(bf16[200,1600]{1,0:T(8,128)(2,1)} %collective-permute-done.161), channel_id=1, source_target_pairs={{16,24},{17,25},{18,26},{19,27},{20,28},{21,29},{22,30},{23,31}} | collective-permute-start | bytes 1920008 | tf_op jit(solution)/shard_map/ppermute | solution.py:224
  881.5 34.2 %collective-permute-start.102 = (bf16[400,768]{1,0:T(8,128)(2,1)S(1)}, bf16[400,768]{1,0:T(8,128)(2,1)S(1)}, u32[]{:S(2)}, u32[]{:S(2)}) collective-permute-start(bf16[400,768]{1,0:T(8,128)(2,1)S(1)} %copy-done.45), channel_id=1, source_target_pairs={{24,16},{25,17},{26,18},{27,19},{28,20},{29,21},{30,22},{31,23}} | collective-permute-start | bytes 1843208 | tf_op jit(solution)/shard_map/ppermute | solution.py:224
  920.2 34.0 %collective-permute-start.170 = (bf16[1,200,1600]{2,1,0:T(8,128)(2,1)}, bf16[1,200,1600]{2,1,0:T(8,128)(2,1)}, u32[]{:S(2)}, u32[]{:S(2)}) collective-permute-start(bf16[1,200,1600]{2,1,0:T(8,128)(2,1)} %bitcast.107), channel_id=1, source_target_pairs={{0,4},{4,0},{1,5},{5,1},{2,6},{6,2},{3,7},{7,3},{8,12},{12,8},{9,1... | collective-permute-start | bytes 1920008 | tf_op jit(solution)/shard_map/ppermute | solution.py:156
  920.3 39.7 %collective-permute-start.163 = (bf16[1,200,1600]{2,1,0:T(8,128)(2,1)}, bf16[1,200,1600]{2,1,0:T(8,128)(2,1)}, u32[]{:S(2)}, u32[]{:S(2)}) collective-permute-start(bf16[1,200,1600]{2,1,0:T(8,128)(2,1)} %bitcast.105), channel_id=1, source_target_pairs={{0,4},{4,0},{1,5},{5,1},{2,6},{6,2},{3,7},{7,3},{8,12},{12,8},{9,1... | collective-permute-start | bytes 1920008 | tf_op jit(solution)/shard_map/ppermute | solution.py:156
  925.8 34.9 %collective-permute-start.95 = (bf16[400,768]{1,0:T(8,128)(2,1)}, bf16[400,768]{1,0:T(8,128)(2,1)}, u32[]{:S(2)}, u32[]{:S(2)}) collective-permute-start(bf16[400,768]{1,0:T(8,128)(2,1)} %collective-permute-done.94), channel_id=1, source_target_pairs={{8,16},{9,17},{10,18},{11,19},{12,20},{13,21},{14,22},{15,23}} | collective-permute-start | bytes 1843208 | tf_op jit(solution)/shard_map/ppermute | solution.py:224
  927.3 34.1 %collective-permute-start.87 = (bf16[400,768]{1,0:T(8,128)(2,1)}, bf16[400,768]{1,0:T(8,128)(2,1)}, u32[]{:S(2)}, u32[]{:S(2)}) collective-permute-start(bf16[400,768]{1,0:T(8,128)(2,1)} %collective-permute-done.86), channel_id=1, source_target_pairs={{16,8},{17,9},{18,10},{19,11},{20,12},{21,13},{22,14},{23,15}} | collective-permute-start | bytes 1843208 | tf_op jit(solution)/shard_map/ppermute | solution.py:224
  931.3 31.4 %collective-permute-start.79 = (bf16[400,768]{1,0:T(8,128)(2,1)}, bf16[400,768]{1,0:T(8,128)(2,1)}, u32[]{:S(2)}, u32[]{:S(2)}) collective-permute-start(bf16[400,768]{1,0:T(8,128)(2,1)} %collective-permute-done.78), channel_id=1, source_target_pairs={{8,16},{9,17},{10,18},{11,19},{12,20},{13,21},{14,22},{15,23}} | collective-permute-start | bytes 1843208 | tf_op jit(solution)/shard_map/ppermute | solution.py:224
  967.0 43.8 %collective-permute-start.104 = (bf16[400,768]{1,0:T(8,128)(2,1)S(1)}, bf16[400,768]{1,0:T(8,128)(2,1)S(1)}, u32[]{:S(2)}, u32[]{:S(2)}) collective-permute-start(bf16[400,768]{1,0:T(8,128)(2,1)S(1)} %collective-permute-done.103), channel_id=1, source_target_pairs={{8,0},{9,1},{10,2},{11,3},{12,4},{13,5},{14,6},{15,7}} | collective-permute-start | bytes 1843208 | tf_op jit(solution)/shard_map/ppermute | solution.py:224
  968.4 35.5 %collective-permute-start.117 = (bf16[200,1600]{1,0:T(8,128)(2,1)S(1)}, bf16[200,1600]{1,0:T(8,128)(2,1)S(1)}, u32[]{:S(2)}, u32[]{:S(2)}) collective-permute-start(bf16[200,1600]{1,0:T(8,128)(2,1)S(1)} %collective-permute-done.116), channel_id=1, source_target_pairs={{8,0},{9,1},{10,2},{11,3},{12,4},{13,5},{14,6},{15,7}} | collective-permute-start | bytes 1920008 | tf_op jit(solution)/shard_map/ppermute | solution.py:224
  970.2 40.9 %collective-permute-start.97 = (bf16[400,768]{1,0:T(8,128)(2,1)S(1)}, bf16[400,768]{1,0:T(8,128)(2,1)S(1)}, u32[]{:S(2)}, u32[]{:S(2)}) collective-permute-start(bf16[400,768]{1,0:T(8,128)(2,1)S(1)} %select_select_fusion.10), channel_id=1, source_target_pairs={{0,1},{1,0},{2,3},{3,2},{4,5},{5,4},{6,7},{7,6},{8,9},{9,8},{10,11... | collective-permute-start | bytes 1843208 | tf_op jit(solution)/shard_map/ppermute | solution.py:156
  976.4 36.1 %collective-permute-start.89 = (bf16[400,768]{1,0:T(8,128)(2,1)S(1)}, bf16[400,768]{1,0:T(8,128)(2,1)S(1)}, u32[]{:S(2)}, u32[]{:S(2)}) collective-permute-start(bf16[400,768]{1,0:T(8,128)(2,1)S(1)} %select_select_fusion.11), channel_id=1, source_target_pairs={{0,2},{1,3},{2,0},{3,1},{4,6},{5,7},{6,4},{7,5},{8,10},{9,11},{10,... | collective-permute-start | bytes 1843208 | tf_op jit(solution)/shard_map/ppermute | solution.py:156
  978.2 34.4 %collective-permute-start.81 = (bf16[400,768]{1,0:T(8,128)(2,1)S(1)}, bf16[400,768]{1,0:T(8,128)(2,1)S(1)}, u32[]{:S(2)}, u32[]{:S(2)}) collective-permute-start(bf16[400,768]{1,0:T(8,128)(2,1)S(1)} %select_select_fusion.12), channel_id=1, source_target_pairs={{0,3},{1,2},{2,1},{3,0},{4,7},{5,6},{6,5},{7,4},{8,11},{9,10},{10,... | collective-permute-start | bytes 1843208 | tf_op jit(solution)/shard_map/ppermute | solution.py:156
  1011.0 33.2 %collective-permute-start.98 = (bf16[1,400,768]{2,1,0:T(8,128)(2,1)S(1)}, bf16[1,400,768]{2,1,0:T(8,128)(2,1)S(1)}, u32[]{:S(2)}, u32[]{:S(2)}) collective-permute-start(bf16[1,400,768]{2,1,0:T(8,128)(2,1)S(1)} %bitcast.292), channel_id=1, source_target_pairs={{0,4},{4,0},{1,5},{5,1},{2,6},{6,2},{3,7},{7,3},{8,12},{12,8},{9,1... | collective-permute-start | bytes 1843208 | tf_op jit(solution)/shard_map/ppermute | solution.py:156
  1012.5 44.9 %collective-permute-start.90 = (bf16[1,400,768]{2,1,0:T(8,128)(2,1)S(1)}, bf16[1,400,768]{2,1,0:T(8,128)(2,1)S(1)}, u32[]{:S(2)}, u32[]{:S(2)}) collective-permute-start(bf16[1,400,768]{2,1,0:T(8,128)(2,1)S(1)} %bitcast.293), channel_id=1, source_target_pairs={{0,4},{4,0},{1,5},{5,1},{2,6},{6,2},{3,7},{7,3},{8,12},{12,8},{9,1... | collective-permute-start | bytes 1843208 | tf_op jit(solution)/shard_map/ppermute | solution.py:156
  1012.6 58.0 %collective-permute-start.82 = (bf16[1,400,768]{2,1,0:T(8,128)(2,1)S(1)}, bf16[1,400,768]{2,1,0:T(8,128)(2,1)S(1)}, u32[]{:S(2)}, u32[]{:S(2)}) collective-permute-start(bf16[1,400,768]{2,1,0:T(8,128)(2,1)S(1)} %bitcast.294), channel_id=1, source_target_pairs={{0,4},{4,0},{1,5},{5,1},{2,6},{6,2},{3,7},{7,3},{8,12},{12,8},{9,1... | collective-permute-start | bytes 1843208 | tf_op jit(solution)/shard_map/ppermute | solution.py:156
  (252 other events, 3690.4 us)

commit v2 on v1

v2 whole, which is shorter than its diff:
```python
import math

import jax
import jax.numpy as jnp
from jax import lax
from jax.experimental import pallas as pl
from jax.experimental.pallas import tpu as pltpu
from jax.sharding import Mesh, PartitionSpec as P

HEAD_DIM = 64
BLOCK = 256
EPSILON = 1e-05
NEGATIVE = -1e30
SEG_STEP = 65536
BF16 = jnp.bfloat16
F32 = jnp.float32


def bits_of(size):
    return [1 << i for i in range(size.bit_length() - 1)]


def norm_parts(values):
    centre = jnp.mean(values, axis=-1, keepdims=True)
    centred = values - centre
    spread = jnp.mean(centred * centred, axis=-1, keepdims=True)
    inverse = lax.rsqrt(spread + EPSILON)
    return centred * inverse, inverse


def gelu_parts(u):
    c = math.sqrt(2.0 / math.pi)
    squared = u * u
    t = jnp.tanh(c * (u + 0.044715 * (u * squared)))
    half = 0.5 * (1.0 + t)
    slope = half + 0.5 * u * (1.0 - t * t) * (c * (1.0 + 3.0 * 0.044715 * squared))
    return u * half, slope


def dot(a, b, contract=((1,), (0,))):
    return lax.dot_general(a, b, (contract, ((), ())), preferred_element_type=F32)


ACROSS_TOKENS = ((0,), (0,))
ON_LAST = ((1,), (1,))


MESH_ID = pl.DeviceIdType.MESH


def remote(src, dst, send_sem, recv_sem, **device):
    return pltpu.make_async_remote_copy(
        src_ref=src,
        dst_ref=dst,
        send_sem=send_sem,
        recv_sem=recv_sem,
        device_id=device,
        device_id_type=MESH_ID,
    )


def partner(axis, bit):
    return {axis: lax.axis_index(axis) ^ bit}


def plane_device(offset, r_size):
    found = {}
    if offset // r_size:
        found["s"] = lax.axis_index("s") ^ (offset // r_size)
    if offset % r_size:
        found["r"] = lax.axis_index("r") ^ (offset % r_size)
    return found


def tree_of(order, r_size):
    levels = []
    known = [(0, 0)]
    for axis, bit in order:
        step = bit * r_size if axis == "s" else bit
        known = known + [(o ^ step, depth + 1) for o, depth in known]
    found = {}
    for o, depth in known:
        if o == 0:
            continue
        for axis, bit in order[::-1]:
            step = bit * r_size if axis == "s" else bit
            if o & step:
                found.setdefault(depth, []).append((o, o ^ step, axis, bit))
                break
    for depth in sorted(found):
        levels.append(found[depth])
    return levels


def chip_orders(r_size):
    chips = [("s", 2)] + [("r", bit) for bit in bits_of(r_size)]
    return [chips + [("s", 1)], chips[::-1] + [("s", 1)]]


class Gather:
    def __init__(self, block, send_sem, recv_sem, r_size, parts=2, own=None):
        self.block = block
        self.own = own or block
        self.send_sem = send_sem
        self.recv_sem = recv_sem
        self.levels = [tree_of(order, r_size) for order in chip_orders(r_size)[:parts]]
        self.parts = parts
        self.arrived = set()

    def copy(self, part, transfer):
        offset, source, axis, bit = transfer
        src = self.own(0, part) if source == 0 else self.block(source, part)
        return remote(
            src,
            self.block(offset, part),
            self.send_sem.at[part, offset],
            self.recv_sem.at[part, offset],
            **partner(axis, bit),
        )

    def transfers(self):
        for level in range(len(self.levels[0])):
            for i in range(len(self.levels[0][level])):
                for part in range(self.parts):
                    yield level, part, self.levels[part][level][i]

    def find(self, part, offset):
        for _, p, t in self.transfers():
            if p == part and t[0] == offset:
                return t

    def need(self, part, offset):
        if offset and (part, offset) not in self.arrived:
            self.arrived.add((part, offset))
            self.copy(part, self.find(part, offset)).wait_recv()

    def start(self, level):
        for lv, part, t in self.transfers():
            if lv == level:
                self.need(part, t[1])
                self.copy(part, t).start()

    def start_rest(self):
        for level in range(1, len(self.levels[0])):
            self.start(level)

    def need_all(self):
        for _, part, t in self.transfers():
            self.need(part, t[0])

    def close(self):
        self.need_all()
        for _, part, t in self.transfers():
            self.copy(part, t).wait_send()


def attention_rows(rows, first, q_ref, k_ref, v_ref, code_q, code_k):
    heads = q_ref.shape[1] // HEAD_DIM
    low_q = (code_q // SEG_STEP) * SEG_STEP
    allowed = jnp.logical_and(code_k >= low_q, code_k <= code_q)
    outs = []
    sums = []
    for h in range(heads):
        cols = slice(h * HEAD_DIM, (h + 1) * HEAD_DIM)
        scores = lax.dot_general(
            q_ref[pl.ds(first, rows), cols],
            k_ref[:, cols],
            (((1,), (1,)), ((), ())),
            preferred_element_type=F32,
        )
        scores = jnp.where(allowed, scores, NEGATIVE)
        top = jnp.max(scores, axis=-1, keepdims=True)
        unnorm = jnp.exp(scores - top)
        total = jnp.sum(unnorm, axis=-1, keepdims=True)
        mixed = jnp.dot(unnorm.astype(BF16), v_ref[:, cols], preferred_element_type=F32)
        outs.append((mixed / total).astype(BF16))
        sums.append(top + jnp.log(total))
    return jnp.concatenate(outs, axis=1), jnp.concatenate(sums, axis=1)


def split_rows(n):
    first = -(-n // 32) * 16
    return ((0, first), (first, n - first))


class WeightPush:
    def __init__(self, source, dest, rows, send_sem, recv_sem, across):
        self.source, self.dest, self.rows = source, dest, rows
        self.send_sem, self.recv_sem = send_sem, recv_sem
        self.across = across

    def core_copy(self):
        s = lax.axis_index("s")
        return remote(
            self.source(s ^ 1),
            self.dest(s, 0, self.rows),
            self.send_sem.at[0],
            self.recv_sem.at[0],
            s=s ^ 1,
        )

    def chip_copy(self, m, part, landed=None):
        s = lax.axis_index("s")
        first, count = split_rows(self.rows)[part]
        return remote(
            self.source(s ^ m).at[pl.ds(first, count)],
            self.dest(s, first, count),
            self.send_sem.at[m],
            self.recv_sem.at[m],
            s=s ^ m,
        )

    def relay_copy(self, m, part):
        s = lax.axis_index("s")
        first, count = split_rows(self.rows)[part]
        ref = self.dest(s ^ m, first, count)
        return remote(
            ref, ref, self.send_sem.at[2 + m], self.recv_sem.at[2 + m], z=lax.axis_index("z") ^ 1
        )

    def per_part(self, act):
        odd = lax.axis_index("z") % 2
        for part in range(2):

            @pl.when(odd == part)
            def _(part=part):
                act(part)

    def start(self):
        if 1 in self.across:
            self.core_copy().start()

        def act(part):
            for m in self.across:
                if m != 1:
                    self.chip_copy(m, part).start()

        self.per_part(act)

    def relay(self):
        def act(part):
            for m in self.across:
                if m != 1:
                    self.chip_copy(m, part).wait_recv()
                    self.relay_copy(m, part).start()

        self.per_part(act)

    def need(self):
        if 1 in self.across:
            self.core_copy().wait_recv()

        def act(part):
            for m in self.across:
                if m != 1:
                    self.relay_copy(m, 1 - part).wait_recv()

        self.per_part(act)

    def close(self):
        if 1 in self.across:
            self.core_copy().wait_send()

        def act(part):
            for m in self.across:
                if m != 1:
                    self.chip_copy(m, part).wait_send()
                    self.relay_copy(m, part).wait_send()

        self.per_part(act)


def forward_kernel(
    x_in, cot_in, code_in, small_in, smallh_in, wq_in, wf_in, wo_in,
    h1_out, h2_out, cot_out, wf_out, wq_out, wo_out, q_ref, k_ref, v_ref, att_ref, lse_ref, code_out,
    middle_out, x_own, small_ref, smallh_ref,
    code_land, small_land, smallh_land, h1, wq_vm, stage_q, wf_vm, stage_f, own_q, full_out, att_land, h2_own,
    x_sem, code_sem, cot_sem, small_sem, load_sem, h1_send, h1_recv, cd_send, cd_recv, ct_send, ct_recv, h2_send,
    h2_recv, wq_send, wq_recv, wf_send, wf_recv, wo_send, wo_recv, at_send, at_recv, out_sem,
):
    s, r, z = (lax.axis_index(a) for a in ("s", "r", "z"))
    s_size, r_size = lax.axis_size("s"), lax.axis_size("r")
    devices = s_size * r_size
    me = s * r_size + r
    rows, width = x_in.shape
    tokens = rows * devices
    own_cols = q_ref.shape[1]
    own_ff = wf_out.shape[1]
    shard_rows = wq_in.shape[0]

    def shard_at(i, first=0, count=shard_rows):
        return pl.ds(pl.multiple_of(i * shard_rows + first, 16), count)

    barrier = pltpu.get_barrier_semaphore()
    for offset in range(1, devices):
        pl.semaphore_signal(barrier, inc=1, device_id=plane_device(offset, r_size), device_id_type=MESH_ID)
    pl.semaphore_signal(barrier, inc=1, device_id={"z": z ^ 1}, device_id_type=MESH_ID)

    @pl.when(s != z)
    def _():
        pl.semaphore_signal(barrier, inc=1, device_id={"z": s, "s": z}, device_id_type=MESH_ID)

    pl.semaphore_wait(barrier, devices + jnp.where(s != z, 1, 0))

    def moved(src, dst, sem):
        far = remote(src, dst, sem.at[0], sem.at[1], z=s, s=z)
        near = pltpu.make_async_copy(src, dst, sem.at[1])

        @pl.when(s != z)
        def _():
            far.start()

        @pl.when(s == z)
        def _():
            near.start()

        def arrived():
            @pl.when(s != z)
            def _():
                far.wait_recv()

            @pl.when(s == z)
            def _():
                near.wait()

        def sent():
            @pl.when(s != z)
            def _():
                far.wait_send()

        return arrived, sent

    x_arrived, x_sent = moved(x_in, x_own, x_sem)
    code_arrived, code_sent = moved(code_in, code_land.at[0], code_sem)
    loads = [
        pltpu.make_async_copy(wq_in, wq_vm, load_sem.at[0]),
        pltpu.make_async_copy(wf_in, wf_vm, load_sem.at[1]),
        pltpu.make_async_copy(wo_in, full_out.at[shard_at(s)], load_sem.at[2]),
    ]
    for load in loads:
        load.start()
    small_copies = []
    for m in range(1, s_size):
        small_copies.append(
            remote(small_in, small_land.at[m], small_sem.at[0, m], small_sem.at[1, m], s=s ^ m)
        )
        small_copies.append(
            remote(smallh_in, smallh_land.at[m], small_sem.at[2, m], small_sem.at[3, m], s=s ^ m)
        )
    for copy in small_copies:
        copy.start()
    if full_out.shape[0] > width:
        full_out[width:, :] = jnp.zeros((full_out.shape[0] - width, width), BF16)

    loads[0].wait()
    for s2 in range(s_size):
        for r2 in range(r_size):

            @pl.when(r == r2)
            def _(s2=s2, r2=r2):
                device = s2 * r_size + r2
                for part in range(3):
                    lo = device * own_cols
                    n = max(0, min(own_cols, width - lo))
                    if n:
                        stage_q[s2, :, part * own_cols : part * own_cols + n] = wq_vm[
                            :, part * width + lo : part * width + lo + n
                        ]
                    if n < own_cols:
                        stage_q[s2, :, part * own_cols + n : (part + 1) * own_cols] = jnp.zeros(
                            (shard_rows, own_cols - n), BF16
                        )

    push_q = WeightPush(
        lambda i: stage_q.at[i],
        lambda i, first, count: own_q.at[shard_at(i, first, count)],
        shard_rows, wq_send, wq_recv, (1, 2, 3),
    )
    push_q.start()
    own_q[shard_at(s), :] = stage_q[s]

    for copy in small_copies:
        copy.wait_recv()
    small = small_in[...]
    smallh = smallh_in[...]
    for m in range(1, s_size):
        small = small + small_land[m]
        smallh = smallh + smallh_land[m]
    small_ref[...] = small
    smallh_ref[...] = smallh
    gain_one, bias_one, out_bias, gain_two, bias_two = (small_ref[i : i + 1, :] for i in range(5))
    x_arrived()
    cot_arrived, cot_sent = moved(cot_in, cot_out.at[pl.ds(0, rows)], cot_sem)
    resid = x_own[...].astype(F32)
    normed, _ = norm_parts(resid)
    h1[0:rows, :] = (normed * gain_one + bias_one).astype(BF16)
    half = rows // 2

    def block_of(ref):
        return lambda offset, part: ref.at[pl.ds(offset * rows + part * half, half)]

    gather_one = Gather(block_of(h1), h1_send, h1_recv, r_size)
    gather_one.start(0)
    code_arrived()
    gather_code = Gather(lambda offset, part: code_land.at[offset], cd_send, cd_recv, r_size, parts=1)
    gather_code.start(0)

    loads[1].wait()
    for s2 in range(s_size):
        for r2 in range(r_size):

            @pl.when(r == r2)
            def _(s2=s2, r2=r2):
                lo = (s2 * r_size + r2) * own_ff
                stage_f[s2] = wf_vm[:, lo : lo + own_ff]

    gather_one.start(1)
    gather_code.start(1)
    push_q.relay()
    for level in range(2, len(gather_one.levels[0])):
        gather_one.start(level)
        gather_code.start(level)

    push_o = WeightPush(
        lambda i: full_out.at[shard_at(s)],
        lambda i, first, count: full_out.at[shard_at(i, first, count)],
        shard_rows, wo_send, wo_recv, (1, 2),
    )
    push_f = WeightPush(
        lambda i: stage_f.at[i],
        lambda i, first, count: wf_out.at[shard_at(i, first, count)],
        shard_rows, wf_send, wf_recv, (1, 2, 3),
    )
    own_f = pltpu.make_async_copy(
        stage_f.at[s], wf_out.at[shard_at(s)], load_sem.at[1]
    )
    own_f.start()
    gather_one.need_all()
    loads[2].wait()
    push_o.start()
    push_f.start()

    push_q.need()
    save_q = pltpu.make_async_copy(own_q, wq_out, out_sem.at[0])
    save_q.start()
    save_h = pltpu.make_async_copy(h1, h1_out, out_sem.at[1])
    save_h.start()
    q_bias = smallh_ref[pl.ds(me, 1), :]
    v_bias = smallh_ref[pl.ds(devices + me, 1), :]
    step = min(512, tokens)
    score_scale = jnp.asarray(1.0 / math.sqrt(HEAD_DIM), BF16)

    def project(i, carry):
        at = pl.ds(pl.multiple_of(i * step, step), step)
        packed = jnp.dot(h1[at, :], own_q[...], preferred_element_type=F32)
        q_ref[at, :] = (packed[:, :own_cols] + q_bias).astype(BF16) * score_scale
        k_ref[at, :] = packed[:, own_cols : 2 * own_cols].astype(BF16)
        v_ref[at, :] = (packed[:, 2 * own_cols :] + v_bias).astype(BF16)
        return carry

    lax.fori_loop(0, tokens // step, project, 0)
    cot_arrived()
    gather_cot = Gather(block_of(cot_out), ct_send, ct_recv, r_size)
    gather_cot.start(0)
    gather_code.need_all()
    code_out[...] = code_land[:, 0, :]
    code_row = jnp.concatenate([code_land[i, 0:1, :] for i in range(devices)], axis=1)

    q_rows = min(rows if tokens > 2048 else 256, tokens)

    def attend(i, carry):
        first = pl.multiple_of(i * q_rows, q_rows)
        per = q_rows // rows
        code_col = jnp.concatenate(
            [jnp.transpose(code_land[i * per + j])[:, 0:1] for j in range(per)], axis=0
        )
        out, sums = attention_rows(q_rows, first, q_ref, k_ref, v_ref, code_col, code_row)
        att_ref[pl.ds(first, q_rows), :] = out
        lse_ref[pl.ds(first, q_rows), :] = sums
        return carry

    lax.fori_loop(0, tokens // q_rows, attend, 0)

    at_copies = []
    for offset in range(1, devices):
        at_copies.append(
            remote(
                att_ref.at[pl.ds(offset * rows, rows)],
                att_land.at[me],
                at_send.at[offset],
                at_recv.at[offset],
                **plane_device(offset, r_size),
            )
        )
    for copy in at_copies:
        copy.start()
    att_land[me] = att_ref[0:rows, :]
    push_o.relay()
    push_o.need()
    far = full_out.at[shard_at(s ^ 2)]
    out_core = remote(far, far, wo_send.at[5], wo_recv.at[5], s=s ^ 1)
    out_core.start()
    gather_cot.start(1)
    for copy in at_copies:
        copy.wait_recv()
    out_core.wait_recv()
    middle = resid + out_bias
    for device in range(devices):
        middle = middle + jnp.dot(
            att_land[device],
            full_out[device * own_cols : (device + 1) * own_cols, :],
            preferred_element_type=F32,
        )
    middle_out[...] = middle
    normed, _ = norm_parts(middle)
    h2_own[...] = (normed * gain_two + bias_two).astype(BF16)
    save_h2 = pltpu.make_async_copy(h2_own, h2_out.at[pl.ds(0, rows)], out_sem.at[2])
    save_h2.start()
    gather_two = Gather(
        block_of(h2_out), h2_send, h2_recv, r_size, own=lambda o, part: h2_own.at[pl.ds(part * half, half)]
    )
    gather_two.start(0)
    save_o = pltpu.make_async_copy(
        full_out.at[pl.ds(pl.multiple_of(me * own_cols, own_cols), own_cols)], wo_out, out_sem.at[3]
    )
    save_o.start()
    for level in range(2, len(gather_cot.levels[0])):
        gather_cot.start(level)
    push_f.relay()
    gather_two.start_rest()
    gather_two.close()
    gather_cot.close()
    gather_one.close()
    gather_code.close()
    push_f.need()
    for push in (push_q, push_o, push_f):
        push.close()
    out_core.wait_send()
    for copy in at_copies + small_copies:
        copy.wait_send()
    x_sent()
    code_sent()
    cot_sent()
    own_f.wait()
    for save in (save_q, save_h, save_h2, save_o):
        save.wait()


def forward_part(x, cot, code, small, smallh, w_qkv, w_fc, w_out):
    s_size, r_size = lax.axis_size("s"), lax.axis_size("r")
    devices = s_size * r_size
    rows, width = x.shape
    tokens = rows * devices
    shard_rows = w_qkv.shape[0]
    heads = width // HEAD_DIM
    own_heads = -(-heads // devices)
    own_cols = own_heads * HEAD_DIM
    own_ff = w_fc.shape[1] // devices
    anywhere = pl.BlockSpec(memory_space=pl.ANY)
    vmem = pl.BlockSpec(memory_space=pltpu.VMEM)
    shape = jax.ShapeDtypeStruct
    dma = pltpu.SemaphoreType.DMA
    flops = 2 * tokens * width * 3 * own_cols + 4 * own_heads * tokens * tokens * HEAD_DIM
    return pl.pallas_call(
        forward_kernel,
        in_specs=[anywhere, anywhere, anywhere, vmem, vmem, anywhere, anywhere, anywhere],
        out_specs=[anywhere] * 6 + [vmem] * 10,
        out_shape=[
            shape((tokens, width), BF16),
            shape((tokens, width), BF16),
            shape((tokens, width), BF16),
            shape((width, own_ff), BF16),
            shape((width, 3 * own_cols), BF16),
            shape((own_cols, width), BF16),
            shape((tokens, own_cols), BF16),
            shape((tokens, own_cols), BF16),
            shape((tokens, own_cols), BF16),
            shape((tokens, own_cols), BF16),
            shape((tokens, own_heads), F32),
            shape((devices, rows), jnp.int32),
            shape((rows, width), F32),
            shape((rows, width), BF16),
            shape(small.shape, F32),
            shape(smallh.shape, F32),
        ],
        scratch_shapes=[
            pltpu.VMEM((devices, 8, rows), jnp.int32),
            pltpu.VMEM((s_size,) + small.shape, F32),
            pltpu.VMEM((s_size,) + smallh.shape, F32),
            pltpu.VMEM((tokens, width), BF16),
            pltpu.VMEM(w_qkv.shape, BF16),
            pltpu.VMEM((s_size, shard_rows, 3 * own_cols), BF16),
            pltpu.VMEM(w_fc.shape, BF16),
            pltpu.VMEM((s_size, shard_rows, own_ff), BF16),
            pltpu.VMEM((width, 3 * own_cols), BF16),
            pltpu.VMEM((devices * own_cols, width), BF16),
            pltpu.VMEM((devices, rows, own_cols), BF16),
            pltpu.VMEM((rows, width), BF16),
            dma((2,)), dma((2,)), dma((2,)), dma((4, s_size)), dma((3,)),
            dma((2, devices)), dma((2, devices)), dma((1, devices)), dma((1, devices)),
            dma((2, devices)), dma((2, devices)), dma((2, devices)), dma((2, devices)),
            dma((6,)), dma((6,)), dma((6,)), dma((6,)), dma((6,)), dma((6,)),
            dma((devices,)), dma((devices,)), dma((4,)),
        ],
        compiler_params=pltpu.CompilerParams(
            collective_id=0, has_side_effects=True, vmem_limit_bytes=60 << 20
        ),
        cost_estimate=pl.CostEstimate(flops=flops, bytes_accessed=40 << 20, transcendentals=0),
        name="forward_part",
    )(x, cot, code, small, smallh, w_qkv, w_fc, w_out)


class Scatter:
    def __init__(self, leaf, acc, land, load, send_sem, recv_sem, r_size):
        self.leaf, self.acc, self.land, self.load = leaf, acc, land, load
        self.send_sem, self.recv_sem = send_sem, recv_sem
        self.levels = [tree_of(order, r_size) for order in chip_orders(r_size)]

    def copy(self, part, transfer):
        offset, _, axis, bit = transfer
        src = self.acc(offset, part) if self.children(part, offset) else self.leaf(offset, part)
        return remote(
            src,
            self.land(offset, part),
            self.send_sem.at[part, offset],
            self.recv_sem.at[part, offset],
            **partner(axis, bit),
        )

    def children(self, part, offset):
        return [t for level in self.levels[part] for t in level if t[1] == offset]

    def start_leaves(self):
        for level in range(len(self.levels[0]) - 1, -1, -1):
            for i in range(len(self.levels[0][level])):
                for part in range(2):
                    t = self.levels[part][level][i]
                    if not self.children(part, t[0]):
                        self.copy(part, t).start()

    def total(self, part, offset):
        value = self.acc(offset, part)[...].astype(F32)
        for t in self.children(part, offset)[::-1]:
            self.copy(part, t).wait_recv()
            value = value + self.load(t[0], part).astype(F32)
        return value

    def start_inner(self):
        for level in range(len(self.levels[0]) - 1, -1, -1):
            for i in range(len(self.levels[0][level])):
                for part in range(2):
                    t = self.levels[part][level][i]
                    if self.children(part, t[0]):
                        self.acc(t[0], part)[...] = self.total(part, t[0]).astype(BF16)
                        self.copy(part, t).start()

    def finish(self):
        return jnp.concatenate([self.total(part, 0) for part in range(2)], axis=0)

    def close(self):
        for part in range(2):
            for level in self.levels[part]:
                for t in level:
                    self.copy(part, t).wait_send()


class LineSum:
    def __init__(self, jobs, land, rs_send, rs_recv, ag_send, ag_recv, home):
        self.jobs, self.land = jobs, land
        self.rs_send, self.rs_recv, self.ag_send, self.ag_recv = rs_send, rs_recv, ag_send, ag_recv
        self.home = home
        self.n = jobs.shape[1]
        self.z = lax.axis_index("z")
        self.last = lax.axis_size("z") - 1
        self.first_dir = jnp.where(self.z * 2 > self.last, 1, 0)
        self.outer = jnp.logical_or(self.z == 0, self.z == self.last)

    def place(self, d):
        return jnp.where(d == 0, self.z, self.last - self.z)

    def up(self, d, j):
        return remote(
            self.jobs.at[d, j], self.land.at[d, j], self.rs_send.at[d, j], self.rs_recv.at[d, j], z=self.z + 1 - 2 * d
        )

    def down(self, d, j):
        return remote(
            self.land.at[d, j], self.land.at[d, j], self.ag_send.at[d, j], self.ag_recv.at[d, j], z=self.z - 1 + 2 * d
        )

    def add(self, d, j):
        place = self.place(d)

        @pl.when(place > 0)
        def _():
            self.up(d, j).wait_recv()
            total = (self.jobs[d, j].astype(F32) + self.land[d, j].astype(F32)).astype(BF16)

            @pl.when(place < self.last)
            def _():
                self.jobs[d, j] = total

            @pl.when(place == self.last)
            def _():
                self.land[d, j] = total

        @pl.when(place < self.last)
        def _():
            self.up(d, j).start()

        @pl.when(place == self.last)
        def _():
            self.down(d, j).start()
            self.home(d, j)

    def back(self, d, j):
        place = self.place(d)

        @pl.when(place < self.last)
        def _():
            self.down(d, j).wait_recv()

            @pl.when(place > 0)
            def _():
                self.down(d, j).start()

            self.home(d, j)

    def add_ticks(self, lo, hi):
        def tick(t, carry):
            @pl.when(t < self.n)
            def _():
                self.add(self.first_dir, t)

            u = t - jnp.where(self.outer, 3, 1)

            @pl.when(jnp.logical_and(u >= 0, u < self.n))
            def _():
                self.add(1 - self.first_dir, u)

            return carry

        lax.fori_loop(lo, hi, tick, 0)

    def back_ticks(self, lo, hi):
        def tick(t, carry):
            @pl.when(t < self.n)
            def _():
                self.back(1 - self.first_dir, t)

            u = t - jnp.where(self.outer, 2, 1)

            @pl.when(jnp.logical_and(u >= 0, u < self.n))
            def _():
                self.back(self.first_dir, u)

            return carry

        lax.fori_loop(lo, hi, tick, 0)

    def close(self):
        def one(i, carry):
            d, j = i // self.n, i % self.n
            place = self.place(d)

            @pl.when(place < self.last)
            def _():
                self.up(d, j).wait_send()

            @pl.when(place > 0)
            def _():
                self.down(d, j).wait_send()

            return carry

        lax.fori_loop(0, 2 * self.n, one, 0)


def job_rows(n, most=80):
    for rows in range(most, 15, -16):
        if n % rows == 0:
            return rows
    return n


def norm_backward_rows(grad, normed, inverse, gain):
    scaled = grad * gain
    mean_scaled = jnp.mean(scaled, axis=-1, keepdims=True)
    mean_product = jnp.mean(scaled * normed, axis=-1, keepdims=True)
    grad_in = inverse * (scaled - mean_scaled - normed * mean_product)
    return (
        grad_in,
        jnp.sum(grad * normed, axis=0, keepdims=True),
        jnp.sum(grad, axis=0, keepdims=True),
    )


def backward_kernel(
    part2, partp, gproj, gfc, h1, wq, wo, q_ref, k_ref, v_ref, att_ref, lse_ref, code_ref, middle_ref, x_ref, cot_in,
    small_ref, fcb_ref,
    out_home, ig_home, home_proj, home_fc, home_qkv, home_out, small_out, landp, gb,
    acc2, accp, land, tmp, jp, jf, jq, jo, lp, lf, lq, lo_, own_q, own_o, cot_v, chunk, gq_acc, do_ref, gp,
    dk_acc, dv_acc, go_acc, vec, vec_land, gb_own, out_v, ig_v,
    load_sem, s2_send, s2_recv, sp_send, sp_recv, s1_send, s1_recv, g_send, g_recv, tmp_sem, home_sem, mv_sem,
    vec_send, vec_recv,
    p_rs, p_rr, p_as, p_ar, f_rs, f_rr, f_as, f_ar, q_rs, q_rr, q_as, q_ar, o_rs, o_rr, o_as, o_ar,
    ph_send, ph_recv, fh_send, fh_recv, qh_send, qh_recv, oh_send, oh_recv,
):
    s, r, z = (lax.axis_index(a) for a in ("s", "r", "z"))
    s_size, r_size, z_size = (lax.axis_size(a) for a in ("s", "r", "z"))
    devices = s_size * r_size
    me = s * r_size + r
    rows, width = x_ref.shape
    tokens = rows * devices
    half = rows // 2
    own_cols = q_ref.shape[1]
    own_ff = gfc.shape[3]
    heads = own_cols // HEAD_DIM
    shard_rows = width // s_size

    barrier = pltpu.get_barrier_semaphore()
    for offset in range(1, devices):
        pl.semaphore_signal(barrier, inc=1, device_id=plane_device(offset, r_size), device_id_type=MESH_ID)
    for bit in bits_of(z_size):
        pl.semaphore_signal(barrier, inc=1, device_id={"z": z ^ bit}, device_id_type=MESH_ID)
    inner = jnp.logical_and(z > 0, z < z_size - 1)

    @pl.when(s != z)
    def _():
        pl.semaphore_signal(barrier, inc=1, device_id={"z": s, "s": z}, device_id_type=MESH_ID)

    @pl.when(inner)
    def _():
        pl.semaphore_signal(
            barrier, inc=1, device_id={"z": jnp.where(z % 2 == 1, z + 1, z - 1)}, device_id_type=MESH_ID
        )

    peers = devices - 1 + len(bits_of(z_size))
    pl.semaphore_wait(barrier, peers + jnp.where(s != z, 1, 0) + jnp.where(inner, 1, 0))

    def core_of(offset):
        return (offset // r_size) % 2

    def slot(offset):
        return (offset // r_size) // 2 * r_size + offset % r_size

    def block(ref):
        return lambda o, part: ref.at[pl.ds(o * rows + part * half, half)]

    def packed_block(ref):
        return lambda o, part: ref.at[pl.ds(slot(o) * rows + part * half, half)]

    loads = []
    plain = [(gproj, jp), (gfc, jf), (wq, own_q), (wo, own_o), (cot_in.at[pl.ds(0, rows)], cot_v)]
    for i, (src, dst) in enumerate(plain):
        loads.append(pltpu.make_async_copy(src, dst, load_sem.at[i]))
    acc_loads = []
    for i, (src, dst) in enumerate(((part2, acc2), (partp, accp))):
        for so in range(0, s_size, 2):
            n = r_size * rows
            acc_loads.append(
                pltpu.make_async_copy(
                    src.at[pl.ds(so * n, n)], dst.at[pl.ds(so // 2 * n, n)], load_sem.at[len(plain) + 2 * i + so // 2]
                )
            )
    scatter_two = Scatter(
        block(part2), packed_block(acc2), block(land), lambda o, part: block(land)(o, part)[...], s2_send, s2_recv, r_size
    )

    def load_from_far(o, part):
        copy = pltpu.make_async_copy(block(landp)(o, part), tmp, tmp_sem.at[0])
        copy.start()
        copy.wait()
        return tmp[...]

    scatter_proj = Scatter(
        block(partp), packed_block(accp), block(landp), load_from_far, sp_send, sp_recv, r_size
    )
    scatter_two.start_leaves()
    for copy in acc_loads[:2] + loads + acc_loads[2:]:
        copy.start()
    scatter_proj.start_leaves()

    def to_home(src, dst, send, recv, s_to, m):
        far = remote(src, dst, send, recv, s=s_to, r=r ^ m)
        if m:
            far.start()
        else:
            near = pltpu.make_async_copy(src, dst, recv)

            @pl.when(s_to == s)
            def _():
                near.start()

            @pl.when(s_to != s)
            def _():
                far.start()

    def home_of_proj(d, j):
        for m in range(r_size):
            src, dst = lp.at[d, j], home_proj.at[r, d, j]
            if m:
                remote(src, dst, ph_send.at[m], ph_recv.at[r], r=r ^ m).start()
            else:
                pltpu.make_async_copy(src, dst, ph_recv.at[r]).start()

    def home_of_columns(landing, home, send, recv):
        per = landing.shape[1] // (s_size // 2)

        def go(d, j):
            s_to = d * (s_size // 2) + j // per
            for m in range(r_size):
                to_home(landing.at[d, j], home.at[me, j % per], send.at[s_to, m], recv.at[me], s_to, m)

        return go

    def out_targets():
        a = (me * own_cols) // shard_rows
        b = (me * own_cols + own_cols - 1) // shard_rows
        return ((a, a < s_size), (b, jnp.logical_and(b != a, b < s_size)))

    def home_of_out(d, j):
        for i, (s_to, valid) in enumerate(out_targets()):

            @pl.when(valid)
            def _(i=i, s_to=s_to):
                for m in range(r_size):
                    to_home(lo_.at[d, j], home_out.at[me, d, j], oh_send.at[i, m], oh_recv.at[me], s_to, m)

    sum_proj = LineSum(jp, lp, p_rs, p_rr, p_as, p_ar, home_of_proj)
    sum_fc = LineSum(jf, lf, f_rs, f_rr, f_as, f_ar, home_of_columns(lf, home_fc, fh_send, fh_recv))
    sum_qkv = LineSum(jq, lq, q_rs, q_rr, q_as, q_ar, home_of_columns(lq, home_qkv, qh_send, qh_recv))
    sum_out = LineSum(jo, lo_, o_rs, o_rr, o_as, o_ar, home_of_out)

    for copy in loads + acc_loads:
        copy.wait()

    scatter_two.start_inner()
    vec[...] = jnp.zeros_like(vec)
    gain_one, gain_two, proj_bias = (small_ref[i : i + 1, :] for i in (0, 3, 5))
    cot = cot_v[...].astype(F32)
    middle = middle_ref[...]
    normed, inverse = norm_parts(middle)
    grad_in, grad_gain, grad_bias = norm_backward_rows(scatter_two.finish(), normed, inverse, gain_two)
    grad_middle = cot + grad_in
    branch = grad_middle.astype(BF16)
    gb_own[...] = branch
    ig_keep = grad_middle
    gather = Gather(block(gb), g_send, g_recv, r_size, own=lambda o, part: gb_own.at[pl.ds(part * half, half)])
    gather.start(0)
    save_gb = pltpu.make_async_copy(gb_own, gb.at[pl.ds(0, rows)], tmp_sem.at[1])
    save_gb.start()
    vec[2:3, :] = jnp.sum(branch.astype(F32), axis=0, keepdims=True)
    vec[3:4, :] = grad_gain
    vec[4:5, :] = grad_bias
    vec[5:6, :] = jnp.sum(cot, axis=0, keepdims=True)
    gather.start_rest()
    scatter_proj.start_inner()
    out_v[...] = (middle + (scatter_proj.finish() + proj_bias)).astype(BF16)

    def moved(src, dst, sem):
        far = remote(src, dst, sem.at[0], sem.at[1], z=s, s=z)
        near = pltpu.make_async_copy(src, dst, sem.at[1])

        @pl.when(s != z)
        def _():
            far.start()

        @pl.when(s == z)
        def _():
            near.start()

        def done():
            @pl.when(s != z)
            def _():
                far.wait()

            @pl.when(s == z)
            def _():
                near.wait()

        return done

    out_done = moved(out_v, out_home, mv_sem.at[0])
    gather.need_all()
    save_gb.wait()

    step = chunk.shape[0]
    go_acc[...] = jnp.zeros_like(go_acc)

    def branch_rows(i, carry):
        at = pl.ds(pl.multiple_of(i * step, step), step)
        copy = pltpu.make_async_copy(gb.at[at], chunk, tmp_sem.at[2])
        copy.start()
        copy.wait()
        do_ref[at, :] = lax.dot_general(
            chunk[...], own_o[...], (((1,), (1,)), ((), ())), preferred_element_type=F32
        ).astype(BF16)
        go_acc[...] += lax.dot_general(
            att_ref[at, :], chunk[...], (((0,), (0,)), ((), ())), preferred_element_type=F32
        )
        return carry

    lax.fori_loop(0, tokens // step, branch_rows, 0)
    out_rows = jo.shape[2]
    for i in range(2 * jo.shape[1]):
        jo[i // jo.shape[1], i % jo.shape[1]] = go_acc[i * out_rows : (i + 1) * out_rows, :].astype(BF16)

    code_row = jnp.concatenate([code_ref[i : i + 1, :] for i in range(devices)], axis=1)
    q_rows = min(rows if tokens > 2048 else 256, tokens)
    dk_acc[...] = jnp.zeros_like(dk_acc)
    dv_acc[...] = jnp.zeros_like(dv_acc)
    contract_last = (((1,), (1,)), ((), ()))
    contract_first = (((0,), (0,)), ((), ()))

    def attend(i, carry):
        at = pl.ds(pl.multiple_of(i * q_rows, q_rows), q_rows)
        per = q_rows // rows
        code_q = jnp.concatenate(
            [
                jnp.transpose(jnp.broadcast_to(code_ref[pl.ds(i * per + j, 1), :], (8, rows)))[:, 0:1]
                for j in range(per)
            ],
            axis=0,
        )
        low_q = (code_q // SEG_STEP) * SEG_STEP
        allowed = jnp.logical_and(code_row >= low_q, code_row <= code_q)
        dqs, dks, dvs = [], [], []
        for h in range(heads):
            cols = slice(h * HEAD_DIM, (h + 1) * HEAD_DIM)
            q, do, k = q_ref[at, cols], do_ref[at, cols], k_ref[:, cols]
            scores = lax.dot_general(q, k, contract_last, preferred_element_type=F32)
            scores = jnp.where(allowed, scores, NEGATIVE)
            probs = jnp.exp(scores - lse_ref[at, h : h + 1])
            dp = lax.dot_general(do, v_ref[:, cols], contract_last, preferred_element_type=F32)
            delta = jnp.sum(probs * dp, axis=-1, keepdims=True)
            ds = (probs * (dp - delta)).astype(BF16)
            dqs.append(jnp.dot(ds, k, preferred_element_type=F32))
            dks.append(lax.dot_general(ds, q, contract_first, preferred_element_type=F32))
            dvs.append(lax.dot_general(probs.astype(BF16), do, contract_first, preferred_element_type=F32))
        gp[at, 0:own_cols] = (jnp.concatenate(dqs, axis=1) * (1.0 / math.sqrt(HEAD_DIM))).astype(BF16)
        dk_acc[...] += jnp.concatenate(dks, axis=1)
        dv_acc[...] += jnp.concatenate(dvs, axis=1)
        return carry

    lax.fori_loop(0, tokens // q_rows, attend, 0)
    gp[:, own_cols : 2 * own_cols] = dk_acc[...].astype(BF16)
    gp[:, 2 * own_cols :] = dv_acc[...].astype(BF16)

    n = r_size * rows
    leaf1 = accp
    scatter_one = Scatter(
        packed_block(leaf1), packed_block(acc2), block(land), lambda o, part: block(land)(o, part)[...],
        s1_send, s1_recv, r_size,
    )
    scatter_two.close()
    scatter_proj.close()
    for dst, odd in ((leaf1, 1), (acc2, 0)):

        def partial(i, carry, dst=dst, odd=odd):
            dst[pl.ds(pl.multiple_of(i * n, n), n), :] = lax.dot_general(
                gp[pl.ds(pl.multiple_of((2 * i + odd) * n, n), n), :], own_q[...], contract_last,
                preferred_element_type=F32,
            ).astype(BF16)
            return carry

        lax.fori_loop(0, s_size // 2, partial, 0)
        if odd:
            scatter_one.start_leaves()
    scatter_one.start_inner()

    gq_acc[...] = jnp.zeros_like(gq_acc)

    def hidden_rows(i, carry):
        at = pl.ds(pl.multiple_of(i * step, step), step)
        copy = pltpu.make_async_copy(h1.at[at], chunk, tmp_sem.at[2])
        copy.start()
        copy.wait()
        gq_acc[...] += lax.dot_general(chunk[...], gp[at, :], contract_first, preferred_element_type=F32)
        return carry

    lax.fori_loop(0, tokens // step, hidden_rows, 0)
    per, q_job = jq.shape[1:3]
    for i in range(2 * per):
        jq[i // per, i % per] = gq_acc[i * q_job : (i + 1) * q_job, :].astype(BF16)

    resid = x_ref[...].astype(F32)
    normed, inverse = norm_parts(resid)
    grad_in, grad_gain, grad_bias = norm_backward_rows(scatter_one.finish(), normed, inverse, gain_one)
    ig_v[...] = (ig_keep + grad_in).astype(BF16)
    ig_done = moved(ig_v, ig_home, mv_sem.at[1])
    vec[0:1, :] = grad_gain
    vec[1:2, :] = grad_bias
    ff_lanes = -(-own_ff // 128) * 128
    q_lanes = -(-own_cols // 128) * 128
    vec[7:8, 0:own_ff] = fcb_ref[...]
    vec[7:8, ff_lanes : ff_lanes + own_cols] = jnp.sum(gp[:, :own_cols].astype(F32), axis=0, keepdims=True)
    vec[7:8, ff_lanes + q_lanes : ff_lanes + q_lanes + own_cols] = jnp.sum(
        gp[:, 2 * own_cols :].astype(F32), axis=0, keepdims=True
    )
    vec[pl.ds(8 + me, 1), :] = vec[7:8, :]

    sum_proj.add_ticks(0, sum_proj.n + 3)
    sum_fc.add_ticks(0, sum_fc.n + 3)
    sum_proj.back_ticks(0, sum_proj.n + 2)
    sum_fc.back_ticks(0, sum_fc.n + 2)
    sum_out.add_ticks(0, sum_out.n + 3)
    sum_qkv.add_ticks(0, sum_qkv.n + 3)

    hops = [("s", 1), ("s", 2)] + [("r", bit) for bit in bits_of(r_size)] + [("z", bit) for bit in bits_of(z_size)]
    for i, (axis, bit) in enumerate(hops):
        copy = remote(vec, vec_land.at[i], vec_send.at[i], vec_recv.at[i], **partner(axis, bit))
        copy.start()
        copy.wait()
        vec[...] = vec[...] + vec_land[i]
    small_out[...] = vec[...]

    sum_out.back_ticks(0, sum_out.n + 2)
    sum_qkv.back_ticks(0, sum_qkv.n + 2)

    scatter_one.close()
    gather.close()
    out_done()
    ig_done()
    for total in (sum_proj, sum_fc, sum_qkv, sum_out):
        total.close()
    for i in range(r_size):
        pltpu.make_async_copy(home_proj.at[i], home_proj.at[i], ph_recv.at[i]).wait()
    for m in range(1, r_size):
        pltpu.make_async_copy(home_proj.at[0], home_proj.at[0], ph_send.at[m]).wait()
    for home, send, recv in ((home_fc, fh_send, fh_recv), (home_qkv, qh_send, qh_recv)):
        for i in range(devices):
            pltpu.make_async_copy(home.at[i], home.at[i], recv.at[i]).wait()
        for s_to in range(s_size):
            for m in range(r_size):
                sent = pltpu.make_async_copy(home.at[0], home.at[0], send.at[s_to, m])
                if m:
                    sent.wait()
                else:

                    @pl.when(s != s_to)
                    def _(sent=sent):
                        sent.wait()

    for i in range(devices):
        a, b = (i * own_cols) // shard_rows, (i * own_cols + own_cols - 1) // shard_rows

        @pl.when(jnp.logical_or(s == a, s == b))
        def _(i=i):
            pltpu.make_async_copy(home_out.at[i], home_out.at[i], oh_recv.at[i]).wait()

    for i, (s_to, valid) in enumerate(out_targets()):
        for m in range(r_size):
            far = valid if m else jnp.logical_and(valid, s_to != s)

            @pl.when(far)
            def _(i=i, m=m):
                pltpu.make_async_copy(home_out.at[0], home_out.at[0], oh_send.at[i, m]).wait()


def backward_part(
    part2, partp, grad_proj, grad_fc, h1, wq, wo, q, k, v, att, lse, code, middle, x_own, cot, small, fcb
):
    s_size, r_size, z_size = (lax.axis_size(a) for a in ("s", "r", "z"))
    devices = s_size * r_size
    rows, width = x_own.shape
    tokens = rows * devices
    own_cols = q.shape[1]
    heads = own_cols // HEAD_DIM
    own_ff = grad_proj.shape[0]
    shard_rows = width // s_size
    p_rows = job_rows(own_ff // 2)
    p_n = own_ff // 2 // p_rows
    c_rows = job_rows(shard_rows)
    c_per = shard_rows // c_rows
    c_n = c_per * s_size // 2
    o_rows = job_rows(own_cols // 2)
    o_n = own_cols // 2 // o_rows
    hops = 2 + len(bits_of(r_size)) + len(bits_of(z_size))
    vec_rows = 8 + devices
    anywhere = pl.BlockSpec(memory_space=pl.ANY)
    vmem = pl.BlockSpec(memory_space=pltpu.VMEM)
    shape = jax.ShapeDtypeStruct
    dma = pltpu.SemaphoreType.DMA
    tree = [dma((2, devices))] * 2
    jobs = [(2, p_n, p_rows, width), (2, c_n, c_rows, own_ff), (2, c_n, c_rows, 3 * own_cols), (2, o_n, o_rows, width)]
    line = [dma(j[:2]) for j in jobs for _ in range(4)]
    return pl.pallas_call(
        backward_kernel,
        in_specs=[anywhere] * 7 + [vmem] * 8 + [anywhere, vmem, vmem],
        out_specs=[anywhere] * 6 + [vmem] + [anywhere] * 2,
        out_shape=[
            shape((rows, width), BF16),
            shape((rows, width), BF16),
            shape((r_size,) + jobs[0], BF16),
            shape((devices, c_per, c_rows, own_ff), BF16),
            shape((devices, c_per, c_rows, 3 * own_cols), BF16),
            shape((devices,) + jobs[3], BF16),
            shape((vec_rows, width), F32),
            shape((tokens, width), BF16),
            shape((tokens, width), BF16),
        ],
        scratch_shapes=[
            pltpu.VMEM((tokens // 2, width), BF16),
            pltpu.VMEM((tokens // 2, width), BF16),
            pltpu.VMEM((tokens, width), BF16),
            pltpu.VMEM((rows // 2, width), BF16),
        ]
        + [pltpu.VMEM(j, BF16) for j in jobs]
        + [pltpu.VMEM(j, BF16) for j in jobs]
        + [
            pltpu.VMEM((width, 3 * own_cols), BF16),
            pltpu.VMEM((own_cols, width), BF16),
            pltpu.VMEM((rows, width), BF16),
            pltpu.VMEM((256 if tokens > 2048 else min(512, tokens), width), BF16),
            pltpu.VMEM((width, 3 * own_cols), F32),
            pltpu.VMEM((tokens, own_cols), BF16),
            pltpu.VMEM((tokens, 3 * own_cols), BF16),
            pltpu.VMEM((tokens, own_cols), F32),
            pltpu.VMEM((tokens, own_cols), F32),
            pltpu.VMEM((own_cols, width), F32),
            pltpu.VMEM((vec_rows, width), F32),
            pltpu.VMEM((hops, vec_rows, width), F32),
            pltpu.VMEM((rows, width), BF16),
            pltpu.VMEM((rows, width), BF16),
            pltpu.VMEM((rows, width), BF16),
            dma((10,)),
        ]
        + tree * 4
        + [dma((3,)), dma((1,)), dma((2, 2)), dma((hops,)), dma((hops,))]
        + line
        + [
            dma((r_size,)), dma((r_size,)),
            dma((s_size, r_size)), dma((devices,)),
            dma((s_size, r_size)), dma((devices,)),
            dma((2, r_size)), dma((devices,)),
        ],
        compiler_params=pltpu.CompilerParams(
            collective_id=1, has_side_effects=True, vmem_limit_bytes=62 << 20
        ),
        cost_estimate=pl.CostEstimate(
            flops=10 * heads * tokens * tokens * HEAD_DIM, bytes_accessed=40 << 20, transcendentals=0
        ),
        name="backward_part",
    )(
        part2, partp, grad_proj.reshape(jobs[0]), grad_fc.reshape(jobs[1]), h1, wq, wo, q, k, v, att, lse, code, middle,
        x_own, cot, small, fcb,
    )


def columns_out_kernel(parts, blocks_ref, out_ref):
    devices = blocks_ref.shape[0]
    each = blocks_ref.shape[3] // len(parts)
    for i, (first, width) in enumerate(parts):
        for device in range(devices):
            n = max(0, min(each, width - device * each))
            if n:
                lo = first + device * each
                out_ref[:, lo : lo + n] = blocks_ref[device, 0, :, i * each : i * each + n].astype(F32)


def columns_out(blocks, parts):
    devices, chunks, rows, columns = blocks.shape
    total = parts[-1][0] + parts[-1][1]
    step = 16 if rows % 16 == 0 else rows
    per = rows // step
    return pl.pallas_call(
        lambda *refs: columns_out_kernel(parts, *refs),
        grid=(chunks, per),
        in_specs=[pl.BlockSpec((devices, 1, step, columns), lambda i, j: (0, i, j, 0))],
        out_specs=pl.BlockSpec((step, total), lambda i, j: (i * per + j, 0)),
        out_shape=jax.ShapeDtypeStruct((chunks * rows, total), F32),
        compiler_params=pltpu.CompilerParams(vmem_limit_bytes=32 << 20),
        name="columns_out",
    )(blocks)


def rows_out_kernel(rows_ref, out_ref):
    out_ref[...] = rows_ref[...].astype(F32)


def rows_out(x):
    rows, width = x.shape
    step = job_rows(rows, 160)
    return pl.pallas_call(
        rows_out_kernel,
        grid=(rows // step,),
        in_specs=[pl.BlockSpec((step, width), lambda i: (i, 0))],
        out_specs=pl.BlockSpec((step, width), lambda i: (i, 0)),
        out_shape=jax.ShapeDtypeStruct((rows, width), F32),
        compiler_params=pltpu.CompilerParams(vmem_limit_bytes=32 << 20),
        name="rows_out",
    )(x)


def place(values_in, total, offset):
    return lax.dynamic_update_slice_in_dim(jnp.zeros((total,), F32), values_in.astype(F32), offset, axis=0)


def local(
    inputs,
    positions,
    segments,
    cotangent,
    ln1_gain,
    ln1_bias,
    w_qkv,
    qv_bias,
    w_out,
    out_bias,
    ln2_gain,
    ln2_bias,
    w_fc,
    fc_bias,
    w_proj,
    proj_bias,
):
    s = lax.axis_index("s")
    r = lax.axis_index("r")
    s_size = lax.axis_size("s")
    r_size = lax.axis_size("r")
    devices = s_size * r_size
    me = s * r_size + r
    rows, width = inputs.shape
    heads = width // HEAD_DIM
    own_heads = -(-heads // devices)
    own_cols = own_heads * HEAD_DIM
    head_total = own_cols * devices
    ff = w_fc.shape[1]
    own_ff = ff // devices
    shard_rows = width // s_size

    def head_pad(a):
        return jnp.pad(a, (0, head_total - width)).reshape(devices, own_cols)

    code = jnp.broadcast_to(segments * SEG_STEP + positions // BLOCK, (8, rows))
    small = jnp.stack(
        [place(a, width, s * shard_rows) for a in (ln1_gain, ln1_bias, out_bias, ln2_gain, ln2_bias, proj_bias)]
        + [jnp.zeros((width,), F32)] * 2
    )
    qv = place(qv_bias, 2 * width, s * 2 * shard_rows)
    smallh = jnp.concatenate([head_pad(qv[:width]), head_pad(qv[width:])])

    (
        hidden_one, hidden_two, cot, own_fc, own_qkv, own_out, queries, keys, values, attended, lse, code_all,
        middle, x_own, small, smallh,
    ) = forward_part(inputs, cotangent, code, small, smallh, w_qkv, w_fc, w_out)
    own_fcb = lax.dynamic_slice_in_dim(fc_bias, r * own_ff, own_ff).astype(F32)
    own_proj = lax.dynamic_slice_in_dim(w_proj, r * own_ff, own_ff, axis=0)
    pre_act = dot(hidden_two, own_fc) + own_fcb
    activated, slope = gelu_parts(pre_act)
    activated = activated.astype(BF16)
    grad_act = dot(cot, own_proj, ON_LAST)
    grad_pre = (grad_act * slope).astype(BF16)
    grad_w_proj = dot(activated, cot, ACROSS_TOKENS).astype(BF16)
    partial_two = dot(grad_pre, own_fc, ON_LAST).astype(BF16)
    grad_w_fc = dot(hidden_two, grad_pre, ACROSS_TOKENS).astype(BF16)
    partial_proj = dot(activated, own_proj).astype(BF16)
    grad_fcb = jnp.sum(grad_pre.astype(F32), axis=0)
    out_home, ig_home, home_proj, home_fc, home_qkv, home_out, sums, _, _ = backward_part(
        partial_two, partial_proj, grad_w_proj, grad_w_fc, hidden_one, own_qkv, own_out, queries, keys, values,
        attended, lse, code_all, middle, x_own, cot, small, grad_fcb.reshape(1, own_ff),
    )

    def own_slice(vector):
        size = vector.shape[0] // s_size
        return lax.dynamic_slice_in_dim(vector, s * size, size)

    ff_lanes = -(-own_ff // 128) * 128
    q_lanes = -(-own_cols // 128) * 128
    by_device = sums[8:]
    g_fcb = by_device[:, :own_ff].reshape(ff)
    g_qb = by_device[:, ff_lanes : ff_lanes + own_cols].reshape(-1)[:width]
    g_vb = by_device[:, ff_lanes + q_lanes : ff_lanes + q_lanes + own_cols].reshape(-1)[:width]
    g_fc = columns_out(home_fc, [(0, ff)])
    g_qkv = columns_out(home_qkv, [(i * width, width) for i in range(3)])
    g_out = lax.dynamic_slice_in_dim(home_out.reshape(head_total, width), s * shard_rows, shard_rows)
    g_proj = rows_out(home_proj.reshape(ff // s_size, width))
    return (
        out_home,
        ig_home.astype(F32),
        own_slice(sums[0]),
        own_slice(sums[1]),
        g_qkv,
        own_slice(jnp.concatenate([g_qb, g_vb])),
        g_out.astype(F32),
        own_slice(sums[2]),
        own_slice(sums[3]),
        own_slice(sums[4]),
        g_fc,
        own_slice(g_fcb),
        g_proj,
        own_slice(sums[5]),
    )


def solution(mesh):
    ctx, shard = mesh.devices.shape
    fine = Mesh(mesh.devices.reshape(shard, ctx // shard, shard), ("z", "r", "s"))
    tokens = ("s", "z", "r")
    arg_specs = (
        P(tokens, None),
        P(tokens),
        P(tokens),
        P(tokens, None),
        P("s"),
        P("s"),
        P("s", None),
        P("s"),
        P("s", None),
        P("s"),
        P("s"),
        P("s"),
        P("s", None),
        P("s"),
        P("s", None),
        P("s"),
    )
    out_specs = (P(tokens, None), P(tokens, None)) + arg_specs[4:]
    return jax.shard_map(local, mesh=fine, in_specs=arg_specs, out_specs=out_specs, check_vma=False)
```

time: 1100 us -> 719 us (0.65)
  Pallas kernels: 27.8 us -> 626 us
  waiting for transfers between devices: 411 us -> 0 us
  starting transfers between devices: 329 us -> 0 us
  other arithmetic: 149 us -> 11.4 us
  local copies, waits for them, and re-layouts: 117 us -> 33.7 us
    pallas_call x2 -> x5, Pallas kernels: 27.8 us -> 626 us  [the longest x1 470 us: backward_part(): pl.pallas_call(backward_kernel, in_specs=[anywhere] * 7 + [vmem] * 8 + [a...]
    ppermute x178 -> x0, waiting for transfers between devices: 411 us -> none  [the longest x92 265 us: swap(): return lax.ppermute(x, axis, [(i, i ^ bit) for i in range(size)])]
    ppermute x178 -> x0, starting transfers between devices: 329 us -> none  [the longest x92 129 us: swap(): return lax.ppermute(x, axis, [(i, i ^ bit) for i in range(size)])]
    convert_element_type x42 -> x1, other arithmetic: 65 us -> 3.15 us  [local(): g_out.astype(F32)]
    select_n x25 -> x0, other arithmetic: 31.6 us -> none  [the longest x12 22.1 us: unxor(): jnp.where(on, blocks[m ^ bit], blocks[m])]
    concatenate x14 -> x0, local copies, waits for them, and re-layouts: 21.8 us -> none  [the longest x1 9.67 us: local(): g_fc = jnp.concatenate(columns_home(grad_w_fc), axis=1).astype(F32)]
    unnamed x298 -> x27, local copies, waits for them, and re-layouts: 28.2 us -> 11.1 us
    split x19 -> x0, local copies, waits for them, and re-layouts: 15.1 us -> none  [the longest x18 12.8 us: plane_scatter(): keep, send = jnp.split(state, 2, axis=0)]
  transfers between devices with their start and end apart: 178 -> 0, of which waited for: 62 -> 0; matrix products, arithmetic and copies ran while one was open for 23% -> 0% of each run, Pallas kernels for 3% -> 0%
where the time goes in v2:
time: 719 us; the launch traced here: 712 us
  Pallas kernels  626 us (87%)
  matrix products  39.5 us (5%)
  local copies, waits for them, and re-layouts  33.7 us (5%)
  other arithmetic  11.4 us (2%)
    pallas_call x1, Pallas kernels, backward_part(): pl.pallas_call(backward_kernel, in_specs=[anywhere] * 7 + [vmem] * 8 + [a...  470 us
    pallas_call x1, Pallas kernels, forward_part(): pl.pallas_call(forward_kernel, in_specs=[anywhere, anywhere, anywhere, vm...  128 us
    dot_general x6, matrix products, dot(): lax.dot_general(a, b, (contract, ((), ())), preferred_element_type=F32)  39.5 us
    pallas_call x2, Pallas kernels, columns_out(): pl.pallas_call(lambda *refs: columns_out_kernel(parts, *refs), grid=(chun...  22.2 us

profile of v2, /device:TPU:1, one launch (start us, length us, event | category | flops | bytes accessed | tf_op | source)
XLA Modules:
  0.0 711.6 jit_solution(9620835386340142312)
XLA Ops:
  0.7 0.7 fusion.18
  1.3 0.7 stack.53
  2.0 0.7 stack.54
  2.7 0.7 stack.55
  3.4 0.7 stack.56
  4.1 0.7 stack.57
  4.7 0.7 stack.58
  5.4 0.6 broadcast_in_dim.7.code_in
  6.0 0.8 dynamic-slice_convert_fusion.1
  6.8 0.3 dynamic_update_slice.31
  7.1 0.3 dynamic_update_slice.30
  7.4 0.3 dynamic_update_slice.29
  7.7 0.3 dynamic_update_slice.28
  8.1 0.3 dynamic_update_slice.27
  8.4 0.3 dynamic_update_slice.32
  8.7 0.7 stack.52.small_in
  9.4 0.8 convert_dynamic-update-slice_fusion
  10.2 0.1 slice.58
  10.3 0.7 slice_select_fusion
  11.0 0.6 pad_maximum_fusion.smallh_in
  11.6 2.0 copy.37.x_in
  13.6 2.0 copy.38.cot_in
  15.5 128.4 %forward_part.1 = (bf16[1024,1600]{1,0:T(8,128)(2,1)}, bf16[1024,1600]{1,0:T(8,128)(2,1)}, bf16[1024,1600]{1,0:T(8,128)(2,1)}, bf16[1600,800]{1,0:T(8,128)(2,1)}...) custom-call(bf16[128,1600]{1,0:T(8,128)(2,1)} %copy.37.x_in, ...), custom_call_target="tpu_custom_call" | custom-call | flops 3590324224 | bytes 41943040 | tf_op jit(solution)/shard_map/forward_part/pallas_call | solution.py:564
  143.9 0.0 copy-start.1
  143.9 6.2 fusion.20
  150.1 0.0 copy-done.1
  150.1 0.0 copy-start.3
  150.1 0.0 copy-start.2
  150.1 7.2 %convert_reduce_fusion = (f32[800]{0:T(1024)S(1)}, bf16[1024,800]{0,1:T(8,128)(2,1)S(1)}) fusion(f32[1024,800]{0,1:T(8,128)S(1)} %fusion.20, f32[800]{0:T(1024)S(1)} %dynamic-slice_convert_fusion.1, bf16[1024,1600]{1,0:T(8,128)(2,1)S(1)} %copy-done.1, bf16[1600,1600]{1,0:T(8,128)(2,1)} %param.30, s32[]{:T(128)S(6)} %select_n.18), kind=kOutput, calls=%fused_computation.16 | convolution fusion | flops 2638642432 | bytes 10860804 | tf_op jit(solution)/shard_map/dot_general | solution.py:41
  157.3 0.0 copy-done.3
  157.3 0.0 copy-start.5
  157.4 0.0 copy-done.2
  157.4 4.8 convolution_convert_fusion.2
  162.1 0.0 copy-done.5
  162.2 0.6 reshape.89.fcb_ref
  162.7 5.2 copy.39
  168.0 7.6 %convolution_convert_fusion = bf16[1024,1600]{0,1:T(8,128)(2,1)} fusion(bf16[1600,800]{1,0:T(8,128)(2,1)} %get-tuple-element.38, bf16[1024,800]{0,1:T(8,128)(2,1)} %copy-done.5), kind=kOutput, calls=%fused_computation.2 | convolution fusion | flops 2623078400 | bytes 7475200 | tf_op jit(solution)/shard_map/dot_general | solution.py:41
  175.5 5.4 copy.40.part2
  180.9 0.0 copy-start.4
  180.9 7.5 %convolution_convert_fusion.3 = bf16[800,1600]{1,0:T(8,128)(2,1)} fusion(bf16[1024,1600]{1,0:T(8,128)(2,1)S(1)} %copy-done.1, f32[1024,800]{0,1:T(8,128)} %copy-done.3, f32[800]{0:T(1024)S(1)} %dynamic-slice_convert_fusion.1), kind=kOutput, calls=%fused_computation.5 | convolution fusion | flops 2630912000 | bytes 9116800 | tf_op jit(solution)/shard_map/dot_general | solution.py:41
  188.5 0.0 copy-done.4
  188.5 6.2 convolution_convert_fusion.1
  194.7 3.5 copy.41.partp
  198.2 469.8 %backward_part.1 = (bf16[128,1600]{1,0:T(8,128)(2,1)}, bf16[128,1600]{1,0:T(8,128)(2,1)}, bf16[2,2,5,80,1600]{4,3,2,1,0:T(8,128)(2,1)}, bf16[8,5,80,800]{3,2,1,0...) custom-call(bf16[1024,1600]{1,0:T(8,128)(2,1)} %copy.40.part2, ...), custom_call_target="tpu_custom_call" | custom-call | flops 2684354560 | bytes 41943040 | tf_op jit(solution)/shard_map/backward_part/pallas_call | solution.py:1188
  668.0 1.9 copy.42
  669.9 0.7 slice_bitcast_fusion
  670.7 0.7 fusion.15
  671.3 0.8 slice.55
  672.1 1.1 fusion.19
  673.2 0.7 constant_dynamic-slice_fusion
  673.9 0.1 reshape.93
  674.0 0.7 dynamic_slice.59
  674.6 0.7 constant_dynamic-slice_fusion.2
  675.3 0.7 constant_dynamic-slice_fusion.4
  676.0 2.1 copy.43
  678.0 3.1 dynamic-slice_convert_fusion
  681.2 2.4 copy-done
  683.6 10.6 %columns_out.2 = f32[400,4800]{1,0:T(8,128)} custom-call(bf16[8,5,80,768]{3,2,1,0:T(8,128)(2,1)S(1)} %copy-done), custom_call_target="tpu_custom_call" | custom-call | tf_op jit(solution)/shard_map/columns_out/pallas_call | solution.py:1267
  694.2 0.0 slice-done
  694.2 0.0 slice-done.1
  694.2 11.5 %columns_out.3 = f32[400,6400]{1,0:T(8,128)} custom-call(bf16[8,5,80,800]{3,2,1,0:T(8,128)(2,1)S(1)} %bitcast.33), custom_call_target="tpu_custom_call" | custom-call | tf_op jit(solution)/shard_map/columns_out/pallas_call | solution.py:1267
  705.8 0.0 slice-done.2
  705.8 0.0 slice-done.3
  705.8 5.6 rows_out.1
  (20 shorter events, 0.1 us)
Async XLA Ops:
  143.9 6.2 copy-start.1
  150.1 7.2 %copy-start.3 = (f32[1024,800]{0,1:T(8,128)}, f32[1024,800]{0,1:T(8,128)S(1)}, u32[]{:S(2)}) copy-start(f32[1024,800]{0,1:T(8,128)S(1)} %fusion.20) | copy-start | bytes 9830404
  150.1 7.2 %copy-start.2 = (bf16[1024,1600]{1,0:T(8,128)(2,1)S(1)}, bf16[1024,1600]{1,0:T(8,128)(2,1)}, u32[]{:S(2)}) copy-start(bf16[1024,1600]{1,0:T(8,128)(2,1)} %get-tuple-element.37) | copy-start | bytes 9830404
  157.3 4.8 copy-start.5
  180.9 7.5 %copy-start.4 = (f32[1024,800]{0,1:T(8,128)S(1)}, f32[1024,800]{0,1:T(8,128)}, u32[]{:S(2)}) copy-start(f32[1024,800]{0,1:T(8,128)} %copy-done.3) | copy-start | bytes 9830404
  678.0 16.2 %slice-start = ((s8[5734400]{0:T(1024)(128)(4,1)}), s8[4194304]{0:T(1024)(128)(4,1)S(1)}, s32[]{:S(2)}) async-start(s8[5734400]{0:T(1024)(128)(4,1)} %bitcast.32), calls=%async_computation | async-start | bytes 8388608
  681.2 2.4 copy-start
  683.6 10.6 %slice-start.1 = ((s8[5734400]{0:T(1024)(128)(4,1)}), s8[1540096]{0:T(1024)(128)(4,1)S(1)}, s32[]{:S(2)}) async-start(s8[5734400]{0:T(1024)(128)(4,1)} %bitcast.32), calls=%async_computation.1 | async-start | bytes 3080192
  683.6 22.2 %slice-start.2 = ((s8[5324800]{0:T(1024)(128)(4,1)}), s8[4194304]{0:T(1024)(128)(4,1)S(1)}, s32[]{:S(2)}) async-start(s8[5324800]{0:T(1024)(128)(4,1)} %bitcast.34), calls=%async_computation.2 | async-start | bytes 8388608
  694.2 11.6 %slice-start.3 = ((s8[5324800]{0:T(1024)(128)(4,1)}), s8[1130496]{0:T(1024)(128)(4,1)S(1)}, s32[]{:S(2)}) async-start(s8[5324800]{0:T(1024)(128)(4,1)} %bitcast.34), calls=%async_computation.3 | async-start | bytes 2260992

commit v3 on v2

--- a/solution.py
+++ b/solution.py
@@ -665,18 +665,18 @@
 
 
 class LineSum:
-    def __init__(self, jobs, land, rs_send, rs_recv, ag_send, ag_recv, home):
+    def __init__(self, jobs, land, rs_send, rs_recv, ag_send, ag_recv, home, start):
         self.jobs, self.land = jobs, land
         self.rs_send, self.rs_recv, self.ag_send, self.ag_recv = rs_send, rs_recv, ag_send, ag_recv
         self.home = home
         self.n = jobs.shape[1]
         self.z = lax.axis_index("z")
         self.last = lax.axis_size("z") - 1
-        self.first_dir = jnp.where(self.z * 2 > self.last, 1, 0)
-        self.outer = jnp.logical_or(self.z == 0, self.z == self.last)
+        self.start = start
+        self.end = start + self.n + 2 * self.last
 
     def place(self, d):
-        return jnp.where(d == 0, self.z, self.last - self.z)
+        return self.z if d == 0 else self.last - self.z
 
     def up(self, d, j):
         return remote(
@@ -715,65 +715,110 @@
 
     def back(self, d, j):
         place = self.place(d)
-
-        @pl.when(place < self.last)
+        self.down(d, j).wait_recv()
+
+        @pl.when(place > 0)
         def _():
-            self.down(d, j).wait_recv()
-
-            @pl.when(place > 0)
-            def _():
-                self.down(d, j).start()
-
-            self.home(d, j)
-
-    def add_ticks(self, lo, hi):
-        def tick(t, carry):
-            @pl.when(t < self.n)
-            def _():
-                self.add(self.first_dir, t)
-
-            u = t - jnp.where(self.outer, 3, 1)
-
-            @pl.when(jnp.logical_and(u >= 0, u < self.n))
-            def _():
-                self.add(1 - self.first_dir, u)
+            self.down(d, j).start()
+
+        self.home(d, j)
+
+    def tick(self, k):
+        for d in range(2):
+            j = k - self.start - self.place(d)
+
+            @pl.when(jnp.logical_and(j >= 0, j < self.n))
+            def _(d=d, j=j):
+                self.add(d, j)
+
+        for d in range(2):
+            place = self.place(d)
+            j = k - self.start - 2 * self.last + place
+
+            @pl.when(jnp.logical_and(place < self.last, jnp.logical_and(j >= 0, j < self.n)))
+            def _(d=d, j=j):
+                self.back(d, j)
+
+    def close(self):
+        def one(j, carry):
+            for d in range(2):
+                place = self.place(d)
+
+                @pl.when(place < self.last)
+                def _(d=d):
+                    self.up(d, j).wait_send()
+
+                @pl.when(place > 0)
+                def _(d=d):
+                    self.down(d, j).wait_send()
 
             return carry
 
-        lax.fori_loop(lo, hi, tick, 0)
-
-    def back_ticks(self, lo, hi):
-        def tick(t, carry):
-            @pl.when(t < self.n)
-            def _():
-                self.back(1 - self.first_dir, t)
-
-            u = t - jnp.where(self.outer, 2, 1)
-
-            @pl.when(jnp.logical_and(u >= 0, u < self.n))
-            def _():
-                self.back(self.first_dir, u)
-
+        lax.fori_loop(0, self.n, one, 0)
+
+
+class Clock:
+    def __init__(self, sums):
+        self.sums = sums
+        self.now = 0
+        self.end = max(one.end for one in sums)
+
+    def ticks(self, first, lo, hi):
+        for one in self.sums:
+            if one.start < hi and one.end > lo:
+                one.tick(first)
+
+    def run(self, count):
+        lo, hi = self.now, min(self.now + count, self.end)
+        self.now = hi
+        if hi - lo == 1:
+            self.ticks(lo, lo, hi)
+        elif hi > lo:
+
+            def step(k, carry):
+                self.ticks(k, lo, hi)
+                return carry
+
+            lax.fori_loop(lo, hi, step, 0)
+
+    def loop(self, count, body):
+        lo, hi = self.now, min(self.now + count, self.end)
+        self.now = hi
+
+        def step(i, carry):
+            body(i)
+            self.ticks(lo + i, lo, lo + count)
             return carry
 
-        lax.fori_loop(lo, hi, tick, 0)
-
-    def close(self):
-        def one(i, carry):
-            d, j = i // self.n, i % self.n
-            place = self.place(d)
-
-            @pl.when(place < self.last)
-            def _():
-                self.up(d, j).wait_send()
-
-            @pl.when(place > 0)
-            def _():
-                self.down(d, j).wait_send()
-
-            return carry
-
-        lax.fori_loop(0, 2 * self.n, one, 0)
+        lax.fori_loop(0, count, step, 0)
+
+
+def product_rows(lhs, rhs, write):
+    for lo in range(0, lhs.shape[1], 256):
+        hi = min(lhs.shape[1], lo + 256)
+        value = lax.dot_general(
+            lhs[:, lo:hi], rhs[...], (((0,), (0,)), ((), ())), preferred_element_type=F32
+        )
+        write(lo, hi, value)
+
+
+def into_jobs(jobs):
+    n, size = jobs.shape[1:3]
+
+    def write(lo, hi, value):
+        value = value.astype(BF16)
+        for job in range(lo // size, -(-hi // size)):
+            a, b = max(lo, job * size), min(hi, (job + 1) * size)
+            jobs[job // n, job % n, a - job * size : b - job * size, :] = value[a - lo : b - lo, :]
+
+    return write
+
+
+def into_sum(acc):
+    def write(lo, hi, value):
+        acc[lo:hi, :] += value
+
+    return write
 
 
 def job_rows(n, most=80):
@@ -796,12 +841,12 @@
 
 
 def backward_kernel(
-    part2, partp, gproj, gfc, h1, wq, wo, q_ref, k_ref, v_ref, att_ref, lse_ref, code_ref, middle_ref, x_ref, cot_in,
+    h2, cot_in, wf, wp, h1, wq, wo, q_ref, k_ref, v_ref, att_ref, lse_ref, code_ref, middle_ref, x_ref,
     small_ref, fcb_ref,
-    out_home, ig_home, home_proj, home_fc, home_qkv, home_out, small_out, landp, gb,
-    acc2, accp, land, tmp, jp, jf, jq, jo, lp, lf, lq, lo_, own_q, own_o, cot_v, chunk, gq_acc, do_ref, gp,
-    dk_acc, dv_acc, go_acc, vec, vec_land, gb_own, out_v, ig_v,
-    load_sem, s2_send, s2_recv, sp_send, sp_recv, s1_send, s1_recv, g_send, g_recv, tmp_sem, home_sem, mv_sem,
+    out_home, ig_home, home_proj, home_fc, home_qkv, home_out, small_out, landp, land_far, gb,
+    acc, leaf, land_near, tmp, jp, jf, jq, jo, lp, lf, lq, lo_, own_f, own_p, own_q, own_o, cot_v, chunk, chunk2,
+    gp_acc, gf_acc, gq_acc, act, gpre, do_ref, gp, dk_acc, dv_acc, go_acc, vec, vec_land, gb_own, out_v, ig_v,
+    load_sem, s2_send, s2_recv, sp_send, sp_recv, s1_send, s1_recv, g_send, g_recv, tmp_sem, mv_sem,
     vec_send, vec_recv,
     p_rs, p_rr, p_as, p_ar, f_rs, f_rr, f_as, f_ar, q_rs, q_rr, q_as, q_ar, o_rs, o_rr, o_as, o_ar,
     ph_send, ph_recv, fh_send, fh_recv, qh_send, qh_recv, oh_send, oh_recv,
@@ -814,9 +859,12 @@
     tokens = rows * devices
     half = rows // 2
     own_cols = q_ref.shape[1]
-    own_ff = gfc.shape[3]
+    own_ff = wf.shape[1]
     heads = own_cols // HEAD_DIM
     shard_rows = width // s_size
+    step = chunk.shape[0]
+    contract_last = (((1,), (1,)), ((), ()))
+    contract_first = (((0,), (0,)), ((), ()))
 
     barrier = pltpu.get_barrier_semaphore()
     for offset in range(1, devices):
@@ -835,51 +883,70 @@
             barrier, inc=1, device_id={"z": jnp.where(z % 2 == 1, z + 1, z - 1)}, device_id_type=MESH_ID
         )
 
+    loads = [
+        pltpu.make_async_copy(src, dst, load_sem.at[i])
+        for i, (src, dst) in enumerate(
+            (
+                (wf, own_f),
+                (wp.at[pl.ds(pl.multiple_of(r * own_ff, 8), own_ff)], own_p),
+                (wo, own_o),
+                (cot_in.at[pl.ds(0, rows)], cot_v),
+            )
+        )
+    ]
+    for load in loads:
+        load.start()
+    if own_q.shape[0] != width:
+        own_q = own_f.at[:, : 3 * own_cols]
+    load_q = pltpu.make_async_copy(wq, own_q, load_sem.at[4])
+
+    loads[0].wait()
+    loads[1].wait()
+    chunks = tokens // step
+    if chunks > 1:
+        gp_acc[...] = jnp.zeros_like(gp_acc)
+        gf_acc[...] = jnp.zeros_like(gf_acc)
+        gq_acc[...] = jnp.zeros_like(gq_acc)
+
+    def fetch(src, at, dst, i):
+        copy = pltpu.make_async_copy(src.at[at], dst, tmp_sem.at[i])
+        copy.start()
+        return copy
+
+    piece = min(256, step)
+
+    def feed_forward(i, carry):
+        at = pl.ds(pl.multiple_of(i * step, step), step)
+        first = fetch(h2, at, chunk, 2)
+        second = fetch(cot_in, at, chunk2, 3)
+        first.wait()
+        second.wait()
+
+        def one(j, inner_carry):
+            here = pl.ds(pl.multiple_of(j * piece, piece), piece)
+            there = pl.ds(pl.multiple_of(i * step + j * piece, piece), piece)
+            pre = jnp.dot(chunk[here, :], own_f[...], preferred_element_type=F32) + fcb_ref[...]
+            value, slope = gelu_parts(pre)
+            act[there, :] = value.astype(BF16)
+            back = lax.dot_general(chunk2[here, :], own_p[...], contract_last, preferred_element_type=F32)
+            gpre[there, :] = (back * slope).astype(BF16)
+            return inner_carry
+
+        lax.fori_loop(0, step // piece, one, 0)
+        product_rows(act.at[at], chunk2, into_jobs(jp) if chunks == 1 else into_sum(gp_acc))
+        if chunks > 1:
+            product_rows(chunk, gpre.at[at], into_sum(gf_acc))
+        return carry
+
+    if chunks == 1:
+        feed_forward(0, 0)
+    else:
+        lax.fori_loop(0, chunks, feed_forward, 0)
+        into_jobs(jp)(0, own_ff, gp_acc[...])
+        into_jobs(jf)(0, width, gf_acc[...])
+
     peers = devices - 1 + len(bits_of(z_size))
     pl.semaphore_wait(barrier, peers + jnp.where(s != z, 1, 0) + jnp.where(inner, 1, 0))
-
-    def core_of(offset):
-        return (offset // r_size) % 2
-
-    def slot(offset):
-        return (offset // r_size) // 2 * r_size + offset % r_size
-
-    def block(ref):
-        return lambda o, part: ref.at[pl.ds(o * rows + part * half, half)]
-
-    def packed_block(ref):
-        return lambda o, part: ref.at[pl.ds(slot(o) * rows + part * half, half)]
-
-    loads = []
-    plain = [(gproj, jp), (gfc, jf), (wq, own_q), (wo, own_o), (cot_in.at[pl.ds(0, rows)], cot_v)]
-    for i, (src, dst) in enumerate(plain):
-        loads.append(pltpu.make_async_copy(src, dst, load_sem.at[i]))
-    acc_loads = []
-    for i, (src, dst) in enumerate(((part2, acc2), (partp, accp))):
-        for so in range(0, s_size, 2):
-            n = r_size * rows
-            acc_loads.append(
-                pltpu.make_async_copy(
-                    src.at[pl.ds(so * n, n)], dst.at[pl.ds(so // 2 * n, n)], load_sem.at[len(plain) + 2 * i + so // 2]
-                )
-            )
-    scatter_two = Scatter(
-        block(part2), packed_block(acc2), block(land), lambda o, part: block(land)(o, part)[...], s2_send, s2_recv, r_size
-    )
-
-    def load_from_far(o, part):
-        copy = pltpu.make_async_copy(block(landp)(o, part), tmp, tmp_sem.at[0])
-        copy.start()
-        copy.wait()
-        return tmp[...]
-
-    scatter_proj = Scatter(
-        block(partp), packed_block(accp), block(landp), load_from_far, sp_send, sp_recv, r_size
-    )
-    scatter_two.start_leaves()
-    for copy in acc_loads[:2] + loads + acc_loads[2:]:
-        copy.start()
-    scatter_proj.start_leaves()
 
     def to_home(src, dst, send, recv, s_to, m):
         far = remote(src, dst, send, recv, s=s_to, r=r ^ m)
@@ -927,17 +994,69 @@
                 for m in range(r_size):
                     to_home(lo_.at[d, j], home_out.at[me, d, j], oh_send.at[i, m], oh_recv.at[me], s_to, m)
 
-    sum_proj = LineSum(jp, lp, p_rs, p_rr, p_as, p_ar, home_of_proj)
-    sum_fc = LineSum(jf, lf, f_rs, f_rr, f_as, f_ar, home_of_columns(lf, home_fc, fh_send, fh_recv))
-    sum_qkv = LineSum(jq, lq, q_rs, q_rr, q_as, q_ar, home_of_columns(lq, home_qkv, qh_send, qh_recv))
-    sum_out = LineSum(jo, lo_, o_rs, o_rr, o_as, o_ar, home_of_out)
-
-    for copy in loads + acc_loads:
-        copy.wait()
+    sum_proj = LineSum(jp, lp, p_rs, p_rr, p_as, p_ar, home_of_proj, 0)
+    start = sum_proj.n
+    sum_fc = LineSum(jf, lf, f_rs, f_rr, f_as, f_ar, home_of_columns(lf, home_fc, fh_send, fh_recv), start)
+    start += sum_fc.n
+    sum_out = LineSum(jo, lo_, o_rs, o_rr, o_as, o_ar, home_of_out, start)
+    start += sum_out.n
+    sum_qkv = LineSum(jq, lq, q_rs, q_rr, q_as, q_ar, home_of_columns(lq, home_qkv, qh_send, qh_recv), start)
+    clock = Clock([sum_proj, sum_fc, sum_out, sum_qkv])
+    clock.run(1)
+
+    def slot(offset):
+        return (offset // r_size) // 2 * r_size + offset % r_size
+
+    def block(ref):
+        return lambda o, part: ref.at[pl.ds(o * rows + part * half, half)]
+
+    def packed_block(ref):
+        return lambda o, part: ref.at[pl.ds(slot(o) * rows + part * half, half)]
+
+    def far_load(ref):
+        def load(o, part):
+            copy = pltpu.make_async_copy(block(ref)(o, part), tmp, tmp_sem.at[0])
+            copy.start()
+            copy.wait()
+            return tmp[...]
+
+        return load
+
+    if land_near.shape[0] == tokens:
+        land, load_land = block(land_near), lambda o, part: block(land_near)(o, part)[...]
+    else:
+        land, load_land = block(land_far), far_load(land_far)
+    scatter_two = Scatter(packed_block(leaf), packed_block(acc), land, load_land, s2_send, s2_recv, r_size)
+    scatter_proj = Scatter(
+        packed_block(leaf), packed_block(acc), block(landp), far_load(landp), sp_send, sp_recv, r_size
+    )
+    scatter_one = Scatter(packed_block(leaf), packed_block(acc), land, load_land, s1_send, s1_recv, r_size)
+    n = r_size * rows
+
+    def partial_sums(dst, odd, lhs, rhs, contract):
+        def one(i, carry):
+            dst[pl.ds(pl.multiple_of(i * n, n), n), :] = lax.dot_general(
+                lhs[pl.ds(pl.multiple_of((2 * i + odd) * n, n), n), :], rhs[...], contract, preferred_element_type=F32
+            ).astype(BF16)
+            return carry
+
+        lax.fori_loop(0, s_size // 2, one, 0)
+
+    partial_sums(leaf, 1, gpre, own_f, contract_last)
+    scatter_two.start_leaves()
+    clock.run(1)
+    partial_sums(acc, 0, gpre, own_f, contract_last)
+    load_q.start()
+    if chunks == 1:
+        product_rows(chunk, gpre, into_jobs(jf))
+    clock.run(1)
 
     scatter_two.start_inner()
+    clock.run(1)
     vec[...] = jnp.zeros_like(vec)
     gain_one, gain_two, proj_bias = (small_ref[i : i + 1, :] for i in (0, 3, 5))
+    for load in loads[2:]:
+        load.wait()
     cot = cot_v[...].astype(F32)
     middle = middle_ref[...]
     normed, inverse = norm_parts(middle)
@@ -945,7 +1064,6 @@
     grad_middle = cot + grad_in
     branch = grad_middle.astype(BF16)
     gb_own[...] = branch
-    ig_keep = grad_middle
     gather = Gather(block(gb), g_send, g_recv, r_size, own=lambda o, part: gb_own.at[pl.ds(part * half, half)])
     gather.start(0)
     save_gb = pltpu.make_async_copy(gb_own, gb.at[pl.ds(0, rows)], tmp_sem.at[1])
@@ -954,8 +1072,36 @@
     vec[3:4, :] = grad_gain
     vec[4:5, :] = grad_bias
     vec[5:6, :] = jnp.sum(cot, axis=0, keepdims=True)
+    clock.run(1)
     gather.start_rest()
+    scatter_two.close()
+    partial_sums(leaf, 1, act, own_p, (((1,), (0,)), ((), ())))
+    scatter_proj.start_leaves()
+    clock.run(1)
+    partial_sums(acc, 0, act, own_p, (((1,), (0,)), ((), ())))
+    gather.need_all()
+    save_gb.wait()
     scatter_proj.start_inner()
+    clock.run(1)
+
+    if chunks > 1:
+        go_acc[...] = jnp.zeros_like(go_acc)
+
+    def branch_rows(i, carry):
+        at = pl.ds(pl.multiple_of(i * step, step), step)
+        fetch(gb, at, chunk2, 3).wait()
+        do_ref[at, :] = lax.dot_general(
+            chunk2[...], own_o[...], contract_last, preferred_element_type=F32
+        ).astype(BF16)
+        product_rows(att_ref.at[at], chunk2, into_jobs(jo) if chunks == 1 else into_sum(go_acc))
+        return carry
+
+    if chunks == 1:
+        branch_rows(0, 0)
+    else:
+        lax.fori_loop(0, chunks, branch_rows, 0)
+        into_jobs(jo)(0, own_cols, go_acc[...])
+    clock.run(1)
     out_v[...] = (middle + (scatter_proj.finish() + proj_bias)).astype(BF16)
 
     def moved(src, dst, sem):
@@ -982,38 +1128,13 @@
         return done
 
     out_done = moved(out_v, out_home, mv_sem.at[0])
-    gather.need_all()
-    save_gb.wait()
-
-    step = chunk.shape[0]
-    go_acc[...] = jnp.zeros_like(go_acc)
-
-    def branch_rows(i, carry):
-        at = pl.ds(pl.multiple_of(i * step, step), step)
-        copy = pltpu.make_async_copy(gb.at[at], chunk, tmp_sem.at[2])
-        copy.start()
-        copy.wait()
-        do_ref[at, :] = lax.dot_general(
-            chunk[...], own_o[...], (((1,), (1,)), ((), ())), preferred_element_type=F32
-        ).astype(BF16)
-        go_acc[...] += lax.dot_general(
-            att_ref[at, :], chunk[...], (((0,), (0,)), ((), ())), preferred_element_type=F32
-        )
-        return carry
-
-    lax.fori_loop(0, tokens // step, branch_rows, 0)
-    out_rows = jo.shape[2]
-    for i in range(2 * jo.shape[1]):
-        jo[i // jo.shape[1], i % jo.shape[1]] = go_acc[i * out_rows : (i + 1) * out_rows, :].astype(BF16)
 
     code_row = jnp.concatenate([code_ref[i : i + 1, :] for i in range(devices)], axis=1)
     q_rows = min(rows if tokens > 2048 else 256, tokens)
     dk_acc[...] = jnp.zeros_like(dk_acc)
     dv_acc[...] = jnp.zeros_like(dv_acc)
-    contract_last = (((1,), (1,)), ((), ()))
-    contract_first = (((0,), (0,)), ((), ()))
-
-    def attend(i, carry):
+
+    def attend(i):
         at = pl.ds(pl.multiple_of(i * q_rows, q_rows), q_rows)
         per = q_rows // rows
         code_q = jnp.concatenate(
@@ -1041,82 +1162,65 @@
         gp[at, 0:own_cols] = (jnp.concatenate(dqs, axis=1) * (1.0 / math.sqrt(HEAD_DIM))).astype(BF16)
         dk_acc[...] += jnp.concatenate(dks, axis=1)
         dv_acc[...] += jnp.concatenate(dvs, axis=1)
-        return carry
-
-    lax.fori_loop(0, tokens // q_rows, attend, 0)
+
+    if chunks == 1:
+        clock.loop(tokens // q_rows, attend)
+    else:
+
+        def attend_step(i, carry):
+            attend(i)
+            return carry
+
+        lax.fori_loop(0, tokens // q_rows, attend_step, 0)
     gp[:, own_cols : 2 * own_cols] = dk_acc[...].astype(BF16)
     gp[:, 2 * own_cols :] = dv_acc[...].astype(BF16)
 
-    n = r_size * rows
-    leaf1 = accp
-    scatter_one = Scatter(
-        packed_block(leaf1), packed_block(acc2), block(land), lambda o, part: block(land)(o, part)[...],
-        s1_send, s1_recv, r_size,
-    )
-    scatter_two.close()
     scatter_proj.close()
-    for dst, odd in ((leaf1, 1), (acc2, 0)):
-
-        def partial(i, carry, dst=dst, odd=odd):
-            dst[pl.ds(pl.multiple_of(i * n, n), n), :] = lax.dot_general(
-                gp[pl.ds(pl.multiple_of((2 * i + odd) * n, n), n), :], own_q[...], contract_last,
-                preferred_element_type=F32,
-            ).astype(BF16)
-            return carry
-
-        lax.fori_loop(0, s_size // 2, partial, 0)
-        if odd:
-            scatter_one.start_leaves()
-    scatter_one.start_inner()
-
-    gq_acc[...] = jnp.zeros_like(gq_acc)
+    load_q.wait()
+    partial_sums(leaf, 1, gp, own_q, contract_last)
+    scatter_one.start_leaves()
+    partial_sums(acc, 0, gp, own_q, contract_last)
+    clock.run(1)
 
     def hidden_rows(i, carry):
         at = pl.ds(pl.multiple_of(i * step, step), step)
-        copy = pltpu.make_async_copy(h1.at[at], chunk, tmp_sem.at[2])
-        copy.start()
-        copy.wait()
-        gq_acc[...] += lax.dot_general(chunk[...], gp[at, :], contract_first, preferred_element_type=F32)
+        fetch(h1, at, chunk, 2).wait()
+        product_rows(chunk, gp.at[at], into_jobs(jq) if chunks == 1 else into_sum(gq_acc))
         return carry
 
-    lax.fori_loop(0, tokens // step, hidden_rows, 0)
-    per, q_job = jq.shape[1:3]
-    for i in range(2 * per):
-        jq[i // per, i % per] = gq_acc[i * q_job : (i + 1) * q_job, :].astype(BF16)
+    if chunks == 1:
+        hidden_rows(0, 0)
+    else:
+        lax.fori_loop(0, chunks, hidden_rows, 0)
+        into_jobs(jq)(0, width, gq_acc[...])
+    scatter_one.start_inner()
+    clock.run(2)
 
     resid = x_ref[...].astype(F32)
     normed, inverse = norm_parts(resid)
     grad_in, grad_gain, grad_bias = norm_backward_rows(scatter_one.finish(), normed, inverse, gain_one)
-    ig_v[...] = (ig_keep + grad_in).astype(BF16)
+    ig_v[...] = (grad_middle + grad_in).astype(BF16)
     ig_done = moved(ig_v, ig_home, mv_sem.at[1])
     vec[0:1, :] = grad_gain
     vec[1:2, :] = grad_bias
     ff_lanes = -(-own_ff // 128) * 128
     q_lanes = -(-own_cols // 128) * 128
-    vec[7:8, 0:own_ff] = fcb_ref[...]
+    vec[7:8, 0:own_ff] = jnp.sum(gpre[...].astype(F32), axis=0, keepdims=True)
     vec[7:8, ff_lanes : ff_lanes + own_cols] = jnp.sum(gp[:, :own_cols].astype(F32), axis=0, keepdims=True)
     vec[7:8, ff_lanes + q_lanes : ff_lanes + q_lanes + own_cols] = jnp.sum(
         gp[:, 2 * own_cols :].astype(F32), axis=0, keepdims=True
     )
     vec[pl.ds(8 + me, 1), :] = vec[7:8, :]
 
-    sum_proj.add_ticks(0, sum_proj.n + 3)
-    sum_fc.add_ticks(0, sum_fc.n + 3)
-    sum_proj.back_ticks(0, sum_proj.n + 2)
-    sum_fc.back_ticks(0, sum_fc.n + 2)
-    sum_out.add_ticks(0, sum_out.n + 3)
-    sum_qkv.add_ticks(0, sum_qkv.n + 3)
-
     hops = [("s", 1), ("s", 2)] + [("r", bit) for bit in bits_of(r_size)] + [("z", bit) for bit in bits_of(z_size)]
     for i, (axis, bit) in enumerate(hops):
         copy = remote(vec, vec_land.at[i], vec_send.at[i], vec_recv.at[i], **partner(axis, bit))
         copy.start()
+        clock.run(1)
         copy.wait()
         vec[...] = vec[...] + vec_land[i]
     small_out[...] = vec[...]
-
-    sum_out.back_ticks(0, sum_out.n + 2)
-    sum_qkv.back_ticks(0, sum_qkv.n + 2)
+    clock.run(clock.end)
 
     scatter_one.close()
     gather.close()
@@ -1158,16 +1262,14 @@
                 pltpu.make_async_copy(home_out.at[0], home_out.at[0], oh_send.at[i, m]).wait()
 
 
-def backward_part(
-    part2, partp, grad_proj, grad_fc, h1, wq, wo, q, k, v, att, lse, code, middle, x_own, cot, small, fcb
-):
+def backward_part(h2, cot, wf, wp, h1, wq, wo, q, k, v, att, lse, code, middle, x_own, small, fcb):
     s_size, r_size, z_size = (lax.axis_size(a) for a in ("s", "r", "z"))
     devices = s_size * r_size
     rows, width = x_own.shape
     tokens = rows * devices
     own_cols = q.shape[1]
     heads = own_cols // HEAD_DIM
-    own_ff = grad_proj.shape[0]
+    own_ff = wf.shape[1]
     shard_rows = width // s_size
     p_rows = job_rows(own_ff // 2)
     p_n = own_ff // 2 // p_rows
@@ -1178,6 +1280,8 @@
     o_n = own_cols // 2 // o_rows
     hops = 2 + len(bits_of(r_size)) + len(bits_of(z_size))
     vec_rows = 8 + devices
+    small_plane = tokens <= 1024
+    step = tokens if small_plane else 256
     anywhere = pl.BlockSpec(memory_space=pl.ANY)
     vmem = pl.BlockSpec(memory_space=pltpu.VMEM)
     shape = jax.ShapeDtypeStruct
@@ -1185,10 +1289,14 @@
     tree = [dma((2, devices))] * 2
     jobs = [(2, p_n, p_rows, width), (2, c_n, c_rows, own_ff), (2, c_n, c_rows, 3 * own_cols), (2, o_n, o_rows, width)]
     line = [dma(j[:2]) for j in jobs for _ in range(4)]
+
+    def sums(*dims):
+        return pltpu.VMEM((8, 128) if small_plane else dims, F32)
+
     return pl.pallas_call(
         backward_kernel,
-        in_specs=[anywhere] * 7 + [vmem] * 8 + [anywhere, vmem, vmem],
-        out_specs=[anywhere] * 6 + [vmem] + [anywhere] * 2,
+        in_specs=[anywhere] * 7 + [vmem] * 10,
+        out_specs=[anywhere] * 6 + [vmem] + [anywhere] * 3,
         out_shape=[
             shape((rows, width), BF16),
             shape((rows, width), BF16),
@@ -1199,35 +1307,43 @@
             shape((vec_rows, width), F32),
             shape((tokens, width), BF16),
             shape((tokens, width), BF16),
+            shape((tokens, width), BF16),
         ],
         scratch_shapes=[
             pltpu.VMEM((tokens // 2, width), BF16),
             pltpu.VMEM((tokens // 2, width), BF16),
-            pltpu.VMEM((tokens, width), BF16),
+            pltpu.VMEM((tokens if small_plane else 16, width), BF16),
             pltpu.VMEM((rows // 2, width), BF16),
         ]
         + [pltpu.VMEM(j, BF16) for j in jobs]
         + [pltpu.VMEM(j, BF16) for j in jobs]
         + [
-            pltpu.VMEM((width, 3 * own_cols), BF16),
+            pltpu.VMEM((width, own_ff), BF16),
+            pltpu.VMEM((own_ff, width), BF16),
+            pltpu.VMEM((16, 128) if small_plane else (width, 3 * own_cols), BF16),
             pltpu.VMEM((own_cols, width), BF16),
             pltpu.VMEM((rows, width), BF16),
-            pltpu.VMEM((256 if tokens > 2048 else min(512, tokens), width), BF16),
-            pltpu.VMEM((width, 3 * own_cols), F32),
+            pltpu.VMEM((step, width), BF16),
+            pltpu.VMEM((step, width), BF16),
+            sums(own_ff, width),
+            sums(width, own_ff),
+            sums(width, 3 * own_cols),
+            pltpu.VMEM((tokens, own_ff), BF16),
+            pltpu.VMEM((tokens, own_ff), BF16),
             pltpu.VMEM((tokens, own_cols), BF16),
             pltpu.VMEM((tokens, 3 * own_cols), BF16),
             pltpu.VMEM((tokens, own_cols), F32),
             pltpu.VMEM((tokens, own_cols), F32),
-            pltpu.VMEM((own_cols, width), F32),
+            sums(own_cols, width),
             pltpu.VMEM((vec_rows, width), F32),
             pltpu.VMEM((hops, vec_rows, width), F32),
             pltpu.VMEM((rows, width), BF16),
             pltpu.VMEM((rows, width), BF16),
             pltpu.VMEM((rows, width), BF16),
-            dma((10,)),
+            dma((5,)),
         ]
         + tree * 4
-        + [dma((3,)), dma((1,)), dma((2, 2)), dma((hops,)), dma((hops,))]
+        + [dma((4,)), dma((2, 2)), dma((hops,)), dma((hops,))]
         + line
         + [
             dma((r_size,)), dma((r_size,)),
@@ -1239,13 +1355,12 @@
             collective_id=1, has_side_effects=True, vmem_limit_bytes=62 << 20
         ),
         cost_estimate=pl.CostEstimate(
-            flops=10 * heads * tokens * tokens * HEAD_DIM, bytes_accessed=40 << 20, transcendentals=0
+            flops=10 * heads * tokens * tokens * HEAD_DIM + 12 * tokens * width * own_ff,
+            bytes_accessed=40 << 20,
+            transcendentals=0,
         ),
         name="backward_part",
-    )(
-        part2, partp, grad_proj.reshape(jobs[0]), grad_fc.reshape(jobs[1]), h1, wq, wo, q, k, v, att, lse, code, middle,
-        x_own, cot, small, fcb,
-    )
+    )(h2, cot, wf, wp, h1, wq, wo, q, k, v, att, lse, code, middle, x_own, small, fcb)
 
 
 def columns_out_kernel(parts, blocks_ref, out_ref):
@@ -1345,22 +1460,11 @@
         hidden_one, hidden_two, cot, own_fc, own_qkv, own_out, queries, keys, values, attended, lse, code_all,
         middle, x_own, small, smallh,
     ) = forward_part(inputs, cotangent, code, small, smallh, w_qkv, w_fc, w_out)
-    own_fcb = lax.dynamic_slice_in_dim(fc_bias, r * own_ff, own_ff).astype(F32)
-    own_proj = lax.dynamic_slice_in_dim(w_proj, r * own_ff, own_ff, axis=0)
-    pre_act = dot(hidden_two, own_fc) + own_fcb
-    activated, slope = gelu_parts(pre_act)
-    activated = activated.astype(BF16)
-    grad_act = dot(cot, own_proj, ON_LAST)
-    grad_pre = (grad_act * slope).astype(BF16)
-    grad_w_proj = dot(activated, cot, ACROSS_TOKENS).astype(BF16)
-    partial_two = dot(grad_pre, own_fc, ON_LAST).astype(BF16)
-    grad_w_fc = dot(hidden_two, grad_pre, ACROSS_TOKENS).astype(BF16)
-    partial_proj = dot(activated, own_proj).astype(BF16)
-    grad_fcb = jnp.sum(grad_pre.astype(F32), axis=0)
-    out_home, ig_home, home_proj, home_fc, home_qkv, home_out, sums, _, _ = backward_part(
-        partial_two, partial_proj, grad_w_proj, grad_w_fc, hidden_one, own_qkv, own_out, queries, keys, values,
-        attended, lse, code_all, middle, x_own, cot, small, grad_fcb.reshape(1, own_ff),
-    )
+    own_fcb = lax.dynamic_slice_in_dim(fc_bias, r * own_ff, own_ff).astype(F32).reshape(1, own_ff)
+    out_home, ig_home, home_proj, home_fc, home_qkv, home_out, sums = backward_part(
+        hidden_two, cot, own_fc, w_proj, hidden_one, own_qkv, own_out, queries, keys, values, attended, lse, code_all,
+        middle, x_own, small, own_fcb,
+    )[:7]
 
     def own_slice(vector):
         size = vector.shape[0] // s_size

time: 719 us -> 519 us (0.72)
  Pallas kernels: 626 us -> 478 us
  matrix products: 39.5 us -> 0 us
  local copies, waits for them, and re-layouts: 33.7 us -> 19.5 us
    pallas_call x1, Pallas kernels: 470 us -> 322 us  [backward_part(): pl.pallas_call(backward_kernel, in_specs=[anywhere] * 7 + [vmem] * 10, ou...]
    dot_general x6 -> x0, matrix products: 39.5 us -> none  [dot(): lax.dot_general(a, b, (contract, ((), ())), preferred_element_type=F32)]
    convert_element_type x3 -> x0, local copies, waits for them, and re-layouts: 14.1 us -> none  [the longest x1 5.4 us: local(): partial_two = dot(grad_pre, own_fc, ON_LAST).astype(BF16)]
where the time goes in v3:
time: 519 us; the launch traced here: 510 us
  Pallas kernels  478 us (92%)
  local copies, waits for them, and re-layouts  19.5 us (4%)
  other arithmetic  11.4 us (2%)
    pallas_call x1, Pallas kernels, backward_part(): pl.pallas_call(backward_kernel, in_specs=[anywhere] * 7 + [vmem] * 10, ou...  322 us
    pallas_call x1, Pallas kernels, forward_part(): pl.pallas_call(forward_kernel, in_specs=[anywhere, anywhere, anywhere, vm...  128 us
    pallas_call x2, Pallas kernels, columns_out(): pl.pallas_call(lambda *refs: columns_out_kernel(parts, *refs), grid=(chun...  22.2 us
    unnamed x17, local copies, waits for them, and re-layouts  11.1 us

profile of v3, /device:TPU:1, one launch (start us, length us, event | category | flops | bytes accessed | tf_op | source)
XLA Modules:
  0.0 510.2 jit_solution(14467653269758573245)
XLA Ops:
  0.7 0.7 fusion.1
  1.3 0.7 stack.53
  2.0 0.7 stack.54
  2.7 0.7 stack.55
  3.4 0.7 stack.56
  4.1 0.7 stack.57
  4.7 0.7 stack.58
  5.4 0.6 broadcast_in_dim.6.code_in
  6.0 0.8 dynamic-slice_convert_fusion.1
  6.8 0.6 reshape.96.fcb_ref
  7.4 0.2 dynamic_update_slice.31
  7.6 0.3 dynamic_update_slice.30
  8.0 0.3 dynamic_update_slice.29
  8.3 0.3 dynamic_update_slice.28
  8.6 0.3 dynamic_update_slice.27
  9.0 0.3 dynamic_update_slice.32
  9.3 0.7 stack.52.small_in
  10.0 0.8 convert_dynamic-update-slice_fusion
  10.8 0.1 slice.58
  10.8 0.7 slice_select_fusion
  11.6 0.6 pad_maximum_fusion.smallh_in
  12.2 2.0 copy.30.x_in
  14.1 2.0 copy.31.cot_in
  16.1 128.4 %forward_part.1 = (bf16[1024,1600]{1,0:T(8,128)(2,1)}, bf16[1024,1600]{1,0:T(8,128)(2,1)}, bf16[1024,1600]{1,0:T(8,128)(2,1)}, bf16[1600,800]{1,0:T(8,128)(2,1)}...) custom-call(bf16[128,1600]{1,0:T(8,128)(2,1)} %copy.30.x_in, ...), custom_call_target="tpu_custom_call" | custom-call | flops 3590324224 | bytes 41943040 | tf_op jit(solution)/shard_map/forward_part/pallas_call | solution.py:564
  144.5 322.0 %backward_part.1 = (bf16[128,1600]{1,0:T(8,128)(2,1)}, bf16[128,1600]{1,0:T(8,128)(2,1)}, bf16[2,2,5,80,1600]{4,3,2,1,0:T(8,128)(2,1)}, bf16[8,5,80,800]{3,2,1,0...) custom-call(bf16[1024,1600]{1,0:T(8,128)(2,1)} %get-tuple-element.36, ...), custom_call_target="tpu_custom_call" | custom-call | flops 18412994560 | bytes 41943040 | tf_op jit(solution)/shard_map/backward_part/pallas_call | solution.py:1296
  466.5 1.9 copy.32
  468.5 0.7 slice_bitcast_fusion
  469.2 0.7 fusion
  469.9 0.8 slice.55
  470.7 1.1 fusion.2
  471.8 0.7 constant_dynamic-slice_fusion
  472.5 0.1 reshape.87
  472.5 0.7 dynamic_slice.55
  473.2 0.7 constant_dynamic-slice_fusion.2
  473.9 0.7 constant_dynamic-slice_fusion.4
  474.5 2.1 copy.33
  476.6 0.0 slice-start
  476.6 3.1 dynamic-slice_convert_fusion
  479.8 0.0 copy-start
  479.8 2.4 copy-done
  482.2 0.0 slice-start.1
  482.2 0.0 slice-start.2
  482.2 10.6 %columns_out.2 = f32[400,4800]{1,0:T(8,128)} custom-call(bf16[8,5,80,768]{3,2,1,0:T(8,128)(2,1)S(1)} %copy-done), custom_call_target="tpu_custom_call" | custom-call | tf_op jit(solution)/shard_map/columns_out/pallas_call | solution.py:1382
  492.8 0.0 slice-done
  492.8 0.0 slice-done.1
  492.8 0.0 slice-start.3
  492.8 11.5 %columns_out.3 = f32[400,6400]{1,0:T(8,128)} custom-call(bf16[8,5,80,800]{3,2,1,0:T(8,128)(2,1)S(1)} %bitcast.23), custom_call_target="tpu_custom_call" | custom-call | tf_op jit(solution)/shard_map/columns_out/pallas_call | solution.py:1382
  504.3 0.0 slice-done.2
  504.3 0.0 slice-done.3
  504.4 5.6 %rows_out.1 = f32[1600,1600]{1,0:T(8,128)} custom-call(bf16[1600,1600]{1,0:T(8,128)(2,1)S(1)} %bitcast.26), custom_call_target="tpu_custom_call" | custom-call | tf_op jit(solution)/shard_map/rows_out/pallas_call | solution.py:1400
  (15 shorter events, 0.1 us)
Async XLA Ops:
  476.6 16.2 %slice-start = ((s8[5734400]{0:T(1024)(128)(4,1)}), s8[4194304]{0:T(1024)(128)(4,1)S(1)}, s32[]{:S(2)}) async-start(s8[5734400]{0:T(1024)(128)(4,1)} %bitcast.22), calls=%async_computation | async-start | bytes 8388608
  479.8 2.4 copy-start
  482.2 10.6 %slice-start.1 = ((s8[5734400]{0:T(1024)(128)(4,1)}), s8[1540096]{0:T(1024)(128)(4,1)S(1)}, s32[]{:S(2)}) async-start(s8[5734400]{0:T(1024)(128)(4,1)} %bitcast.22), calls=%async_computation.1 | async-start | bytes 3080192
  482.2 22.2 %slice-start.2 = ((s8[5324800]{0:T(1024)(128)(4,1)}), s8[4194304]{0:T(1024)(128)(4,1)S(1)}, s32[]{:S(2)}) async-start(s8[5324800]{0:T(1024)(128)(4,1)} %bitcast.24), calls=%async_computation.2 | async-start | bytes 8388608
  492.8 11.6 %slice-start.3 = ((s8[5324800]{0:T(1024)(128)(4,1)}), s8[1130496]{0:T(1024)(128)(4,1)S(1)}, s32[]{:S(2)}) async-start(s8[5324800]{0:T(1024)(128)(4,1)} %bitcast.24), calls=%async_computation.3 | async-start | bytes 2260992

commit v4 on v3

--- a/solution.py
+++ b/solution.py
@@ -271,10 +271,10 @@
 
 
 def forward_kernel(
-    x_in, cot_in, code_in, small_in, smallh_in, wq_in, wf_in, wo_in,
+    x_in, cot_in, code_in, g1_in, b1_in, ob_in, g2_in, b2_in, pb_in, qv_in, fcb_in, wq_in, wf_in, wo_in,
     h1_out, h2_out, cot_out, wf_out, wq_out, wo_out, q_ref, k_ref, v_ref, att_ref, lse_ref, code_out,
-    middle_out, x_own, small_ref, smallh_ref,
-    code_land, small_land, smallh_land, h1, wq_vm, stage_q, wf_vm, stage_f, own_q, full_out, att_land, h2_own,
+    middle_out, x_own, small_ref, fcb_out,
+    xt_vm, ct_vm, x_vm, cot_vm, vec_in, code_land, vec_land, bias_ref, h1, wq_vm, stage_q, wf_vm, stage_f, own_q, full_out, att_land, h2_own,
     x_sem, code_sem, cot_sem, small_sem, load_sem, h1_send, h1_recv, cd_send, cd_recv, ct_send, ct_recv, h2_send,
     h2_recv, wq_send, wq_recv, wf_send, wf_recv, wo_send, wo_recv, at_send, at_recv, out_sem,
 ):
@@ -282,7 +282,7 @@
     s_size, r_size = lax.axis_size("s"), lax.axis_size("r")
     devices = s_size * r_size
     me = s * r_size + r
-    rows, width = x_in.shape
+    width, rows = x_in.shape
     tokens = rows * devices
     own_cols = q_ref.shape[1]
     own_ff = wf_out.shape[1]
@@ -291,6 +291,13 @@
     def shard_at(i, first=0, count=shard_rows):
         return pl.ds(pl.multiple_of(i * shard_rows + first, 16), count)
 
+    x_loads = [
+        pltpu.make_async_copy(x_in, xt_vm, load_sem.at[3]),
+        pltpu.make_async_copy(cot_in, ct_vm, load_sem.at[4]),
+    ]
+    for load in x_loads:
+        load.start()
+
     barrier = pltpu.get_barrier_semaphore()
     for offset in range(1, devices):
         pl.semaphore_signal(barrier, inc=1, device_id=plane_device(offset, r_size), device_id_type=MESH_ID)
@@ -300,6 +307,13 @@
     def _():
         pl.semaphore_signal(barrier, inc=1, device_id={"z": s, "s": z}, device_id_type=MESH_ID)
 
+    at = 0
+    for ref in (g1_in, b1_in, ob_in, g2_in, b2_in, pb_in, qv_in, fcb_in):
+        vec_in[0:1, at : at + ref.shape[0]] = ref[...].astype(F32).reshape(1, ref.shape[0])
+        at += ref.shape[0]
+    for load, src, dst in zip(x_loads, (xt_vm, ct_vm), (x_vm, cot_vm)):
+        load.wait()
+        dst[...] = jnp.transpose(src[...])
     pl.semaphore_wait(barrier, devices + jnp.where(s != z, 1, 0))
 
     def moved(src, dst, sem):
@@ -330,7 +344,7 @@
 
         return arrived, sent
 
-    x_arrived, x_sent = moved(x_in, x_own, x_sem)
+    x_arrived, x_sent = moved(x_vm, x_own, x_sem)
     code_arrived, code_sent = moved(code_in, code_land.at[0], code_sem)
     loads = [
         pltpu.make_async_copy(wq_in, wq_vm, load_sem.at[0]),
@@ -339,16 +353,12 @@
     ]
     for load in loads:
         load.start()
-    small_copies = []
-    for m in range(1, s_size):
-        small_copies.append(
-            remote(small_in, small_land.at[m], small_sem.at[0, m], small_sem.at[1, m], s=s ^ m)
-        )
-        small_copies.append(
-            remote(smallh_in, smallh_land.at[m], small_sem.at[2, m], small_sem.at[3, m], s=s ^ m)
-        )
+    small_copies = [
+        remote(vec_in, vec_land.at[s], small_sem.at[0, m], small_sem.at[1, m], s=s ^ m) for m in range(1, s_size)
+    ]
     for copy in small_copies:
         copy.start()
+    vec_land[s] = vec_in[...]
     if full_out.shape[0] > width:
         full_out[width:, :] = jnp.zeros((full_out.shape[0] - width, width), BF16)
 
@@ -381,16 +391,30 @@
 
     for copy in small_copies:
         copy.wait_recv()
-    small = small_in[...]
-    smallh = smallh_in[...]
-    for m in range(1, s_size):
-        small = small + small_land[m]
-        smallh = smallh + smallh_land[m]
-    small_ref[...] = small
-    smallh_ref[...] = smallh
+    per = shard_rows
+    small_ref[...] = jnp.zeros_like(small_ref)
+    for s2 in range(s_size):
+        for i in range(6):
+            small_ref[i : i + 1, s2 * per : (s2 + 1) * per] = vec_land[s2, :, i * per : (i + 1) * per]
+    for part in range(2):
+        q_or_v = jnp.concatenate(
+            [vec_land[part * s_size // 2 + i, :, 6 * per : 8 * per] for i in range(s_size // 2)], axis=1
+        )
+        for device in range(devices):
+            n = max(0, min(own_cols, width - device * own_cols))
+            if n:
+                bias_ref[part, device : device + 1, 0:n] = q_or_v[:, device * own_cols : device * own_cols + n]
+            if n < own_cols:
+                bias_ref[part, device : device + 1, n:] = jnp.zeros((1, own_cols - n), F32)
+    for r2 in range(r_size):
+
+        @pl.when(r == r2)
+        def _(r2=r2):
+            fcb_out[...] = vec_in[:, 8 * per + r2 * own_ff : 8 * per + (r2 + 1) * own_ff]
+
     gain_one, bias_one, out_bias, gain_two, bias_two = (small_ref[i : i + 1, :] for i in range(5))
     x_arrived()
-    cot_arrived, cot_sent = moved(cot_in, cot_out.at[pl.ds(0, rows)], cot_sem)
+    cot_arrived, cot_sent = moved(cot_vm, cot_out.at[pl.ds(0, rows)], cot_sem)
     resid = x_own[...].astype(F32)
     normed, _ = norm_parts(resid)
     h1[0:rows, :] = (normed * gain_one + bias_one).astype(BF16)
@@ -445,8 +469,8 @@
     save_q.start()
     save_h = pltpu.make_async_copy(h1, h1_out, out_sem.at[1])
     save_h.start()
-    q_bias = smallh_ref[pl.ds(me, 1), :]
-    v_bias = smallh_ref[pl.ds(devices + me, 1), :]
+    q_bias = bias_ref[0, pl.ds(me, 1), :]
+    v_bias = bias_ref[1, pl.ds(me, 1), :]
     step = min(512, tokens)
     score_scale = jnp.asarray(1.0 / math.sqrt(HEAD_DIM), BF16)
 
@@ -546,10 +570,10 @@
         save.wait()
 
 
-def forward_part(x, cot, code, small, smallh, w_qkv, w_fc, w_out):
+def forward_part(x, cot, code, small, w_qkv, w_fc, w_out):
     s_size, r_size = lax.axis_size("s"), lax.axis_size("r")
     devices = s_size * r_size
-    rows, width = x.shape
+    width, rows = x.shape
     tokens = rows * devices
     shard_rows = w_qkv.shape[0]
     heads = width // HEAD_DIM
@@ -563,7 +587,7 @@
     flops = 2 * tokens * width * 3 * own_cols + 4 * own_heads * tokens * tokens * HEAD_DIM
     return pl.pallas_call(
         forward_kernel,
-        in_specs=[anywhere, anywhere, anywhere, vmem, vmem, anywhere, anywhere, anywhere],
+        in_specs=[anywhere] * 3 + [vmem] * 8 + [anywhere] * 3,
         out_specs=[anywhere] * 6 + [vmem] * 10,
         out_shape=[
             shape((tokens, width), BF16),
@@ -580,13 +604,18 @@
             shape((devices, rows), jnp.int32),
             shape((rows, width), F32),
             shape((rows, width), BF16),
-            shape(small.shape, F32),
-            shape(smallh.shape, F32),
+            shape((8, width), F32),
+            shape((1, own_ff), F32),
         ],
         scratch_shapes=[
+            pltpu.VMEM((width, rows), BF16),
+            pltpu.VMEM((width, rows), BF16),
+            pltpu.VMEM((rows, width), BF16),
+            pltpu.VMEM((rows, width), BF16),
+            pltpu.VMEM((1, sum(a.shape[0] for a in small)), F32),
             pltpu.VMEM((devices, 8, rows), jnp.int32),
-            pltpu.VMEM((s_size,) + small.shape, F32),
-            pltpu.VMEM((s_size,) + smallh.shape, F32),
+            pltpu.VMEM((s_size, 1, sum(a.shape[0] for a in small)), F32),
+            pltpu.VMEM((2, devices, own_cols), F32),
             pltpu.VMEM((tokens, width), BF16),
             pltpu.VMEM(w_qkv.shape, BF16),
             pltpu.VMEM((s_size, shard_rows, 3 * own_cols), BF16),
@@ -596,7 +625,7 @@
             pltpu.VMEM((devices * own_cols, width), BF16),
             pltpu.VMEM((devices, rows, own_cols), BF16),
             pltpu.VMEM((rows, width), BF16),
-            dma((2,)), dma((2,)), dma((2,)), dma((4, s_size)), dma((3,)),
+            dma((2,)), dma((2,)), dma((2,)), dma((2, s_size)), dma((5,)),
             dma((2, devices)), dma((2, devices)), dma((1, devices)), dma((1, devices)),
             dma((2, devices)), dma((2, devices)), dma((2, devices)), dma((2, devices)),
             dma((6,)), dma((6,)), dma((6,)), dma((6,)), dma((6,)), dma((6,)),
@@ -607,7 +636,7 @@
         ),
         cost_estimate=pl.CostEstimate(flops=flops, bytes_accessed=40 << 20, transcendentals=0),
         name="forward_part",
-    )(x, cot, code, small, smallh, w_qkv, w_fc, w_out)
+    )(x, cot, code, *small, w_qkv, w_fc, w_out)
 
 
 class Scatter:
@@ -986,13 +1015,20 @@
         b = (me * own_cols + own_cols - 1) // shard_rows
         return ((a, a < s_size), (b, jnp.logical_and(b != a, b < s_size)))
 
+    margin = (home_out.shape[0] - shard_rows) // 2
+
+    def out_at(s_to, d, j):
+        n_out, size = lo_.shape[1:3]
+        first = margin + me * own_cols - s_to * shard_rows + (d * n_out + j) * size
+        return pl.ds(pl.multiple_of(first, 16), size)
+
     def home_of_out(d, j):
         for i, (s_to, valid) in enumerate(out_targets()):
 
             @pl.when(valid)
             def _(i=i, s_to=s_to):
                 for m in range(r_size):
-                    to_home(lo_.at[d, j], home_out.at[me, d, j], oh_send.at[i, m], oh_recv.at[me], s_to, m)
+                    to_home(lo_.at[d, j], home_out.at[out_at(s_to, d, j)], oh_send.at[i, m], oh_recv.at[me], s_to, m)
 
     sum_proj = LineSum(jp, lp, p_rs, p_rr, p_as, p_ar, home_of_proj, 0)
     start = sum_proj.n
@@ -1246,12 +1282,13 @@
                     def _(sent=sent):
                         sent.wait()
 
+    out_block = home_out.at[pl.ds(0, own_cols)]
     for i in range(devices):
         a, b = (i * own_cols) // shard_rows, (i * own_cols + own_cols - 1) // shard_rows
 
         @pl.when(jnp.logical_or(s == a, s == b))
         def _(i=i):
-            pltpu.make_async_copy(home_out.at[i], home_out.at[i], oh_recv.at[i]).wait()
+            pltpu.make_async_copy(out_block, out_block, oh_recv.at[i]).wait()
 
     for i, (s_to, valid) in enumerate(out_targets()):
         for m in range(r_size):
@@ -1259,7 +1296,7 @@
 
             @pl.when(far)
             def _(i=i, m=m):
-                pltpu.make_async_copy(home_out.at[0], home_out.at[0], oh_send.at[i, m]).wait()
+                pltpu.make_async_copy(out_block, out_block, oh_send.at[i, m]).wait()
 
 
 def backward_part(h2, cot, wf, wp, h1, wq, wo, q, k, v, att, lse, code, middle, x_own, small, fcb):
@@ -1303,7 +1340,7 @@
             shape((r_size,) + jobs[0], BF16),
             shape((devices, c_per, c_rows, own_ff), BF16),
             shape((devices, c_per, c_rows, 3 * own_cols), BF16),
-            shape((devices,) + jobs[3], BF16),
+            shape((2 * (-(-own_cols // c_rows)) * c_rows + shard_rows, width), BF16),
             shape((vec_rows, width), F32),
             shape((tokens, width), BF16),
             shape((tokens, width), BF16),
@@ -1363,53 +1400,115 @@
     )(h2, cot, wf, wp, h1, wq, wo, q, k, v, att, lse, code, middle, x_own, small, fcb)
 
 
-def columns_out_kernel(parts, blocks_ref, out_ref):
-    devices = blocks_ref.shape[0]
-    each = blocks_ref.shape[3] // len(parts)
-    for i, (first, width) in enumerate(parts):
+def results_kernel(
+    out_in, ig_in, proj_in, fc_in, qkv_in, wo_in, sums,
+    out, ig, g1, b1, qkv, qv, wo, ob, g2, b2, fc, fcb, proj, pb,
+):
+    devices = fc_in.shape[0]
+    own_ff, own_cols = fc_in.shape[3], qkv_in.shape[3] // 3
+    width = wo.shape[1]
+    proj[...] = proj_in[...].astype(F32)
+    wo[...] = wo_in[...].astype(F32)
+    fc[...] = jnp.concatenate([fc_in[device, 0] for device in range(devices)], axis=1).astype(F32)
+    parts = []
+    for part in range(3):
         for device in range(devices):
-            n = max(0, min(each, width - device * each))
+            n = max(0, min(own_cols, width - device * own_cols))
             if n:
-                lo = first + device * each
-                out_ref[:, lo : lo + n] = blocks_ref[device, 0, :, i * each : i * each + n].astype(F32)
-
-
-def columns_out(blocks, parts):
-    devices, chunks, rows, columns = blocks.shape
-    total = parts[-1][0] + parts[-1][1]
-    step = 16 if rows % 16 == 0 else rows
-    per = rows // step
+                parts.append(qkv_in[device, 0, :, part * own_cols : part * own_cols + n])
+    qkv[...] = jnp.concatenate(parts, axis=1).astype(F32)
+
+    @pl.when(pl.program_id(0) == 0)
+    def _():
+        out[...] = jnp.transpose(out_in[...])
+        ig[...] = jnp.transpose(ig_in[...].astype(F32))
+        s = lax.axis_index("s")
+        s_size = lax.axis_size("s")
+        ff_lanes = -(-own_ff // 128) * 128
+        q_lanes = -(-own_cols // 128) * 128
+        by_device = devices // s_size
+
+        def heads_of(first):
+            return jnp.concatenate(
+                [sums[8 + d : 9 + d, first : first + own_cols] for d in range(devices)], axis=1
+            )[:, :width]
+
+        qv_all = jnp.concatenate([heads_of(ff_lanes), heads_of(ff_lanes + q_lanes)], axis=1)
+        for s2 in range(s_size):
+
+            @pl.when(s == s2)
+            def _(s2=s2):
+                n = width // s_size
+                for i, ref in enumerate((g1, b1, ob, g2, b2, pb)):
+                    ref[...] = sums[i, s2 * n : (s2 + 1) * n]
+                qv[...] = qv_all[0, 2 * s2 * n : 2 * (s2 + 1) * n]
+                fcb[...] = jnp.concatenate(
+                    [sums[8 + d : 9 + d, 0:own_ff] for d in range(s2 * by_device, (s2 + 1) * by_device)], axis=1
+                )[0]
+
+
+def results(out_home, ig_home, home_proj, home_fc, home_qkv, home_out, sums):
+    devices, c_per, c_rows, own_ff = home_fc.shape
+    rows, width = out_home.shape
+    shard_rows = c_per * c_rows
+    own_cols = home_qkv.shape[3] // 3
+    proj = home_proj.reshape(-1, width)
+    ff = devices * own_ff
+    steps = c_per
+    proj_rows = proj.shape[0] // steps
+    first = (home_out.shape[0] - shard_rows) // 2 // c_rows
+    whole = lambda *dims: pl.BlockSpec(dims, lambda i: (0,) * len(dims))
+    by_rows = lambda n, columns: pl.BlockSpec((n, columns), lambda i: (i, 0))
+    by_device = lambda columns: pl.BlockSpec((devices, 1, c_rows, columns), lambda i: (0, i, 0, 0))
+    shape = lambda *dims: jax.ShapeDtypeStruct(dims, F32)
+    vector = whole(shard_rows)
     return pl.pallas_call(
-        lambda *refs: columns_out_kernel(parts, *refs),
-        grid=(chunks, per),
-        in_specs=[pl.BlockSpec((devices, 1, step, columns), lambda i, j: (0, i, j, 0))],
-        out_specs=pl.BlockSpec((step, total), lambda i, j: (i * per + j, 0)),
-        out_shape=jax.ShapeDtypeStruct((chunks * rows, total), F32),
-        compiler_params=pltpu.CompilerParams(vmem_limit_bytes=32 << 20),
-        name="columns_out",
-    )(blocks)
-
-
-def rows_out_kernel(rows_ref, out_ref):
-    out_ref[...] = rows_ref[...].astype(F32)
-
-
-def rows_out(x):
-    rows, width = x.shape
-    step = job_rows(rows, 160)
-    return pl.pallas_call(
-        rows_out_kernel,
-        grid=(rows // step,),
-        in_specs=[pl.BlockSpec((step, width), lambda i: (i, 0))],
-        out_specs=pl.BlockSpec((step, width), lambda i: (i, 0)),
-        out_shape=jax.ShapeDtypeStruct((rows, width), F32),
-        compiler_params=pltpu.CompilerParams(vmem_limit_bytes=32 << 20),
-        name="rows_out",
-    )(x)
-
-
-def place(values_in, total, offset):
-    return lax.dynamic_update_slice_in_dim(jnp.zeros((total,), F32), values_in.astype(F32), offset, axis=0)
+        results_kernel,
+        grid=(steps,),
+        in_specs=[
+            whole(rows, width),
+            whole(rows, width),
+            by_rows(proj_rows, width),
+            by_device(own_ff),
+            by_device(3 * own_cols),
+            pl.BlockSpec((c_rows, width), lambda i: (first + i, 0)),
+            whole(*sums.shape),
+        ],
+        out_specs=[
+            whole(width, rows),
+            whole(width, rows),
+            vector,
+            vector,
+            by_rows(c_rows, 3 * width),
+            whole(2 * shard_rows),
+            by_rows(c_rows, width),
+            vector,
+            vector,
+            vector,
+            by_rows(c_rows, ff),
+            whole(proj.shape[0]),
+            by_rows(proj_rows, width),
+            vector,
+        ],
+        out_shape=[
+            jax.ShapeDtypeStruct((width, rows), BF16),
+            shape(width, rows),
+            shape(shard_rows),
+            shape(shard_rows),
+            shape(shard_rows, 3 * width),
+            shape(2 * shard_rows),
+            shape(shard_rows, width),
+            shape(shard_rows),
+            shape(shard_rows),
+            shape(shard_rows),
+            shape(shard_rows, ff),
+            shape(proj.shape[0]),
+            shape(*proj.shape),
+            shape(shard_rows),
+        ],
+        compiler_params=pltpu.CompilerParams(vmem_limit_bytes=61 << 20),
+        name="results",
+    )(out_home, ig_home, proj, home_fc, home_qkv, home_out, sums)
 
 
 def local(
@@ -1430,72 +1529,20 @@
     w_proj,
     proj_bias,
 ):
-    s = lax.axis_index("s")
-    r = lax.axis_index("r")
-    s_size = lax.axis_size("s")
-    r_size = lax.axis_size("r")
-    devices = s_size * r_size
-    me = s * r_size + r
-    rows, width = inputs.shape
-    heads = width // HEAD_DIM
-    own_heads = -(-heads // devices)
-    own_cols = own_heads * HEAD_DIM
-    head_total = own_cols * devices
-    ff = w_fc.shape[1]
-    own_ff = ff // devices
-    shard_rows = width // s_size
-
-    def head_pad(a):
-        return jnp.pad(a, (0, head_total - width)).reshape(devices, own_cols)
-
+    rows = inputs.shape[0]
     code = jnp.broadcast_to(segments * SEG_STEP + positions // BLOCK, (8, rows))
-    small = jnp.stack(
-        [place(a, width, s * shard_rows) for a in (ln1_gain, ln1_bias, out_bias, ln2_gain, ln2_bias, proj_bias)]
-        + [jnp.zeros((width,), F32)] * 2
-    )
-    qv = place(qv_bias, 2 * width, s * 2 * shard_rows)
-    smallh = jnp.concatenate([head_pad(qv[:width]), head_pad(qv[width:])])
+    vectors = (ln1_gain, ln1_bias, out_bias, ln2_gain, ln2_bias, proj_bias, qv_bias, fc_bias)
 
     (
         hidden_one, hidden_two, cot, own_fc, own_qkv, own_out, queries, keys, values, attended, lse, code_all,
-        middle, x_own, small, smallh,
-    ) = forward_part(inputs, cotangent, code, small, smallh, w_qkv, w_fc, w_out)
-    own_fcb = lax.dynamic_slice_in_dim(fc_bias, r * own_ff, own_ff).astype(F32).reshape(1, own_ff)
-    out_home, ig_home, home_proj, home_fc, home_qkv, home_out, sums = backward_part(
+        middle, x_own, small, own_fcb,
+    ) = forward_part(inputs.T, cotangent.T, code, vectors, w_qkv, w_fc, w_out)
+    found = backward_part(
         hidden_two, cot, own_fc, w_proj, hidden_one, own_qkv, own_out, queries, keys, values, attended, lse, code_all,
         middle, x_own, small, own_fcb,
-    )[:7]
-
-    def own_slice(vector):
-        size = vector.shape[0] // s_size
-        return lax.dynamic_slice_in_dim(vector, s * size, size)
-
-    ff_lanes = -(-own_ff // 128) * 128
-    q_lanes = -(-own_cols // 128) * 128
-    by_device = sums[8:]
-    g_fcb = by_device[:, :own_ff].reshape(ff)
-    g_qb = by_device[:, ff_lanes : ff_lanes + own_cols].reshape(-1)[:width]
-    g_vb = by_device[:, ff_lanes + q_lanes : ff_lanes + q_lanes + own_cols].reshape(-1)[:width]
-    g_fc = columns_out(home_fc, [(0, ff)])
-    g_qkv = columns_out(home_qkv, [(i * width, width) for i in range(3)])
-    g_out = lax.dynamic_slice_in_dim(home_out.reshape(head_total, width), s * shard_rows, shard_rows)
-    g_proj = rows_out(home_proj.reshape(ff // s_size, width))
-    return (
-        out_home,
-        ig_home.astype(F32),
-        own_slice(sums[0]),
-        own_slice(sums[1]),
-        g_qkv,
-        own_slice(jnp.concatenate([g_qb, g_vb])),
-        g_out.astype(F32),
-        own_slice(sums[2]),
-        own_slice(sums[3]),
-        own_slice(sums[4]),
-        g_fc,
-        own_slice(g_fcb),
-        g_proj,
-        own_slice(sums[5]),
     )
+    out, input_grad, *grads = results(*found[:7])
+    return (out.T, input_grad.T, *grads)
 
 
 def solution(mesh):

time: 519 us -> 477 us (0.919)
  local copies, waits for them, and re-layouts: 19.5 us -> 0.6 us
  Pallas kernels: 478 us -> 467 us
  other arithmetic: 11.4 us -> 0.68 us
    unnamed x17 -> x0, local copies, waits for them, and re-layouts: 11.1 us -> none
    pallas_call x4 -> x2, Pallas kernels: 156 us -> 147 us  [the longest x1 129 us: forward_part(): pl.pallas_call(forward_kernel, in_specs=[anywhere] * 3 + [vmem] * 8 + [an...]
where the time goes in v4:
time: 477 us; the launch traced here: 469 us
  Pallas kernels  467 us (98%)
    pallas_call x1, Pallas kernels, backward_part(): pl.pallas_call(backward_kernel, in_specs=[anywhere] * 7 + [vmem] * 10, ou...  320 us
    pallas_call x1, Pallas kernels, forward_part(): pl.pallas_call(forward_kernel, in_specs=[anywhere] * 3 + [vmem] * 8 + [an...  129 us
    pallas_call x1, Pallas kernels, results(): pl.pallas_call(results_kernel, grid=(steps,), in_specs=[whole(rows, width...  18.6 us

profile of v4, /device:TPU:1, one launch (start us, length us, event | category | flops | bytes accessed | tf_op | source)
XLA Modules:
  0.0 469.3 jit_solution(14778549307780310324)
XLA Ops:
  0.6 0.7 fusion
  1.3 0.6 broadcast_in_dim.3.code_in
  1.9 128.7 %forward_part.1 = (bf16[1024,1600]{1,0:T(8,128)(2,1)}, bf16[1024,1600]{1,0:T(8,128)(2,1)}, bf16[1024,1600]{1,0:T(8,128)(2,1)}, bf16[1600,800]{1,0:T(8,128)(2,1)}...) custom-call(bf16[1600,128]{1,0:T(8,128)(2,1)} %bitcast.7, ...), custom_call_target="tpu_custom_call" | custom-call | flops 3590324224 | bytes 41943040 | tf_op jit(solution)/shard_map/forward_part/pallas_call | solution.py:588
  130.6 319.8 %backward_part.1 = (bf16[128,1600]{1,0:T(8,128)(2,1)}, bf16[128,1600]{1,0:T(8,128)(2,1)}, bf16[2,2,5,80,1600]{4,3,2,1,0:T(8,128)(2,1)}, bf16[8,5,80,800]{3,2,1,0...) custom-call(bf16[1024,1600]{1,0:T(8,128)(2,1)} %get-tuple-element.51, ...), custom_call_target="tpu_custom_call" | custom-call | flops 18412994560 | bytes 41943040 | tf_op jit(solution)/shard_map/backward_part/pallas_call | solution.py:1333
  450.5 18.6 %results.1 = (bf16[1600,128]{1,0:T(8,128)(2,1)}, f32[1600,128]{1,0:T(8,128)}, f32[400]{0:T(512)}, f32[400]{0:T(512)}, f32[400,4800]{1,0:T(8,128)}, /*index=5*/f3...) custom-call(bf16[128,1600]{1,0:T(8,128)(2,1)} %get-tuple-element.67., ...), custom_call_target="tpu_custom_call" | custom-call | tf_op jit(solution)/shard_map/results/pallas_call | solution.py:1465

commit v5 on v4

--- a/solution.py
+++ b/solution.py
@@ -414,7 +414,6 @@
 
     gain_one, bias_one, out_bias, gain_two, bias_two = (small_ref[i : i + 1, :] for i in range(5))
     x_arrived()
-    cot_arrived, cot_sent = moved(cot_vm, cot_out.at[pl.ds(0, rows)], cot_sem)
     resid = x_own[...].astype(F32)
     normed, _ = norm_parts(resid)
     h1[0:rows, :] = (normed * gain_one + bias_one).astype(BF16)
@@ -460,6 +459,7 @@
     )
     own_f.start()
     gather_one.need_all()
+    cot_arrived, cot_sent = moved(cot_vm, cot_out.at[pl.ds(0, rows)], cot_sem)
     loads[2].wait()
     push_o.start()
     push_f.start()
@@ -483,9 +483,6 @@
         return carry
 
     lax.fori_loop(0, tokens // step, project, 0)
-    cot_arrived()
-    gather_cot = Gather(block_of(cot_out), ct_send, ct_recv, r_size)
-    gather_cot.start(0)
     gather_code.need_all()
     code_out[...] = code_land[:, 0, :]
     code_row = jnp.concatenate([code_land[i, 0:1, :] for i in range(devices)], axis=1)
@@ -519,6 +516,9 @@
     for copy in at_copies:
         copy.start()
     att_land[me] = att_ref[0:rows, :]
+    cot_arrived()
+    gather_cot = Gather(block_of(cot_out), ct_send, ct_recv, r_size)
+    gather_cot.start(0)
     push_o.relay()
     push_o.need()
     far = full_out.at[shard_at(s ^ 2)]
@@ -694,7 +694,7 @@
 
 
 class LineSum:
-    def __init__(self, jobs, land, rs_send, rs_recv, ag_send, ag_recv, home, start):
+    def __init__(self, jobs, land, rs_send, rs_recv, ag_send, ag_recv, home, start, lag):
         self.jobs, self.land = jobs, land
         self.rs_send, self.rs_recv, self.ag_send, self.ag_recv = rs_send, rs_recv, ag_send, ag_recv
         self.home = home
@@ -702,7 +702,8 @@
         self.z = lax.axis_index("z")
         self.last = lax.axis_size("z") - 1
         self.start = start
-        self.end = start + self.n + 2 * self.last
+        self.lag = lag
+        self.end = start + self.n + 2 * lag * self.last
 
     def place(self, d):
         return self.z if d == 0 else self.last - self.z
@@ -754,7 +755,7 @@
 
     def tick(self, k):
         for d in range(2):
-            j = k - self.start - self.place(d)
+            j = k - self.start - self.lag * self.place(d)
 
             @pl.when(jnp.logical_and(j >= 0, j < self.n))
             def _(d=d, j=j):
@@ -762,7 +763,7 @@
 
         for d in range(2):
             place = self.place(d)
-            j = k - self.start - 2 * self.last + place
+            j = k - self.start - self.lag * (2 * self.last - place)
 
             @pl.when(jnp.logical_and(place < self.last, jnp.logical_and(j >= 0, j < self.n)))
             def _(d=d, j=j):
@@ -810,13 +811,14 @@
 
             lax.fori_loop(lo, hi, step, 0)
 
-    def loop(self, count, body):
-        lo, hi = self.now, min(self.now + count, self.end)
+    def loop(self, count, per, body):
+        lo, hi = self.now, min(self.now + count * per, self.end)
         self.now = hi
 
         def step(i, carry):
             body(i)
-            self.ticks(lo + i, lo, lo + count)
+            for j in range(per):
+                self.ticks(lo + i * per + j, lo, lo + count * per)
             return carry
 
         lax.fori_loop(0, count, step, 0)
@@ -867,6 +869,10 @@
         jnp.sum(grad * normed, axis=0, keepdims=True),
         jnp.sum(grad, axis=0, keepdims=True),
     )
+
+
+TICKS = (1, 1, 1, 1, 1, 1, 1, 1, 1, 1, 2, 1)
+LAG = 1
 
 
 def backward_kernel(
@@ -925,6 +931,14 @@
     ]
     for load in loads:
         load.start()
+    early = []
+    if tokens == step:
+        early = [
+            pltpu.make_async_copy(h2, chunk, tmp_sem.at[2]),
+            pltpu.make_async_copy(cot_in, chunk2, tmp_sem.at[3]),
+        ]
+        for load in early:
+            load.start()
     if own_q.shape[0] != width:
         own_q = own_f.at[:, : 3 * own_cols]
     load_q = pltpu.make_async_copy(wq, own_q, load_sem.at[4])
@@ -946,8 +960,7 @@
 
     def feed_forward(i, carry):
         at = pl.ds(pl.multiple_of(i * step, step), step)
-        first = fetch(h2, at, chunk, 2)
-        second = fetch(cot_in, at, chunk2, 3)
+        first, second = early or (fetch(h2, at, chunk, 2), fetch(cot_in, at, chunk2, 3))
         first.wait()
         second.wait()
 
@@ -1030,15 +1043,18 @@
                 for m in range(r_size):
                     to_home(lo_.at[d, j], home_out.at[out_at(s_to, d, j)], oh_send.at[i, m], oh_recv.at[me], s_to, m)
 
-    sum_proj = LineSum(jp, lp, p_rs, p_rr, p_as, p_ar, home_of_proj, 0)
+    def line(jobs, landing, sems, home, start):
+        return LineSum(jobs, landing, *sems, home, start, LAG)
+
+    sum_proj = line(jp, lp, (p_rs, p_rr, p_as, p_ar), home_of_proj, 0)
     start = sum_proj.n
-    sum_fc = LineSum(jf, lf, f_rs, f_rr, f_as, f_ar, home_of_columns(lf, home_fc, fh_send, fh_recv), start)
+    sum_fc = line(jf, lf, (f_rs, f_rr, f_as, f_ar), home_of_columns(lf, home_fc, fh_send, fh_recv), start)
     start += sum_fc.n
-    sum_out = LineSum(jo, lo_, o_rs, o_rr, o_as, o_ar, home_of_out, start)
+    sum_out = line(jo, lo_, (o_rs, o_rr, o_as, o_ar), home_of_out, start)
     start += sum_out.n
-    sum_qkv = LineSum(jq, lq, q_rs, q_rr, q_as, q_ar, home_of_columns(lq, home_qkv, qh_send, qh_recv), start)
+    sum_qkv = line(jq, lq, (q_rs, q_rr, q_as, q_ar), home_of_columns(lq, home_qkv, qh_send, qh_recv), start)
     clock = Clock([sum_proj, sum_fc, sum_out, sum_qkv])
-    clock.run(1)
+    clock.run(TICKS[0])
 
     def slot(offset):
         return (offset // r_size) // 2 * r_size + offset % r_size
@@ -1063,9 +1079,11 @@
     else:
         land, load_land = block(land_far), far_load(land_far)
     scatter_two = Scatter(packed_block(leaf), packed_block(acc), land, load_land, s2_send, s2_recv, r_size)
-    scatter_proj = Scatter(
-        packed_block(leaf), packed_block(acc), block(landp), far_load(landp), sp_send, sp_recv, r_size
-    )
+    if chunks == 1:
+        land_p, load_p = block(chunk2), lambda o, part: block(chunk2)(o, part)[...]
+    else:
+        land_p, load_p = block(landp), far_load(landp)
+    scatter_proj = Scatter(packed_block(leaf), packed_block(acc), land_p, load_p, sp_send, sp_recv, r_size)
     scatter_one = Scatter(packed_block(leaf), packed_block(acc), land, load_land, s1_send, s1_recv, r_size)
     n = r_size * rows
 
@@ -1080,15 +1098,15 @@
 
     partial_sums(leaf, 1, gpre, own_f, contract_last)
     scatter_two.start_leaves()
-    clock.run(1)
+    clock.run(TICKS[1])
     partial_sums(acc, 0, gpre, own_f, contract_last)
     load_q.start()
     if chunks == 1:
         product_rows(chunk, gpre, into_jobs(jf))
-    clock.run(1)
+    clock.run(TICKS[2])
 
     scatter_two.start_inner()
-    clock.run(1)
+    clock.run(TICKS[3])
     vec[...] = jnp.zeros_like(vec)
     gain_one, gain_two, proj_bias = (small_ref[i : i + 1, :] for i in (0, 3, 5))
     for load in loads[2:]:
@@ -1108,28 +1126,28 @@
     vec[3:4, :] = grad_gain
     vec[4:5, :] = grad_bias
     vec[5:6, :] = jnp.sum(cot, axis=0, keepdims=True)
-    clock.run(1)
+    clock.run(TICKS[4])
     gather.start_rest()
     scatter_two.close()
     partial_sums(leaf, 1, act, own_p, (((1,), (0,)), ((), ())))
     scatter_proj.start_leaves()
-    clock.run(1)
+    clock.run(TICKS[5])
     partial_sums(acc, 0, act, own_p, (((1,), (0,)), ((), ())))
     gather.need_all()
     save_gb.wait()
     scatter_proj.start_inner()
-    clock.run(1)
+    clock.run(TICKS[6])
 
     if chunks > 1:
         go_acc[...] = jnp.zeros_like(go_acc)
 
     def branch_rows(i, carry):
         at = pl.ds(pl.multiple_of(i * step, step), step)
-        fetch(gb, at, chunk2, 3).wait()
+        fetch(gb, at, chunk, 2).wait()
         do_ref[at, :] = lax.dot_general(
-            chunk2[...], own_o[...], contract_last, preferred_element_type=F32
+            chunk[...], own_o[...], contract_last, preferred_element_type=F32
         ).astype(BF16)
-        product_rows(att_ref.at[at], chunk2, into_jobs(jo) if chunks == 1 else into_sum(go_acc))
+        product_rows(att_ref.at[at], chunk, into_jobs(jo) if chunks == 1 else into_sum(go_acc))
         return carry
 
     if chunks == 1:
@@ -1137,7 +1155,7 @@
     else:
         lax.fori_loop(0, chunks, branch_rows, 0)
         into_jobs(jo)(0, own_cols, go_acc[...])
-    clock.run(1)
+    clock.run(TICKS[7])
     out_v[...] = (middle + (scatter_proj.finish() + proj_bias)).astype(BF16)
 
     def moved(src, dst, sem):
@@ -1164,6 +1182,9 @@
         return done
 
     out_done = moved(out_v, out_home, mv_sem.at[0])
+    if chunks == 1:
+        early = [pltpu.make_async_copy(h1, chunk2, tmp_sem.at[3])]
+        early[0].start()
 
     code_row = jnp.concatenate([code_ref[i : i + 1, :] for i in range(devices)], axis=1)
     q_rows = min(rows if tokens > 2048 else 256, tokens)
@@ -1200,7 +1221,7 @@
         dv_acc[...] += jnp.concatenate(dvs, axis=1)
 
     if chunks == 1:
-        clock.loop(tokens // q_rows, attend)
+        clock.loop(tokens // q_rows, TICKS[8], attend)
     else:
 
         def attend_step(i, carry):
@@ -1215,13 +1236,13 @@
     load_q.wait()
     partial_sums(leaf, 1, gp, own_q, contract_last)
     scatter_one.start_leaves()
+    clock.run(TICKS[9])
     partial_sums(acc, 0, gp, own_q, contract_last)
-    clock.run(1)
 
     def hidden_rows(i, carry):
         at = pl.ds(pl.multiple_of(i * step, step), step)
-        fetch(h1, at, chunk, 2).wait()
-        product_rows(chunk, gp.at[at], into_jobs(jq) if chunks == 1 else into_sum(gq_acc))
+        (early[0] if early else fetch(h1, at, chunk2, 3)).wait()
+        product_rows(chunk2, gp.at[at], into_jobs(jq) if chunks == 1 else into_sum(gq_acc))
         return carry
 
     if chunks == 1:
@@ -1230,7 +1251,7 @@
         lax.fori_loop(0, chunks, hidden_rows, 0)
         into_jobs(jq)(0, width, gq_acc[...])
     scatter_one.start_inner()
-    clock.run(2)
+    clock.run(TICKS[10])
 
     resid = x_ref[...].astype(F32)
     normed, inverse = norm_parts(resid)
@@ -1252,7 +1273,7 @@
     for i, (axis, bit) in enumerate(hops):
         copy = remote(vec, vec_land.at[i], vec_send.at[i], vec_recv.at[i], **partner(axis, bit))
         copy.start()
-        clock.run(1)
+        clock.run(TICKS[11])
         copy.wait()
         vec[...] = vec[...] + vec_land[i]
     small_out[...] = vec[...]

time: 477 us -> 472 us (0.990)
  Pallas kernels: 467 us -> 462 us
    pallas_call x1, Pallas kernels: 129 us -> 123 us  [forward_part(): pl.pallas_call(forward_kernel, in_specs=[anywhere] * 3 + [vmem] * 8 + [an...]
where the time goes in v5:
time: 472 us; the launch traced here: 465 us
  Pallas kernels  462 us (98%)
    pallas_call x1, Pallas kernels, backward_part(): pl.pallas_call(backward_kernel, in_specs=[anywhere] * 7 + [vmem] * 10, ou...  320 us
    pallas_call x1, Pallas kernels, forward_part(): pl.pallas_call(forward_kernel, in_specs=[anywhere] * 3 + [vmem] * 8 + [an...  123 us
    pallas_call x1, Pallas kernels, results(): pl.pallas_call(results_kernel, grid=(steps,), in_specs=[whole(rows, width...  18.6 us

profile of v5, /device:TPU:1, one launch (start us, length us, event | category | flops | bytes accessed | tf_op | source)
XLA Modules:
  0.0 464.6 jit_solution(1856010511958264642)
XLA Ops:
  0.6 0.7 fusion
  1.3 0.6 broadcast_in_dim.3.code_in
  1.9 123.4 %forward_part.1 = (bf16[1024,1600]{1,0:T(8,128)(2,1)}, bf16[1024,1600]{1,0:T(8,128)(2,1)}, bf16[1024,1600]{1,0:T(8,128)(2,1)}, bf16[1600,800]{1,0:T(8,128)(2,1)}...) custom-call(bf16[1600,128]{1,0:T(8,128)(2,1)} %bitcast.7, ...), custom_call_target="tpu_custom_call" | custom-call | flops 3590324224 | bytes 41943040 | tf_op jit(solution)/shard_map/forward_part/pallas_call | solution.py:588
  125.3 320.5 %backward_part.1 = (bf16[128,1600]{1,0:T(8,128)(2,1)}, bf16[128,1600]{1,0:T(8,128)(2,1)}, bf16[2,2,5,80,1600]{4,3,2,1,0:T(8,128)(2,1)}, bf16[8,5,80,800]{3,2,1,0...) custom-call(bf16[1024,1600]{1,0:T(8,128)(2,1)} %get-tuple-element.51, ...), custom_call_target="tpu_custom_call" | custom-call | flops 18412994560 | bytes 41943040 | tf_op jit(solution)/shard_map/backward_part/pallas_call | solution.py:1354
  445.8 18.6 %results.1 = (bf16[1600,128]{1,0:T(8,128)(2,1)}, f32[1600,128]{1,0:T(8,128)}, f32[400]{0:T(512)}, f32[400]{0:T(512)}, f32[400,4800]{1,0:T(8,128)}, /*index=5*/f3...) custom-call(bf16[128,1600]{1,0:T(8,128)(2,1)} %get-tuple-element.67., ...), custom_call_target="tpu_custom_call" | custom-call | tf_op jit(solution)/shard_map/results/pallas_call | solution.py:1486

commit v6 on v5

--- a/solution.py
+++ b/solution.py
@@ -755,19 +755,19 @@
 
     def tick(self, k):
         for d in range(2):
+            place = self.place(d)
+            j = k - self.start - self.lag * (2 * self.last - place)
+
+            @pl.when(jnp.logical_and(place < self.last, jnp.logical_and(j >= 0, j < self.n)))
+            def _(d=d, j=j):
+                self.back(d, j)
+
+        for d in range(2):
             j = k - self.start - self.lag * self.place(d)
 
             @pl.when(jnp.logical_and(j >= 0, j < self.n))
             def _(d=d, j=j):
                 self.add(d, j)
-
-        for d in range(2):
-            place = self.place(d)
-            j = k - self.start - self.lag * (2 * self.last - place)
-
-            @pl.when(jnp.logical_and(place < self.last, jnp.logical_and(j >= 0, j < self.n)))
-            def _(d=d, j=j):
-                self.back(d, j)
 
     def close(self):
         def one(j, carry):

time: 472 us -> 470 us (level)
  no operation moved by 1% of the time
where the time goes in v6:
time: 470 us; the launch traced here: 463 us
  Pallas kernels  461 us (98%)
    pallas_call x1, Pallas kernels, backward_part(): pl.pallas_call(backward_kernel, in_specs=[anywhere] * 7 + [vmem] * 10, ou...  319 us
    pallas_call x1, Pallas kernels, forward_part(): pl.pallas_call(forward_kernel, in_specs=[anywhere] * 3 + [vmem] * 8 + [an...  123 us
    pallas_call x1, Pallas kernels, results(): pl.pallas_call(results_kernel, grid=(steps,), in_specs=[whole(rows, width...  18.6 us

profile of v6, /device:TPU:1, one launch (start us, length us, event | category | flops | bytes accessed | tf_op | source)
XLA Modules:
  0.0 463.1 jit_solution(7106459454762729964)
XLA Ops:
  0.6 0.7 fusion
  1.3 0.6 broadcast_in_dim.3.code_in
  1.9 123.4 %forward_part.1 = (bf16[1024,1600]{1,0:T(8,128)(2,1)}, bf16[1024,1600]{1,0:T(8,128)(2,1)}, bf16[1024,1600]{1,0:T(8,128)(2,1)}, bf16[1600,800]{1,0:T(8,128)(2,1)}...) custom-call(bf16[1600,128]{1,0:T(8,128)(2,1)} %bitcast.7, ...), custom_call_target="tpu_custom_call" | custom-call | flops 3590324224 | bytes 41943040 | tf_op jit(solution)/shard_map/forward_part/pallas_call | solution.py:588
  125.3 318.9 %backward_part.1 = (bf16[128,1600]{1,0:T(8,128)(2,1)}, bf16[128,1600]{1,0:T(8,128)(2,1)}, bf16[2,2,5,80,1600]{4,3,2,1,0:T(8,128)(2,1)}, bf16[8,5,80,800]{3,2,1,0...) custom-call(bf16[1024,1600]{1,0:T(8,128)(2,1)} %get-tuple-element.51, ...), custom_call_target="tpu_custom_call" | custom-call | flops 18412994560 | bytes 41943040 | tf_op jit(solution)/shard_map/backward_part/pallas_call | solution.py:1354
  444.3 18.6 %results.1 = (bf16[1600,128]{1,0:T(8,128)(2,1)}, f32[1600,128]{1,0:T(8,128)}, f32[400]{0:T(512)}, f32[400]{0:T(512)}, f32[400,4800]{1,0:T(8,128)}, /*index=5*/f3...) custom-call(bf16[128,1600]{1,0:T(8,128)(2,1)} %get-tuple-element.67., ...), custom_call_target="tpu_custom_call" | custom-call | tf_op jit(solution)/shard_map/results/pallas_call | solution.py:1486
